TPU v7x, 512 devices: a whole 4x8x8 slice. The times are simulated.
512 devices in a mesh: ctx: 64 (over y_lo, z, core), head: 8 (over x, y_hi).
Axes of the slice: x: 4, y: 8 (y_hi: 2, y_lo: 4; y = y_hi * 4 + y_lo), z: 8, core: 2. Of those that a mesh axis runs over, the one named last changes fastest.
Arguments:
- queries: bfloat16 [24576, 4096], P(('ctx', 'head')), may hold values from -6 to 6
- keys: bfloat16 [24576, 1024], P(('ctx', 'head')), may hold values from -6 to 6
- values: bfloat16 [24576, 1024], P(('ctx', 'head')), may hold values from -6 to 6
- output_gradient: bfloat16 [24576, 4096], P(('ctx', 'head')), may hold values from -6 to 6
- doc_lengths: int32 [64], replicated, may hold values from 1 to 1536, 24576 in all
Outputs:
- attended: bfloat16 [24576, 4096], P(('ctx', 'head'))
- query_gradient_rows: bfloat16 [24576, 4096], P(('ctx', 'head'))
- grad_keys: bfloat16 [24576, 1024], P(('ctx', 'head'))
- grad_values: bfloat16 [24576, 1024], P(('ctx', 'head'))
Inputs may be any that keep to these rules, and one draw needn't show every extreme that they name: `doc_lengths`: the 64 documents are packed in order and their lengths sum to 24576; the longest is exactly 1536, so a document covers positions of at most 5 consecutive ctx indices.
All inputs are finite; a program needn't handle non-finite values.
Results may differ from a plain program's by a relative error of at most 0.034.
Values may be sent and summed in bfloat16 or wider, within the bound.
No kernel may reach another device: no remote copies, remote signals or barrier semaphores. Data moves between devices by JAX's collectives and lax.ppermute only.
A program may use at most 128 MiB of HBM per device.

v0:
```python
from functools import reduce
import math

import jax
import jax.numpy as jnp
from jax import lax
from jax.sharding import PartitionSpec as P

QUERY_HEAD_COUNT = 32
KEY_VALUE_HEADS = 8
HEAD_SIZE = 128
REACH = 4


def shifted(shard, axis, by):
    peers = lax.axis_size(axis)
    pairs = [(i, i + by) for i in range(peers) if 0 <= i + by < peers]
    return lax.ppermute(shard, axis, pairs)


def document_ids(doc_lengths, positions):
    ends = jnp.cumsum(doc_lengths)
    return jnp.sum((ends[None, :] <= positions[:, None]).astype(jnp.int32), axis=1)


def allowed(query_pos, key_pos, doc_lengths):
    same = (
        document_ids(doc_lengths, query_pos)[:, None] == document_ids(doc_lengths, key_pos)[None, :]
    )
    return same & (key_pos[None, :] <= query_pos[:, None]) & (key_pos[None, :] >= 0)


def split_pair(pair, kv_heads):
    rows = pair.shape[1]
    return (pair[0].reshape(rows, kv_heads, HEAD_SIZE), pair[1].reshape(rows, kv_heads, HEAD_SIZE))


def tile_scores(query_heads, tile_keys, mask, scale):
    scores = (
        jnp.einsum("qgjd,kgd->gjqk", query_heads, tile_keys, preferred_element_type=jnp.float32)
        * scale
    )
    return jnp.where(mask, scores, -jnp.inf)


def tile_weights(scores, mask, top, tile_values):
    weights = jnp.where(mask, jnp.exp(scores - top[..., None]), 0.0)
    summed = jnp.einsum(
        "gjqk,kgd->qgjd",
        weights.astype(jnp.bfloat16),
        tile_values,
        preferred_element_type=jnp.float32,
    )
    return (jnp.sum(weights, axis=-1), summed)


def tile_grads(scores, mask, log_total, delta, grad_heads, tile_values):
    probs = jnp.where(mask, jnp.exp(scores - log_total[..., None]), 0.0)
    dprobs = jnp.einsum(
        "qgjd,kgd->gjqk", grad_heads, tile_values, preferred_element_type=jnp.float32
    )
    dscores = (probs * (dprobs - delta[..., None])).astype(jnp.bfloat16)
    return (probs.astype(jnp.bfloat16), dscores)


def query_term(dscores, tile_keys):
    return jnp.einsum("gjqk,kgd->qgjd", dscores, tile_keys, preferred_element_type=jnp.float32)


def key_terms(probs_b, dscores, query_heads, grad_heads):
    key_part = jnp.einsum(
        "gjqk,qgjd->kgd", dscores, query_heads, preferred_element_type=jnp.float32
    )
    value_part = jnp.einsum(
        "gjqk,qgjd->kgd", probs_b, grad_heads, preferred_element_type=jnp.float32
    )
    return jnp.stack([key_part, value_part])


def local(queries, keys, values, output_gradient, doc_lengths):
    query_loc, key_loc, value_loc, grad_loc = (
        lax.all_to_all(queries, "head", split_axis=1, concat_axis=0, tiled=True),
        lax.all_to_all(keys, "head", split_axis=1, concat_axis=0, tiled=True),
        lax.all_to_all(values, "head", split_axis=1, concat_axis=0, tiled=True),
        lax.all_to_all(output_gradient, "head", split_axis=1, concat_axis=0, tiled=True),
    )
    rows = query_loc.shape[0]
    kv_heads = key_loc.shape[1] // HEAD_SIZE
    head_group = QUERY_HEAD_COUNT // KEY_VALUE_HEADS
    scale = 1.0 / math.sqrt(HEAD_SIZE)
    place = lax.axis_index("ctx")
    offsets = jnp.arange(rows, dtype=jnp.int32)
    query_pos = place * rows + offsets
    query_heads = query_loc.reshape(rows, kv_heads, head_group, HEAD_SIZE)
    grad_heads = grad_loc.reshape(rows, kv_heads, head_group, HEAD_SIZE)
    own_pair = jnp.stack([key_loc, value_loc])
    pairs = [own_pair]
    current = own_pair
    for step in range(REACH):
        current = shifted(current, "ctx", 1)
        pairs.append(current)
    tiles_kv = [split_pair(pair, kv_heads) for pair in pairs]
    masks = [
        allowed(query_pos, (place - step) * rows + offsets, doc_lengths)
        for step in range(REACH + 1)
    ]
    scored = []
    for step in range(REACH + 1):
        scored.append(tile_scores(query_heads, tiles_kv[step][0], masks[step], scale))
    top = reduce(jnp.maximum, [jnp.max(tile, axis=-1) for tile in scored])
    total = jnp.zeros((kv_heads, head_group, rows), jnp.float32)
    accum = jnp.zeros((rows, kv_heads, head_group, HEAD_SIZE), jnp.float32)
    for step in range(REACH + 1):
        tile_total, tile_sum = tile_weights(scored[step], masks[step], top, tiles_kv[step][1])
        total = total + tile_total
        accum = accum + tile_sum
    attended = (accum / jnp.transpose(total, (2, 0, 1))[..., None]).astype(jnp.bfloat16)
    attended_tokens = lax.all_to_all(
        attended.reshape(rows, -1), "head", split_axis=0, concat_axis=1, tiled=True
    )
    log_total = top + jnp.log(total)
    delta = jnp.transpose(
        jnp.sum(grad_heads.astype(jnp.float32) * attended.astype(jnp.float32), axis=-1), (1, 2, 0)
    )
    own_keys, own_values = tiles_kv[0]
    probs_b, dscores = tile_grads(scored[0], masks[0], log_total, delta, grad_heads, own_values)
    grad_query = query_term(dscores, own_keys)
    key_parts = key_terms(probs_b, dscores, query_heads, grad_heads)
    for step in range(1, REACH + 1):
        tile_probs, tile_dscores = tile_grads(
            scored[step], masks[step], log_total, delta, grad_heads, tiles_kv[step][1]
        )
        query_part = query_term(tile_dscores, tiles_kv[step][0])
        pair_part = key_terms(tile_probs, tile_dscores, query_heads, grad_heads)
        grad_query = grad_query + query_part
        key_parts = key_parts + shifted(pair_part.astype(jnp.bfloat16), "ctx", -step).astype(
            pair_part.dtype
        )
    grad_query_b = (grad_query * scale).astype(jnp.bfloat16).reshape(rows, -1)
    grad_key_b = (key_parts[0] * scale).astype(jnp.bfloat16).reshape(rows, -1)
    grad_value_b = key_parts[1].astype(jnp.bfloat16).reshape(rows, -1)
    grads = (
        lax.all_to_all(grad_query_b, "head", split_axis=0, concat_axis=1, tiled=True),
        lax.all_to_all(grad_key_b, "head", split_axis=0, concat_axis=1, tiled=True),
        lax.all_to_all(grad_value_b, "head", split_axis=0, concat_axis=1, tiled=True),
    )
    return (attended_tokens, grads[0], grads[1], grads[2])


def solution(mesh):
    in_specs = (
        P(("ctx", "head"), None),
        P(("ctx", "head"), None),
        P(("ctx", "head"), None),
        P(("ctx", "head"), None),
        P(),
    )
    out_specs = (
        P(("ctx", "head"), None),
        P(("ctx", "head"), None),
        P(("ctx", "head"), None),
        P(("ctx", "head"), None),
    )
    return jax.shard_map(local, mesh=mesh, in_specs=in_specs, out_specs=out_specs, check_vma=False)
```

profile of v0, /device:TPU:16, one launch (start us, length us, event | category | flops | bytes accessed | tf_op | source)
XLA Modules:
  0.0 212.1 jit_solution(12206824954266971283)
XLA Ops:
  0.7 0.9 copy-done
  1.5 0.7 copy_bitcast_fusion.5
  2.2 7.8 %all-to-all-start = ((bf16[48,8,128]{2,0,1:T(8,128)(2,1)}), bf16[48,8,128]{2,0,1:T(8,128)(2,1)S(1)}, u32[]{:S(2)}, u32[]{:S(2)}) async-start(bf16[48,8,128]{2,0,1:T(8,128)(2,1)} %copy_bitcast_fusion.5), calls=%async_computation | async-start | bytes 196608 | tf_op jit(solution)/shard_map/all_to_all | solution.py:83
  10.0 1.5 copy_bitcast_fusion.4
  11.5 9.3 %all-to-all-done = bf16[48,8,128]{2,0,1:T(8,128)(2,1)S(1)} async-done(((bf16[48,8,128]{2,0,1:T(8,128)(2,1)}), bf16[48,8,128]{2,0,1:T(8,128)(2,1)S(1)}, u32[]{:S(2)}, u32[]{:S(2)}) %all-to-all-start) | async-done | bytes 98336 | tf_op jit(solution)/shard_map/all_to_all | solution.py:83
  20.8 3.4 %all-to-all-start.2 = ((bf16[48,8,128]{2,0,1:T(8,128)(2,1)}), bf16[48,8,128]{2,0,1:T(8,128)(2,1)S(1)}, u32[]{:S(2)}, u32[]{:S(2)}) async-start(bf16[48,8,128]{2,0,1:T(8,128)(2,1)} %copy_bitcast_fusion.4), calls=%async_computation.2 | async-start | bytes 196608 | tf_op jit(solution)/shard_map/all_to_all | solution.py:84
  24.2 1.8 copy.355
  26.0 8.6 %all-to-all-done.2 = bf16[48,8,128]{2,0,1:T(8,128)(2,1)S(1)} async-done(((bf16[48,8,128]{2,0,1:T(8,128)(2,1)}), bf16[48,8,128]{2,0,1:T(8,128)(2,1)S(1)}, u32[]{:S(2)}, u32[]{:S(2)}) %all-to-all-start.2) | async-done | bytes 98336 | tf_op jit(solution)/shard_map/all_to_all | solution.py:84
  34.6 3.5 %all-to-all-start.1 = ((bf16[48,8,512]{2,0,1:T(8,128)(2,1)}), bf16[48,8,512]{2,0,1:T(8,128)(2,1)S(1)}, u32[]{:S(2)}, u32[]{:S(2)}) async-start(bf16[48,8,512]{2,0,1:T(8,128)(2,1)} %bitcast.440), calls=%async_computation.1 | async-start | bytes 786432 | tf_op jit(solution)/shard_map/all_to_all | solution.py:82
  38.1 0.8 copy.354
  38.9 11.2 %all-to-all-done.1 = bf16[48,8,512]{2,0,1:T(8,128)(2,1)S(1)} async-done(((bf16[48,8,512]{2,0,1:T(8,128)(2,1)}), bf16[48,8,512]{2,0,1:T(8,128)(2,1)S(1)}, u32[]{:S(2)}, u32[]{:S(2)}) %all-to-all-start.1) | async-done | bytes 393248 | tf_op jit(solution)/shard_map/all_to_all | solution.py:82
  50.0 3.5 %all-to-all-start.4 = ((bf16[48,8,512]{2,0,1:T(8,128)(2,1)}), bf16[48,8,512]{2,0,1:T(8,128)(2,1)S(1)}, u32[]{:S(2)}, u32[]{:S(2)}) async-start(bf16[48,8,512]{2,0,1:T(8,128)(2,1)} %bitcast.439), calls=%async_computation.4 | async-start | bytes 786432 | tf_op jit(solution)/shard_map/all_to_all | solution.py:85
  53.9 1.9 collective-permute-start
  55.9 18.4 %collective-permute-done = bf16[2,384,128]{2,1,0:T(8,128)(2,1)S(1)} collective-permute-done((bf16[2,384,128]{2,1,0:T(8,128)(2,1)S(1)}, bf16[2,384,128]{2,1,0:T(8,128)(2,1)S(1)}, u32[]{:S(2)}, u32[]{:S(2)}) %collective-permute-start) | collective-permute-done | bytes 196640 | tf_op jit(solution)/shard_map/ppermute | solution.py:18
  74.3 1.9 collective-permute-start.1
  76.2 2.1 and_and_fusion.3
  78.3 5.2 %collective-permute-done.1 = bf16[2,384,128]{2,1,0:T(8,128)(2,1)} collective-permute-done((bf16[2,384,128]{2,1,0:T(8,128)(2,1)S(1)}, bf16[2,384,128]{2,1,0:T(8,128)(2,1)}, u32[]{:S(2)}, u32[]{:S(2)}) %collective-permute-start.1) | collective-permute-done | bytes 196640 | tf_op jit(solution)/shard_map/ppermute | solution.py:18
  83.5 1.9 collective-permute-start.2
  86.3 0.5 fusion.179
  86.9 1.4 fusion.178
  88.3 0.5 fusion.180
  88.9 4.0 %collective-permute-done.2 = bf16[2,384,128]{2,1,0:T(8,128)(2,1)} collective-permute-done((bf16[2,384,128]{2,1,0:T(8,128)(2,1)}, bf16[2,384,128]{2,1,0:T(8,128)(2,1)}, u32[]{:S(2)}, u32[]{:S(2)}) %collective-permute-start.2) | collective-permute-done | bytes 196640 | tf_op jit(solution)/shard_map/ppermute | solution.py:18
  92.9 2.1 collective-permute-start.3
  95.0 1.4 fusion.177
  96.5 5.7 %collective-permute-done.3 = bf16[2,384,128]{2,1,0:T(8,128)(2,1)S(1)} collective-permute-done((bf16[2,384,128]{2,1,0:T(8,128)(2,1)}, bf16[2,384,128]{2,1,0:T(8,128)(2,1)S(1)}, u32[]{:S(2)}, u32[]{:S(2)}) %collective-permute-start.3) | collective-permute-done | bytes 196640 | tf_op jit(solution)/shard_map/ppermute | solution.py:18
  102.2 0.5 fusion.176
  102.8 2.3 %fusion.12 = (f32[4,384]{1,0:T(4,128)S(1)}, f32[4,384]{1,0:T(4,128)S(1)}, f32[4,384]{1,0:T(4,128)S(1)}, f32[4,384]{1,0:T(4,128)S(1)}, f32[4,384]{1,0:T(4,128)S(1)}) fusion(f32[1,4,384,384]{2,3,1,0:T(8,128)S(1)} %get-tuple-element.30, f32[4,384]{1,0:T(4,128)S(1)} %maximum_maximum_fusion, pred[384,384]{0,1:T(8,128)(4,1)S(1)} %get-tuple-element.16, ...), kind=kLoop, calls=%fused_computation.32 | loop fusion | flops 8839680 | bytes 12570624 | tf_op jit(solution)/shard_map/reduce_sum | solution.py:54
  105.1 0.5 fusion.124
  108.1 0.6 convolution_add_fusion.7
  108.7 1.5 convolution_add_fusion.6
  110.2 1.5 convolution_add_fusion.5
  111.6 1.4 multiply_reduce_fusion
  113.0 0.8 fusion.25
  113.8 0.8 fusion.26
  115.2 1.9 collective-permute-start.4
  117.1 1.7 fusion.27
  119.4 1.9 collective-permute-start.5
  121.3 1.7 fusion.28
  123.5 1.9 collective-permute-start.6
  125.5 0.8 fusion.29
  126.8 2.1 %collective-permute-start.7 = (bf16[2,384,1,128]{3,1,2,0:T(8,128)(2,1)S(1)}, bf16[2,384,1,128]{3,1,2,0:T(8,128)(2,1)S(1)}, u32[]{:S(2)}, u32[]{:S(2)}) collective-permute-start(bf16[2,384,1,128]{3,1,2,0:T(8,128)(2,1)S(1)} %pad_maximum_fusion.4), channel_id=1, source_target_pairs={{32,0},{40,8},{48,16},{56,24},{64,32},{72,40},{80,48},{88,56},{96,... | collective-permute-start | bytes 589832 | tf_op jit(solution)/shard_map/ppermute | solution.py:18
  129.5 0.6 convolution_add_fusion.3
  130.1 1.5 convolution_add_fusion.2
  131.6 1.5 convolution_add_fusion.1
  133.1 0.5 fusion.89
  134.4 4.5 %collective-permute-done.6 = bf16[2,384,1,128]{3,1,2,0:T(8,128)(2,1)S(1)} collective-permute-done((bf16[2,384,1,128]{3,1,2,0:T(8,128)(2,1)S(1)}, bf16[2,384,1,128]{3,1,2,0:T(8,128)(2,1)S(1)}, u32[]{:S(2)}, u32[]{:S(2)}) %collective-permute-start.6) | collective-permute-done | bytes 196640 | tf_op jit(solution)/shard_map/ppermute | solution.py:18
  138.9 5.7 %collective-permute-done.7 = bf16[2,384,1,128]{3,1,2,0:T(8,128)(2,1)S(1)} collective-permute-done((bf16[2,384,1,128]{3,1,2,0:T(8,128)(2,1)S(1)}, bf16[2,384,1,128]{3,1,2,0:T(8,128)(2,1)S(1)}, u32[]{:S(2)}, u32[]{:S(2)}) %collective-permute-start.7) | collective-permute-done | bytes 196640 | tf_op jit(solution)/shard_map/ppermute | solution.py:18
  144.7 0.7 slice.79
  145.4 7.5 %all-to-all-start.7 = ((bf16[8,48,128]{2,1,0:T(8,128)(2,1)}), bf16[8,48,128]{2,1,0:T(8,128)(2,1)S(1)}, u32[]{:S(2)}, u32[]{:S(2)}) async-start(bf16[8,48,128]{2,1,0:T(8,128)(2,1)} %bitcast.140), calls=%async_computation.7 | async-start | bytes 196608 | tf_op jit(solution)/shard_map/all_to_all | solution.py:145
  152.9 0.7 fusion.145
  153.5 10.3 %all-to-all-done.7 = bf16[8,48,128]{2,1,0:T(8,128)(2,1)S(1)} async-done(((bf16[8,48,128]{2,1,0:T(8,128)(2,1)}), bf16[8,48,128]{2,1,0:T(8,128)(2,1)S(1)}, u32[]{:S(2)}, u32[]{:S(2)}) %all-to-all-start.7) | async-done | bytes 98336 | tf_op jit(solution)/shard_map/all_to_all | solution.py:145
  163.8 3.4 %all-to-all-start.6 = ((bf16[8,48,128]{2,1,0:T(8,128)(2,1)}), bf16[8,48,128]{2,1,0:T(8,128)(2,1)S(1)}, u32[]{:S(2)}, u32[]{:S(2)}) async-start(bf16[8,48,128]{2,1,0:T(8,128)(2,1)} %bitcast.138), calls=%async_computation.6 | async-start | bytes 196608 | tf_op jit(solution)/shard_map/all_to_all | solution.py:144
  167.2 0.6 fusion.33
  168.1 0.9 all_to_all.116
  169.0 10.2 %all-to-all-done.6 = bf16[8,48,128]{2,1,0:T(8,128)(2,1)S(1)} async-done(((bf16[8,48,128]{2,1,0:T(8,128)(2,1)}), bf16[8,48,128]{2,1,0:T(8,128)(2,1)S(1)}, u32[]{:S(2)}, u32[]{:S(2)}) %all-to-all-start.6) | async-done | bytes 98336 | tf_op jit(solution)/shard_map/all_to_all | solution.py:144
  179.3 3.5 %all-to-all-start.5 = ((bf16[8,48,512]{2,1,0:T(8,128)(2,1)}), bf16[8,48,512]{2,1,0:T(8,128)(2,1)S(1)}, u32[]{:S(2)}, u32[]{:S(2)}) async-start(bf16[8,48,512]{2,1,0:T(8,128)(2,1)} %all_to_all.116), calls=%async_computation.5 | async-start | bytes 786432 | tf_op jit(solution)/shard_map/all_to_all | solution.py:143
  183.0 0.9 all_to_all.109
  183.9 12.1 %all-to-all-done.5 = bf16[8,48,512]{2,1,0:T(8,128)(2,1)S(1)} async-done(((bf16[8,48,512]{2,1,0:T(8,128)(2,1)}), bf16[8,48,512]{2,1,0:T(8,128)(2,1)S(1)}, u32[]{:S(2)}, u32[]{:S(2)}) %all-to-all-start.5) | async-done | bytes 393248 | tf_op jit(solution)/shard_map/all_to_all | solution.py:143
  196.0 3.5 %all-to-all-start.3 = ((bf16[8,48,512]{2,1,0:T(8,128)(2,1)}), bf16[8,48,512]{2,1,0:T(8,128)(2,1)S(1)}, u32[]{:S(2)}, u32[]{:S(2)}) async-start(bf16[8,48,512]{2,1,0:T(8,128)(2,1)} %all_to_all.109), calls=%async_computation.3 | async-start | bytes 786432 | tf_op jit(solution)/shard_map/all_to_all | solution.py:118
  199.5 0.6 copy_bitcast_fusion.2
  200.1 0.6 copy_bitcast_fusion.3
  200.8 0.8 copy.295
  201.5 9.7 %all-to-all-done.3 = bf16[8,48,512]{2,1,0:T(8,128)(2,1)S(1)} async-done(((bf16[8,48,512]{2,1,0:T(8,128)(2,1)}), bf16[8,48,512]{2,1,0:T(8,128)(2,1)S(1)}, u32[]{:S(2)}, u32[]{:S(2)}) %all-to-all-start.3) | async-done | bytes 393248 | tf_op jit(solution)/shard_map/all_to_all | solution.py:118
  211.3 0.8 copy.294
  (63 shorter events, 7.8 us)
Async XLA Ops:
  0.6 0.9 copy-start
  0.6 37.4 %copy-start.8 = (bf16[48,4096]{1,0:T(8,128)(2,1)S(1)}, bf16[48,4096]{1,0:T(8,128)(2,1)}, u32[]{:S(2)}) copy-start(bf16[48,4096]{1,0:T(8,128)(2,1)} %param.8) | copy-start | bytes 1179652
  1.5 52.0 %copy-start.12 = (s32[64]{0:T(128)S(1)}, s32[64]{0:T(128)}, u32[]{:S(2)}) copy-start(s32[64]{0:T(128)} %param.9) | copy-start | bytes 772
  2.2 18.6 %all-to-all-start = ((bf16[48,8,128]{2,0,1:T(8,128)(2,1)}), bf16[48,8,128]{2,0,1:T(8,128)(2,1)S(1)}, u32[]{:S(2)}, u32[]{:S(2)}) async-start(bf16[48,8,128]{2,0,1:T(8,128)(2,1)} %copy_bitcast_fusion.5), calls=%async_computation | async-start | bytes 196608 | tf_op jit(solution)/shard_map/all_to_all | solution.py:83
  20.8 13.8 %all-to-all-start.2 = ((bf16[48,8,128]{2,0,1:T(8,128)(2,1)}), bf16[48,8,128]{2,0,1:T(8,128)(2,1)S(1)}, u32[]{:S(2)}, u32[]{:S(2)}) async-start(bf16[48,8,128]{2,0,1:T(8,128)(2,1)} %copy_bitcast_fusion.4), calls=%async_computation.2 | async-start | bytes 196608 | tf_op jit(solution)/shard_map/all_to_all | solution.py:84
  34.6 41.7 %copy-start.2 = (bf16[48,8,128]{2,0,1:T(8,128)(2,1)}, bf16[48,8,128]{2,0,1:T(8,128)(2,1)S(1)}, u32[]{:S(2)}) copy-start(bf16[48,8,128]{2,0,1:T(8,128)(2,1)S(1)} %all-to-all-done.2) | copy-start | bytes 294916
  34.6 15.5 %all-to-all-start.1 = ((bf16[48,8,512]{2,0,1:T(8,128)(2,1)}), bf16[48,8,512]{2,0,1:T(8,128)(2,1)S(1)}, u32[]{:S(2)}, u32[]{:S(2)}) async-start(bf16[48,8,512]{2,0,1:T(8,128)(2,1)} %bitcast.440), calls=%async_computation.1 | async-start | bytes 786432 | tf_op jit(solution)/shard_map/all_to_all | solution.py:82
  50.0 35.5 %all-to-all-start.4 = ((bf16[48,8,512]{2,0,1:T(8,128)(2,1)}), bf16[48,8,512]{2,0,1:T(8,128)(2,1)S(1)}, u32[]{:S(2)}, u32[]{:S(2)}) async-start(bf16[48,8,512]{2,0,1:T(8,128)(2,1)} %bitcast.439), calls=%async_computation.4 | async-start | bytes 786432 | tf_op jit(solution)/shard_map/all_to_all | solution.py:85
  53.9 20.5 %collective-permute-start = (bf16[2,384,128]{2,1,0:T(8,128)(2,1)S(1)}, bf16[2,384,128]{2,1,0:T(8,128)(2,1)S(1)}, u32[]{:S(2)}, u32[]{:S(2)}) collective-permute-start(bf16[2,384,128]{2,1,0:T(8,128)(2,1)S(1)} %pad_maximum_fusion), channel_id=1, source_target_pairs={{0,8},{8,16},{16,24},{24,32},{32,40},{40,48},{48,56},{56,64},{64,7... | collective-permute-start | bytes 589832 | tf_op jit(solution)/shard_map/ppermute | solution.py:18
  74.3 11.1 %copy-start.4 = (bf16[2,384,128]{2,1,0:T(8,128)(2,1)}, bf16[2,384,128]{2,1,0:T(8,128)(2,1)S(1)}, u32[]{:S(2)}) copy-start(bf16[2,384,128]{2,1,0:T(8,128)(2,1)S(1)} %collective-permute-done) | copy-start | bytes 589828
  74.3 9.2 %collective-permute-start.1 = (bf16[2,384,128]{2,1,0:T(8,128)(2,1)S(1)}, bf16[2,384,128]{2,1,0:T(8,128)(2,1)}, u32[]{:S(2)}, u32[]{:S(2)}) collective-permute-start(bf16[2,384,128]{2,1,0:T(8,128)(2,1)S(1)} %collective-permute-done), channel_id=1, source_target_pairs={{0,8},{8,16},{16,24},{24,32},{32,40},{40,48},{48,56},{56,64},{64,7... | collective-permute-start | bytes 589832 | tf_op jit(solution)/shard_map/ppermute | solution.py:18
  83.5 9.4 %collective-permute-start.2 = (bf16[2,384,128]{2,1,0:T(8,128)(2,1)}, bf16[2,384,128]{2,1,0:T(8,128)(2,1)}, u32[]{:S(2)}, u32[]{:S(2)}) collective-permute-start(bf16[2,384,128]{2,1,0:T(8,128)(2,1)} %collective-permute-done.1), channel_id=1, source_target_pairs={{0,8},{8,16},{16,24},{24,32},{32,40},{40,48},{48,56},{56,64},{64,7... | collective-permute-start | bytes 589832 | tf_op jit(solution)/shard_map/ppermute | solution.py:18
  86.3 2.0 copy-start.5
  88.3 13.9 %copy-start.1 = (pred[384,384]{0,1:T(8,128)(4,1)S(1)}, pred[384,384]{0,1:T(8,128)(4,1)}, u32[]{:S(2)}) copy-start(pred[384,384]{0,1:T(8,128)(4,1)} %get-tuple-element.18) | copy-start | bytes 442372
  92.9 9.3 %collective-permute-start.3 = (bf16[2,384,128]{2,1,0:T(8,128)(2,1)}, bf16[2,384,128]{2,1,0:T(8,128)(2,1)S(1)}, u32[]{:S(2)}, u32[]{:S(2)}) collective-permute-start(bf16[2,384,128]{2,1,0:T(8,128)(2,1)} %collective-permute-done.2), channel_id=1, source_target_pairs={{0,8},{8,16},{16,24},{24,32},{32,40},{40,48},{48,56},{56,64},{64,7... | collective-permute-start | bytes 589832 | tf_op jit(solution)/shard_map/ppermute | solution.py:18
  102.2 23.3 %copy-start.6 = (bf16[2,384,128]{2,1,0:T(8,128)(2,1)}, bf16[2,384,128]{2,1,0:T(8,128)(2,1)S(1)}, u32[]{:S(2)}) copy-start(bf16[2,384,128]{2,1,0:T(8,128)(2,1)S(1)} %collective-permute-done.3) | copy-start | bytes 589828
  106.7 0.9 copy-start.3
  115.2 18.9 %collective-permute-start.4 = (bf16[2,384,1,128]{3,1,2,0:T(8,128)(2,1)S(1)}, bf16[2,384,1,128]{3,1,2,0:T(8,128)(2,1)S(1)}, u32[]{:S(2)}, u32[]{:S(2)}) collective-permute-start(bf16[2,384,1,128]{3,1,2,0:T(8,128)(2,1)S(1)} %pad_maximum_fusion.1), channel_id=1, source_target_pairs={{8,0},{16,8},{24,16},{32,24},{40,32},{48,40},{56,48},{64,56},{72,6... | collective-permute-start | bytes 589832 | tf_op jit(solution)/shard_map/ppermute | solution.py:18
  119.4 15.0 %collective-permute-start.5 = (bf16[2,384,1,128]{3,1,2,0:T(8,128)(2,1)S(1)}, bf16[2,384,1,128]{3,1,2,0:T(8,128)(2,1)S(1)}, u32[]{:S(2)}, u32[]{:S(2)}) collective-permute-start(bf16[2,384,1,128]{3,1,2,0:T(8,128)(2,1)S(1)} %pad_maximum_fusion.2), channel_id=1, source_target_pairs={{16,0},{24,8},{32,16},{40,24},{48,32},{56,40},{64,48},{72,56},{80,... | collective-permute-start | bytes 589832 | tf_op jit(solution)/shard_map/ppermute | solution.py:18
  123.5 15.3 %collective-permute-start.6 = (bf16[2,384,1,128]{3,1,2,0:T(8,128)(2,1)S(1)}, bf16[2,384,1,128]{3,1,2,0:T(8,128)(2,1)S(1)}, u32[]{:S(2)}, u32[]{:S(2)}) collective-permute-start(bf16[2,384,1,128]{3,1,2,0:T(8,128)(2,1)S(1)} %pad_maximum_fusion.3), channel_id=1, source_target_pairs={{24,0},{32,8},{40,16},{48,24},{56,32},{64,40},{72,48},{80,56},{88,... | collective-permute-start | bytes 589832 | tf_op jit(solution)/shard_map/ppermute | solution.py:18
  126.8 17.8 %collective-permute-start.7 = (bf16[2,384,1,128]{3,1,2,0:T(8,128)(2,1)S(1)}, bf16[2,384,1,128]{3,1,2,0:T(8,128)(2,1)S(1)}, u32[]{:S(2)}, u32[]{:S(2)}) collective-permute-start(bf16[2,384,1,128]{3,1,2,0:T(8,128)(2,1)S(1)} %pad_maximum_fusion.4), channel_id=1, source_target_pairs={{32,0},{40,8},{48,16},{56,24},{64,32},{72,40},{80,48},{88,56},{96,... | collective-permute-start | bytes 589832 | tf_op jit(solution)/shard_map/ppermute | solution.py:18
  133.6 33.5 %copy-start.7 = (bf16[2,384,128]{2,1,0:T(8,128)(2,1)S(1)}, bf16[2,384,128]{2,1,0:T(8,128)(2,1)}, u32[]{:S(2)}) copy-start(bf16[2,384,128]{2,1,0:T(8,128)(2,1)} %copy-done.6) | copy-start | bytes 589828
  145.4 18.4 %all-to-all-start.7 = ((bf16[8,48,128]{2,1,0:T(8,128)(2,1)}), bf16[8,48,128]{2,1,0:T(8,128)(2,1)S(1)}, u32[]{:S(2)}, u32[]{:S(2)}) async-start(bf16[8,48,128]{2,1,0:T(8,128)(2,1)} %bitcast.140), calls=%async_computation.7 | async-start | bytes 196608 | tf_op jit(solution)/shard_map/all_to_all | solution.py:145
  163.8 15.4 %all-to-all-start.6 = ((bf16[8,48,128]{2,1,0:T(8,128)(2,1)}), bf16[8,48,128]{2,1,0:T(8,128)(2,1)S(1)}, u32[]{:S(2)}, u32[]{:S(2)}) async-start(bf16[8,48,128]{2,1,0:T(8,128)(2,1)} %bitcast.138), calls=%async_computation.6 | async-start | bytes 196608 | tf_op jit(solution)/shard_map/all_to_all | solution.py:144
  167.2 15.5 %copy-start.9 = (bf16[384,1,4,128]{0,3,2,1:T(8,128)(2,1)S(1)}, bf16[384,1,4,128]{0,3,2,1:T(8,128)(2,1)}, u32[]{:S(2)}) copy-start(bf16[384,1,4,128]{0,3,2,1:T(8,128)(2,1)} %get-tuple-element.32) | copy-start | bytes 1179652
  179.3 3.5 %copy-start.10 = (bf16[8,48,128]{2,1,0:T(8,128)(2,1)}, bf16[8,48,128]{2,1,0:T(8,128)(2,1)S(1)}, u32[]{:S(2)}) copy-start(bf16[8,48,128]{2,1,0:T(8,128)(2,1)S(1)} %all-to-all-done.6) | copy-start | bytes 294916
  179.3 16.7 %all-to-all-start.5 = ((bf16[8,48,512]{2,1,0:T(8,128)(2,1)}), bf16[8,48,512]{2,1,0:T(8,128)(2,1)S(1)}, u32[]{:S(2)}, u32[]{:S(2)}) async-start(bf16[8,48,512]{2,1,0:T(8,128)(2,1)} %all_to_all.116), calls=%async_computation.5 | async-start | bytes 786432 | tf_op jit(solution)/shard_map/all_to_all | solution.py:143
  182.7 17.4 %copy-start.11 = (bf16[8,48,128]{2,1,0:T(8,128)(2,1)S(1)}, bf16[8,48,128]{2,1,0:T(8,128)(2,1)}, u32[]{:S(2)}) copy-start(bf16[8,48,128]{2,1,0:T(8,128)(2,1)} %copy-done.10) | copy-start | bytes 294916
  196.0 15.3 %all-to-all-start.3 = ((bf16[8,48,512]{2,1,0:T(8,128)(2,1)}), bf16[8,48,512]{2,1,0:T(8,128)(2,1)S(1)}, u32[]{:S(2)}, u32[]{:S(2)}) async-start(bf16[8,48,512]{2,1,0:T(8,128)(2,1)} %all_to_all.109), calls=%async_computation.3 | async-start | bytes 786432 | tf_op jit(solution)/shard_map/all_to_all | solution.py:118
where the time goes:
time: 213 us; the launch traced here: 212 us
  waiting for transfers between devices  115 us (54%)
  starting transfers between devices  51.5 us (24%)
  matrix products  25.6 us (12%)
  local copies, waits for them, and re-layouts  12.7 us (6%)
  other arithmetic  5.68 us (3%)
    ppermute x8, waiting for transfers between devices, shifted(): return lax.ppermute(shard, axis, pairs)  43.8 us
    ppermute x8, starting transfers between devices, shifted(): return lax.ppermute(shard, axis, pairs)  15.7 us
    all_to_all x1, waiting for transfers between devices, local(): lax.all_to_all(grad_query_b, 'head', split_axis=0, concat_axis=1, tiled=T...  12.1 us
    all_to_all x1, waiting for transfers between devices, local(): lax.all_to_all(queries, 'head', split_axis=1, concat_axis=0, tiled=True)  11.2 us
    all_to_all x1, waiting for transfers between devices, local(): lax.all_to_all(grad_value_b, 'head', split_axis=0, concat_axis=1, tiled=T...  10.3 us
    all_to_all x1, waiting for transfers between devices, local(): lax.all_to_all(grad_key_b, 'head', split_axis=0, concat_axis=1, tiled=True)  10.2 us
    all_to_all x1, waiting for transfers between devices, local(): lax.all_to_all(attended.reshape(rows, -1), 'head', split_axis=0, concat_a...  9.75 us
    all_to_all x1, waiting for transfers between devices, local(): lax.all_to_all(keys, 'head', split_axis=1, concat_axis=0, tiled=True)  9.32 us
  transfers between devices with their start and end apart: 16, of which 14 were waited for; matrix products, arithmetic and copies ran while one was open for 12% of the time, Pallas kernels for 0%

commit v1 on v0

v1 whole, which is shorter than its diff:
```python
import math

import jax
import jax.numpy as jnp
from jax import lax
from jax.experimental import pallas as pl
from jax.experimental.pallas import tpu as pltpu
from jax.sharding import PartitionSpec as P

HEADS = 8
GROUP = 4
D = 128
ROWS = 384
SUB = 48
XS = 4
CHIP = 2 * ROWS
BACK = 2
OWN = BACK * CHIP
TK = 256
WINDOW = OWN + CHIP + TK
TQ = 128
QTILES = ROWS // TQ
LANES = TQ * GROUP
QDO = 2 * GROUP * D
SCALE = 1.0 / math.sqrt(D)
LOG2E = 1.4426950408889634
MASKED = -1e30

NT = (((1,), (1,)), ((), ()))
TN = (((0,), (0,)), ((), ()))

SMEM = pl.BlockSpec(memory_space=pltpu.SMEM)
VMEM = pl.BlockSpec(memory_space=pltpu.VMEM)


def dot(a, b):
    return jnp.dot(a, b, preferred_element_type=jnp.float32)


def dot_nt(a, b):
    return lax.dot_general(a, b, NT, preferred_element_type=jnp.float32)


def dot_tn(a, b):
    return lax.dot_general(a, b, TN, preferred_element_type=jnp.float32)


def pack_kernel(a_ref, b_ref, out_ref):
    width = a_ref.shape[1] // HEADS
    for head in range(HEADS):
        out_ref[head, :, :width] = a_ref[:, head * width : (head + 1) * width]
        out_ref[head, :, width:] = b_ref[:, head * width : (head + 1) * width]


def pack(a, b):
    width = a.shape[1] // HEADS
    return pl.pallas_call(
        pack_kernel,
        out_shape=jax.ShapeDtypeStruct((HEADS, SUB, 2 * width), jnp.bfloat16),
        in_specs=[VMEM] * 2,
        out_specs=VMEM,
        cost_estimate=pl.CostEstimate(
            flops=0, bytes_accessed=8 * HEADS * SUB * width, transcendentals=0
        ),
        name="pack",
    )(a, b)


def unpack_kernel(got_ref, a_ref, b_ref):
    width = a_ref.shape[1] // HEADS
    for head in range(HEADS):
        a_ref[:, head * width : (head + 1) * width] = got_ref[head, :, :width]
        b_ref[:, head * width : (head + 1) * width] = got_ref[head, :, width:]


def unpack(got):
    width = got.shape[2] // 2
    part = jax.ShapeDtypeStruct((SUB, HEADS * width), jnp.bfloat16)
    return pl.pallas_call(
        unpack_kernel,
        out_shape=(part, part),
        in_specs=[VMEM],
        out_specs=(VMEM, VMEM),
        cost_estimate=pl.CostEstimate(
            flops=0, bytes_accessed=8 * HEADS * SUB * width, transcendentals=0
        ),
        name="unpack",
    )(got)


def attention_kernel(half, span, start_ref, own_ref, qdo, *refs):
    kv_refs, odq, g_refs = refs[:6], refs[6], refs[7:13]
    kv, weights, weights_b, dprobs, dkv, acc_t = refs[13:]

    def stripes(j):
        return [
            (
                slice((i * XS + x) * SUB, (i * XS + x + 1) * SUB),
                pl.multiple_of(i * ROWS + (2 * x + (half[0] ^ j)) * SUB, SUB),
            )
            for i in range(2)
            for x in range(XS)
        ]

    kv[OWN + CHIP :, :] = jnp.zeros((TK, 2 * D), kv.dtype)
    for j in range(2):
        for held, place in stripes(j):
            for chip in range(BACK + 1):
                kv[pl.ds(place + OWN - chip * CHIP, SUB), :] = kv_refs[2 * chip + j][held, :]
    dkv[...] = jnp.zeros_like(dkv)
    key_iota = lax.broadcasted_iota(jnp.int32, (TK, LANES), 0)

    def query_tile(qi, _):
        rows = pl.ds(pl.multiple_of(qi * TQ, TQ), TQ)
        q = jnp.concatenate([qdo[rows, j * D : (j + 1) * D] for j in range(GROUP)], axis=0)
        do = jnp.concatenate(
            [qdo[rows, (GROUP + j) * D : (GROUP + j + 1) * D] for j in range(GROUP)], axis=0
        )
        start = start_ref[qi]
        own = own_ref[qi]
        low = span[qi] // TK
        high = span[QTILES + qi] // TK + 1
        steps = (high - low + 1) // 2

        def tiles(step):
            first = low + 2 * step
            return [pl.multiple_of((first + t) * TK, TK) for t in range(2)]

        def score(step, top):
            for base in tiles(step):
                keys = pl.ds(base, TK)
                s = dot_nt(kv[keys, :D], q)
                s = jnp.where((key_iota >= start - base) & (key_iota <= own - base), s, MASKED)
                weights[keys, :] = s
                top = jnp.maximum(top, jnp.max(s.reshape(TK // 8, 8, LANES), axis=0))
            return top

        top = lax.fori_loop(0, steps, score, jnp.full((8, LANES), MASKED, jnp.float32))
        top = jnp.max(top, axis=0, keepdims=True) * (SCALE * LOG2E)
        acc_t[...] = jnp.zeros_like(acc_t)

        def weigh(step, total):
            summed = 0.0
            for base in tiles(step):
                keys = pl.ds(base, TK)
                dprobs[keys, :] = dot_nt(kv[keys, D:], do)
                w = jnp.exp2(weights[keys, :] * (SCALE * LOG2E) - top)
                w_b = w.astype(jnp.bfloat16)
                weights_b[keys, :] = w_b
                summed += dot_tn(kv[keys, D:], w_b)
                total = total + jnp.sum(w.reshape(TK // 8, 8, LANES), axis=0)
            acc_t[...] += summed
            return total

        total = lax.fori_loop(0, steps, weigh, jnp.zeros((8, LANES), jnp.float32))
        inverse = 1.0 / jnp.sum(total, axis=0, keepdims=True)
        attended_t = (acc_t[...] * inverse).astype(jnp.bfloat16)
        delta = jnp.sum(
            do.T.astype(jnp.float32) * attended_t.astype(jnp.float32), axis=0, keepdims=True
        )
        inverse = inverse.astype(jnp.bfloat16)
        for j in range(GROUP):
            odq[rows, j * D : (j + 1) * D] = attended_t[:, j * TQ : (j + 1) * TQ].T
        acc_t[...] = jnp.zeros_like(acc_t)

        def grads(step, carry):
            summed = 0.0
            for base in tiles(step):
                keys = pl.ds(base, TK)
                probs = weights_b[keys, :] * inverse
                dscores = probs * (dprobs[keys, :] - delta).astype(jnp.bfloat16)
                summed += dot_tn(kv[keys, :D], dscores)
                dkv[keys, :D] += dot(dscores, q)
                dkv[keys, D:] += dot(probs, do)
            acc_t[...] += summed
            return carry

        lax.fori_loop(0, steps, grads, 0)
        dq_t = (acc_t[...] * SCALE).astype(jnp.bfloat16)
        for j in range(GROUP):
            odq[rows, (GROUP + j) * D : (GROUP + j + 1) * D] = dq_t[:, j * TQ : (j + 1) * TQ].T
        return 0

    lax.fori_loop(0, QTILES, query_tile, 0)
    for j in range(2):
        for held, place in stripes(j):
            for chip in range(BACK + 1):
                part = dkv[pl.ds(place + OWN - chip * CHIP, SUB), :]
                part = jnp.concatenate([part[:, :D] * SCALE, part[:, D:]], axis=1)
                ref = g_refs[2 * chip + j]
                ref[held, :] = part.astype(ref.dtype)


def attention(half, span, start, own, qdo, blocks):
    part = jax.ShapeDtypeStruct((ROWS, 2 * D), jnp.bfloat16)
    kept = jax.ShapeDtypeStruct((ROWS, 2 * D), jnp.float32)
    return pl.pallas_call(
        attention_kernel,
        out_shape=(jax.ShapeDtypeStruct((ROWS, QDO), jnp.bfloat16), kept, kept) + (part,) * 4,
        in_specs=[SMEM, SMEM] + [VMEM] * 9,
        out_specs=(VMEM,) * 7,
        scratch_shapes=[
            pltpu.VMEM((WINDOW, 2 * D), jnp.bfloat16),
            pltpu.VMEM((WINDOW, LANES), jnp.float32),
            pltpu.VMEM((WINDOW, LANES), jnp.bfloat16),
            pltpu.VMEM((WINDOW, LANES), jnp.float32),
            pltpu.VMEM((WINDOW, 2 * D), jnp.float32),
            pltpu.VMEM((D, LANES), jnp.float32),
        ],
        compiler_params=pltpu.CompilerParams(vmem_limit_bytes=44 << 20),
        cost_estimate=pl.CostEstimate(
            flops=6 * 2 * D * ROWS * GROUP * 1200, bytes_accessed=4 << 20, transcendentals=0
        ),
        name="attention",
    )(half, span, start, own, qdo, *blocks)


def query_spans(doc_lengths, place, half):
    ends = jnp.cumsum(doc_lengths)
    row = jnp.arange(ROWS, dtype=jnp.int32)
    stripe = row // SUB
    own = OWN + (stripe // XS) * ROWS + (2 * (stripe % XS) + half) * SUB + row % SUB
    base = (place // 2) * CHIP - OWN
    pos = own + base
    start = jnp.max(jnp.where(ends[None, :] <= pos[:, None], ends[None, :], 0), axis=1) - base
    span = jnp.concatenate([start[::TQ], own[TQ - 1 :: TQ]])

    def tiled(v):
        v = jnp.broadcast_to(v.reshape(QTILES, 1, 1, TQ), (QTILES, 1, GROUP, TQ))
        return v.reshape(QTILES, 1, LANES)

    return span, tiled(start), tiled(own)


CTX = ("y_low", "z", "core")


def exchanged(pieces):
    return lax.all_to_all(pieces, ("core", "x"), split_axis=0, concat_axis=0, tiled=True)


def shifted(shard, by):
    peers = lax.axis_size(CTX)
    pairs = [(i, i + by) for i in range(peers) if 0 <= i + by < peers]
    return lax.ppermute(shard, CTX, pairs)


def half_swapped(shard):
    return lax.ppermute(shard, "y_high", [(0, 1), (1, 0)])


def local(queries, keys, values, output_gradient, doc_lengths):
    place = lax.axis_index(CTX)
    half = lax.axis_index("y_high").astype(jnp.int32)
    own = exchanged(pack(keys, values)).reshape(ROWS, 2 * D)
    theirs = half_swapped(own)
    own1, own2 = shifted(own, 2), shifted(own, 4)
    qdo = exchanged(pack(queries, output_gradient)).reshape(ROWS, QDO)
    theirs1, theirs2 = shifted(theirs, 2), shifted(theirs, 4)
    span, start, own_pos = query_spans(doc_lengths, place, half)

    blocks = (own, theirs, own1, theirs1, own2, theirs2)
    odq, g0, h0, g1, h1, g2, h2 = attention(half.reshape(1), span, start, own_pos, qdo, blocks)
    h1, h2 = shifted(h1, -2), shifted(h2, -4)
    odq_rows = exchanged(odq.reshape(HEADS, SUB, QDO))
    theirs = (h0 + h1.astype(jnp.float32) + h2.astype(jnp.float32)).astype(jnp.bfloat16)
    theirs, g1, g2 = lax.optimization_barrier((theirs, g1, g2))
    got = half_swapped(theirs).astype(jnp.float32)
    g1, g2 = shifted(g1, -2), shifted(g2, -4)
    total = g0 + g1.astype(jnp.float32) + g2.astype(jnp.float32) + got
    odq_rows, total = lax.optimization_barrier((odq_rows, total.astype(jnp.bfloat16)))
    dkv_rows = exchanged(total.reshape(HEADS, SUB, 2 * D))
    return (*unpack(odq_rows), *unpack(dkv_rows))


def solution(mesh):
    mesh = jax.sharding.Mesh(
        mesh.devices.reshape(4, 8, 2, 4, 2), ("y_low", "z", "core", "x", "y_high")
    )
    spec = P(("y_low", "z", "core", "x", "y_high"), None)
    return jax.shard_map(
        local,
        mesh=mesh,
        in_specs=(spec, spec, spec, spec, P()),
        out_specs=(spec, spec, spec, spec),
        check_vma=False,
    )
```

time: 213 us -> 135 us (0.63)
  the two profiles are of different devices: /device:TPU:16 before, /device:TPU:17 now
where the time goes in v1:
time: 135 us; the launch traced here: 134 us
  starting transfers between devices  66.7 us (49%)
  waiting for transfers between devices  46.8 us (35%)
  Pallas kernels  17.1 us (13%)
  local copies, waits for them, and re-layouts  1.62 us (1%)
    ppermute x8, waiting for transfers between devices, shifted(): return lax.ppermute(shard, CTX, pairs)  40.1 us
    ppermute x8, starting transfers between devices, shifted(): return lax.ppermute(shard, CTX, pairs)  39.9 us
    all_to_all x4, starting transfers between devices, exchanged(): lax.all_to_all(pieces, ('core', 'x'), split_axis=0, concat_axis=0, tiled=...  19.1 us
    pallas_call x1, Pallas kernels, attention(): pl.pallas_call(attention_kernel, out_shape=(jax.ShapeDtypeStruct((ROWS, Q...  9.72 us
    ppermute x2, starting transfers between devices, half_swapped(): return lax.ppermute(shard, 'y_high', [(0, 1), (1, 0)])  7.58 us
    all_to_all x4, waiting for transfers between devices, exchanged(): lax.all_to_all(pieces, ('core', 'x'), split_axis=0, concat_axis=0, tiled=...  6.66 us
    pallas_call x2, Pallas kernels, pack(): pl.pallas_call(pack_kernel, out_shape=jax.ShapeDtypeStruct((HEADS, SUB, 2...  3.72 us
    pallas_call x2, Pallas kernels, unpack(): pl.pallas_call(unpack_kernel, out_shape=(part, part), in_specs=[VMEM], ou...  3.7 us
  transfers between devices with their start and end apart: 14, of which 7 were waited for; matrix products, arithmetic and copies ran while one was open for 1% of the time, Pallas kernels for 3%

profile of v1, /device:TPU:17, one launch (start us, length us, event | category | flops | bytes accessed | tf_op | source)
XLA Modules:
  0.0 134.3 jit_solution(6846521366244033738)
XLA Ops:
  0.6 1.7 %pack.3 = bf16[8,48,256]{2,1,0:T(8,128)(2,1)} custom-call(bf16[48,1024]{1,0:T(8,128)(2,1)} %a_ref.3, bf16[48,1024]{1,0:T(8,128)(2,1)} %b_ref.3), custom_call_target="tpu_custom_call" | custom-call | bytes 393216 | tf_op jit(solution)/shard_map/pack/pallas_call | solution.py:57
  2.3 5.0 %all-to-all-start.1 = ((bf16[8,48,256]{2,1,0:T(8,128)(2,1)}), bf16[8,48,256]{2,1,0:T(8,128)(2,1)S(1)}, u32[]{:S(2)}, u32[]{:S(2)}) async-start(bf16[8,48,256]{2,1,0:T(8,128)(2,1)} %pack.3), calls=%async_computation.1 | async-start | bytes 393216 | tf_op jit(solution)/shard_map/all_to_all | solution.py:239
  7.3 0.0 copy-start.2
  7.3 0.7 copy-done.2
  7.9 0.1 copy.11
  8.0 0.1 reduce-window.8
  8.1 0.1 reduce
  8.2 2.1 %pack.2 = bf16[8,48,1024]{2,1,0:T(8,128)(2,1)} custom-call(bf16[48,4096]{1,0:T(8,128)(2,1)} %a_ref.2, bf16[48,4096]{1,0:T(8,128)(2,1)} %b_ref.2), custom_call_target="tpu_custom_call" | custom-call | bytes 1572864 | tf_op jit(solution)/shard_map/pack/pallas_call | solution.py:57
  10.3 2.8 %all-to-all-done.1 = bf16[8,48,256]{2,1,0:T(8,128)(2,1)S(1)} async-done(((bf16[8,48,256]{2,1,0:T(8,128)(2,1)}), bf16[8,48,256]{2,1,0:T(8,128)(2,1)S(1)}, u32[]{:S(2)}, u32[]{:S(2)}) %all-to-all-start.1) | async-done | bytes 196640 | tf_op jit(solution)/shard_map/all_to_all | solution.py:239
  13.1 3.9 %all-to-all-start = ((bf16[8,48,1024]{2,1,0:T(8,128)(2,1)}), bf16[8,48,1024]{2,1,0:T(8,128)(2,1)S(1)}, u32[]{:S(2)}, u32[]{:S(2)}) async-start(bf16[8,48,1024]{2,1,0:T(8,128)(2,1)} %pack.2), calls=%async_computation | async-start | bytes 1572864 | tf_op jit(solution)/shard_map/all_to_all | solution.py:239
  17.0 0.1 select_reduce_fusion
  17.1 0.1 slice.7
  17.2 0.1 slice.6
  17.3 5.7 %collective-permute-start = (bf16[384,256]{1,0:T(8,128)(2,1)S(1)}, bf16[384,256]{1,0:T(8,128)(2,1)S(1)}, u32[]{:S(2)}, u32[]{:S(2)}) collective-permute-start(bf16[384,256]{1,0:T(8,128)(2,1)S(1)} %bitcast.11), channel_id=1, source_target_pairs={{0,1},{1,0},{2,3},{3,2},{4,5},{5,4},{6,7},{7,6},{8,9},{9,8},{10,11... | collective-permute-start | bytes 589832 | tf_op jit(solution)/shard_map/ppermute | solution.py:249
  23.0 0.1 pad_add_fusion.span
  23.1 5.8 %collective-permute-start.3 = (bf16[384,256]{1,0:T(8,128)(2,1)S(1)}, bf16[384,256]{1,0:T(8,128)(2,1)S(1)}, u32[]{:S(2)}, u32[]{:S(2)}) collective-permute-start(bf16[384,256]{1,0:T(8,128)(2,1)S(1)} %bitcast.12), channel_id=1, source_target_pairs={{0,32},{8,40},{16,48},{24,56},{32,64},{40,72},{48,80},{56,88},{64,... | collective-permute-start | bytes 589832 | tf_op jit(solution)/shard_map/ppermute | solution.py:245
  28.9 4.0 %collective-permute-start.1 = (bf16[384,256]{1,0:T(8,128)(2,1)S(1)}, bf16[384,256]{1,0:T(8,128)(2,1)S(1)}, u32[]{:S(2)}, u32[]{:S(2)}) collective-permute-start(bf16[384,256]{1,0:T(8,128)(2,1)S(1)} %bitcast.13), channel_id=1, source_target_pairs={{0,16},{8,24},{16,32},{24,40},{32,48},{40,56},{48,64},{56,72},{64,... | collective-permute-start | bytes 589832 | tf_op jit(solution)/shard_map/ppermute | solution.py:245
  32.9 0.0 collective-permute-done.refs_1_
  32.9 7.0 %collective-permute-start.4 = (bf16[384,256]{1,0:T(8,128)(2,1)S(1)}, bf16[384,256]{1,0:T(8,128)(2,1)S(1)}, u32[]{:S(2)}, u32[]{:S(2)}) collective-permute-start(bf16[384,256]{1,0:T(8,128)(2,1)S(1)} %collective-permute-done.refs_1_), channel_id=1, source_target_pairs={{0,32},{8,40},{16,48},{24,56},{32,64},{40,72},{48,80},{56,88},{64,... | collective-permute-start | bytes 589832 | tf_op jit(solution)/shard_map/ppermute | solution.py:245
  39.9 4.0 %collective-permute-start.2 = (bf16[384,256]{1,0:T(8,128)(2,1)S(1)}, bf16[384,256]{1,0:T(8,128)(2,1)S(1)}, u32[]{:S(2)}, u32[]{:S(2)}) collective-permute-start(bf16[384,256]{1,0:T(8,128)(2,1)S(1)} %collective-permute-done.refs_1_), channel_id=1, source_target_pairs={{0,16},{8,24},{16,32},{24,40},{32,48},{40,56},{48,64},{56,72},{64,... | collective-permute-start | bytes 589832 | tf_op jit(solution)/shard_map/ppermute | solution.py:245
  44.0 6.5 %collective-permute-done.3.refs_4_ = bf16[384,256]{1,0:T(8,128)(2,1)S(1)} collective-permute-done((bf16[384,256]{1,0:T(8,128)(2,1)S(1)}, bf16[384,256]{1,0:T(8,128)(2,1)S(1)}, u32[]{:S(2)}, u32[]{:S(2)}) %collective-permute-start.3) | collective-permute-done | bytes 196640 | tf_op jit(solution)/shard_map/ppermute | solution.py:245
  50.5 8.6 %collective-permute-done.1.refs_2_ = bf16[384,256]{1,0:T(8,128)(2,1)S(1)} collective-permute-done((bf16[384,256]{1,0:T(8,128)(2,1)S(1)}, bf16[384,256]{1,0:T(8,128)(2,1)S(1)}, u32[]{:S(2)}, u32[]{:S(2)}) %collective-permute-start.1) | collective-permute-done | bytes 196640 | tf_op jit(solution)/shard_map/ppermute | solution.py:245
  59.1 0.0 collective-permute-done.4.refs_5_
  59.1 8.7 %collective-permute-done.2.refs_3_ = bf16[384,256]{1,0:T(8,128)(2,1)S(1)} collective-permute-done((bf16[384,256]{1,0:T(8,128)(2,1)S(1)}, bf16[384,256]{1,0:T(8,128)(2,1)S(1)}, u32[]{:S(2)}, u32[]{:S(2)}) %collective-permute-start.2) | collective-permute-done | bytes 196640 | tf_op jit(solution)/shard_map/ppermute | solution.py:245
  67.8 0.0 all-to-all-done
  67.8 9.7 %attention.1 = (bf16[384,1024]{1,0:T(8,128)(2,1)}, f32[384,256]{1,0:T(8,128)S(1)}, f32[384,256]{1,0:T(8,128)S(1)}, bf16[384,256]{1,0:T(8,128)(2,1)S(1)}, bf16[38...) custom-call(s32[1]{0:T(128)} %bitcast.half, s32[6]{0:T(128)S(1)} %pad_add_fusion.span, ...), custom_call_target="tpu_custom_call" | custom-call | flops 2831155200 | bytes 4194304 | tf_op jit(solution)/shard_map/attention/pallas_call | solution.py:197
  77.5 8.2 %collective-permute-start.5 = (bf16[384,256]{1,0:T(8,128)(2,1)S(1)}, bf16[384,256]{1,0:T(8,128)(2,1)S(1)}, u32[]{:S(2)}, u32[]{:S(2)}) collective-permute-start(bf16[384,256]{1,0:T(8,128)(2,1)S(1)} %get-tuple-element.23), channel_id=1, source_target_pairs={{16,0},{24,8},{32,16},{40,24},{48,32},{56,40},{64,48},{72,56},{80,... | collective-permute-start | bytes 589832 | tf_op jit(solution)/shard_map/ppermute | solution.py:245
  85.7 1.9 %collective-permute-start.6 = (bf16[384,256]{1,0:T(8,128)(2,1)S(1)}, bf16[384,256]{1,0:T(8,128)(2,1)S(1)}, u32[]{:S(2)}, u32[]{:S(2)}) collective-permute-start(bf16[384,256]{1,0:T(8,128)(2,1)S(1)} %get-tuple-element.24), channel_id=1, source_target_pairs={{32,0},{40,8},{48,16},{56,24},{64,32},{72,40},{80,48},{88,56},{96,... | collective-permute-start | bytes 589832 | tf_op jit(solution)/shard_map/ppermute | solution.py:245
  87.6 4.9 %all-to-all-start.2 = ((bf16[8,48,1024]{2,1,0:T(8,128)(2,1)}), bf16[8,48,1024]{2,1,0:T(8,128)(2,1)S(1)}, u32[]{:S(2)}, u32[]{:S(2)}) async-start(bf16[8,48,1024]{2,1,0:T(8,128)(2,1)} %bitcast.7), calls=%async_computation.2 | async-start | bytes 1572864 | tf_op jit(solution)/shard_map/all_to_all | solution.py:239
  92.5 0.0 collective-permute-done.5
  92.5 5.3 %collective-permute-done.6 = bf16[384,256]{1,0:T(8,128)(2,1)S(1)} collective-permute-done((bf16[384,256]{1,0:T(8,128)(2,1)S(1)}, bf16[384,256]{1,0:T(8,128)(2,1)S(1)}, u32[]{:S(2)}, u32[]{:S(2)}) %collective-permute-start.6) | collective-permute-done | bytes 196640 | tf_op jit(solution)/shard_map/ppermute | solution.py:245
  97.8 0.1 add_convert_fusion.1
  97.9 3.2 %collective-permute-start.7 = (bf16[384,256]{1,0:T(8,128)(2,1)S(1)}, bf16[384,256]{1,0:T(8,128)(2,1)S(1)}, u32[]{:S(2)}, u32[]{:S(2)}) collective-permute-start(bf16[384,256]{1,0:T(8,128)(2,1)S(1)} %get-tuple-element.27), channel_id=1, source_target_pairs={{16,0},{24,8},{32,16},{40,24},{48,32},{56,40},{64,48},{72,56},{80,... | collective-permute-start | bytes 589832 | tf_op jit(solution)/shard_map/ppermute | solution.py:245
  101.1 5.8 %collective-permute-start.8 = (bf16[384,256]{1,0:T(8,128)(2,1)S(1)}, bf16[384,256]{1,0:T(8,128)(2,1)S(1)}, u32[]{:S(2)}, u32[]{:S(2)}) collective-permute-start(bf16[384,256]{1,0:T(8,128)(2,1)S(1)} %get-tuple-element.28), channel_id=1, source_target_pairs={{32,0},{40,8},{48,16},{56,24},{64,32},{72,40},{80,48},{88,56},{96,... | collective-permute-start | bytes 589832 | tf_op jit(solution)/shard_map/ppermute | solution.py:245
  106.9 1.9 %collective-permute-start.9 = (bf16[384,256]{1,0:T(8,128)(2,1)S(1)}, bf16[384,256]{1,0:T(8,128)(2,1)S(1)}, u32[]{:S(2)}, u32[]{:S(2)}) collective-permute-start(bf16[384,256]{1,0:T(8,128)(2,1)S(1)} %add_convert_fusion.1), channel_id=1, source_target_pairs={{0,1},{1,0},{2,3},{3,2},{4,5},{5,4},{6,7},{7,6},{8,9},{9,8},{10,11... | collective-permute-start | bytes 589832 | tf_op jit(solution)/shard_map/ppermute | solution.py:249
  108.9 0.0 collective-permute-done.7
  108.9 11.0 %collective-permute-done.8 = bf16[384,256]{1,0:T(8,128)(2,1)S(1)} collective-permute-done((bf16[384,256]{1,0:T(8,128)(2,1)S(1)}, bf16[384,256]{1,0:T(8,128)(2,1)S(1)}, u32[]{:S(2)}, u32[]{:S(2)}) %collective-permute-start.8) | collective-permute-done | bytes 196640 | tf_op jit(solution)/shard_map/ppermute | solution.py:245
  119.9 0.0 collective-permute-done.9
  119.9 0.8 add_convert_fusion
  120.7 0.0 all-to-all-done.2.got_ref
  120.7 0.0 copy-start
  120.7 5.4 %all-to-all-start.3 = ((bf16[8,48,256]{2,1,0:T(8,128)(2,1)}), bf16[8,48,256]{2,1,0:T(8,128)(2,1)S(1)}, u32[]{:S(2)}, u32[]{:S(2)}) async-start(bf16[8,48,256]{2,1,0:T(8,128)(2,1)} %bitcast.8), calls=%async_computation.3 | async-start | bytes 393216 | tf_op jit(solution)/shard_map/all_to_all | solution.py:239
  126.0 0.0 copy-done
  126.0 2.1 %unpack.2 = (bf16[48,4096]{1,0:T(8,128)(2,1)}, bf16[48,4096]{1,0:T(8,128)(2,1)}) custom-call(bf16[8,48,1024]{2,1,0:T(8,128)(2,1)} %copy-done), custom_call_target="tpu_custom_call" | custom-call | bytes 1572864 | tf_op jit(solution)/shard_map/unpack/pallas_call | solution.py:79
  128.1 3.8 %all-to-all-done.3.got_ref = bf16[8,48,256]{2,1,0:T(8,128)(2,1)S(1)} async-done(((bf16[8,48,256]{2,1,0:T(8,128)(2,1)}), bf16[8,48,256]{2,1,0:T(8,128)(2,1)S(1)}, u32[]{:S(2)}, u32[]{:S(2)}) %all-to-all-start.3) | async-done | bytes 196640 | tf_op jit(solution)/shard_map/all_to_all | solution.py:239
  131.9 0.0 copy-start.1
  131.9 0.7 copy-done.1
  132.6 1.6 %unpack.3 = (bf16[48,1024]{1,0:T(8,128)(2,1)}, bf16[48,1024]{1,0:T(8,128)(2,1)}) custom-call(bf16[8,48,256]{2,1,0:T(8,128)(2,1)} %copy-done.1), custom_call_target="tpu_custom_call" | custom-call | bytes 393216 | tf_op jit(solution)/shard_map/unpack/pallas_call | solution.py:79
  (6 shorter events, 0.1 us)
Async XLA Ops:
  2.3 10.9 %all-to-all-start.1 = ((bf16[8,48,256]{2,1,0:T(8,128)(2,1)}), bf16[8,48,256]{2,1,0:T(8,128)(2,1)S(1)}, u32[]{:S(2)}, u32[]{:S(2)}) async-start(bf16[8,48,256]{2,1,0:T(8,128)(2,1)} %pack.3), calls=%async_computation.1 | async-start | bytes 393216 | tf_op jit(solution)/shard_map/all_to_all | solution.py:239
  7.3 0.7 copy-start.2
  13.1 54.6 %all-to-all-start = ((bf16[8,48,1024]{2,1,0:T(8,128)(2,1)}), bf16[8,48,1024]{2,1,0:T(8,128)(2,1)S(1)}, u32[]{:S(2)}, u32[]{:S(2)}) async-start(bf16[8,48,1024]{2,1,0:T(8,128)(2,1)} %pack.2), calls=%async_computation | async-start | bytes 1572864 | tf_op jit(solution)/shard_map/all_to_all | solution.py:239
  17.3 15.6 %collective-permute-start = (bf16[384,256]{1,0:T(8,128)(2,1)S(1)}, bf16[384,256]{1,0:T(8,128)(2,1)S(1)}, u32[]{:S(2)}, u32[]{:S(2)}) collective-permute-start(bf16[384,256]{1,0:T(8,128)(2,1)S(1)} %bitcast.11), channel_id=1, source_target_pairs={{0,1},{1,0},{2,3},{3,2},{4,5},{5,4},{6,7},{7,6},{8,9},{9,8},{10,11... | collective-permute-start | bytes 589832 | tf_op jit(solution)/shard_map/ppermute | solution.py:249
  23.1 27.4 %collective-permute-start.3 = (bf16[384,256]{1,0:T(8,128)(2,1)S(1)}, bf16[384,256]{1,0:T(8,128)(2,1)S(1)}, u32[]{:S(2)}, u32[]{:S(2)}) collective-permute-start(bf16[384,256]{1,0:T(8,128)(2,1)S(1)} %bitcast.12), channel_id=1, source_target_pairs={{0,32},{8,40},{16,48},{24,56},{32,64},{40,72},{48,80},{56,88},{64,... | collective-permute-start | bytes 589832 | tf_op jit(solution)/shard_map/ppermute | solution.py:245
  28.9 30.2 %collective-permute-start.1 = (bf16[384,256]{1,0:T(8,128)(2,1)S(1)}, bf16[384,256]{1,0:T(8,128)(2,1)S(1)}, u32[]{:S(2)}, u32[]{:S(2)}) collective-permute-start(bf16[384,256]{1,0:T(8,128)(2,1)S(1)} %bitcast.13), channel_id=1, source_target_pairs={{0,16},{8,24},{16,32},{24,40},{32,48},{40,56},{48,64},{56,72},{64,... | collective-permute-start | bytes 589832 | tf_op jit(solution)/shard_map/ppermute | solution.py:245
  32.9 26.2 %collective-permute-start.4 = (bf16[384,256]{1,0:T(8,128)(2,1)S(1)}, bf16[384,256]{1,0:T(8,128)(2,1)S(1)}, u32[]{:S(2)}, u32[]{:S(2)}) collective-permute-start(bf16[384,256]{1,0:T(8,128)(2,1)S(1)} %collective-permute-done.refs_1_), channel_id=1, source_target_pairs={{0,32},{8,40},{16,48},{24,56},{32,64},{40,72},{48,80},{56,88},{64,... | collective-permute-start | bytes 589832 | tf_op jit(solution)/shard_map/ppermute | solution.py:245
  39.9 27.8 %collective-permute-start.2 = (bf16[384,256]{1,0:T(8,128)(2,1)S(1)}, bf16[384,256]{1,0:T(8,128)(2,1)S(1)}, u32[]{:S(2)}, u32[]{:S(2)}) collective-permute-start(bf16[384,256]{1,0:T(8,128)(2,1)S(1)} %collective-permute-done.refs_1_), channel_id=1, source_target_pairs={{0,16},{8,24},{16,32},{24,40},{32,48},{40,56},{48,64},{56,72},{64,... | collective-permute-start | bytes 589832 | tf_op jit(solution)/shard_map/ppermute | solution.py:245
  77.5 15.1 %collective-permute-start.5 = (bf16[384,256]{1,0:T(8,128)(2,1)S(1)}, bf16[384,256]{1,0:T(8,128)(2,1)S(1)}, u32[]{:S(2)}, u32[]{:S(2)}) collective-permute-start(bf16[384,256]{1,0:T(8,128)(2,1)S(1)} %get-tuple-element.23), channel_id=1, source_target_pairs={{16,0},{24,8},{32,16},{40,24},{48,32},{56,40},{64,48},{72,56},{80,... | collective-permute-start | bytes 589832 | tf_op jit(solution)/shard_map/ppermute | solution.py:245
  85.7 12.2 %collective-permute-start.6 = (bf16[384,256]{1,0:T(8,128)(2,1)S(1)}, bf16[384,256]{1,0:T(8,128)(2,1)S(1)}, u32[]{:S(2)}, u32[]{:S(2)}) collective-permute-start(bf16[384,256]{1,0:T(8,128)(2,1)S(1)} %get-tuple-element.24), channel_id=1, source_target_pairs={{32,0},{40,8},{48,16},{56,24},{64,32},{72,40},{80,48},{88,56},{96,... | collective-permute-start | bytes 589832 | tf_op jit(solution)/shard_map/ppermute | solution.py:245
  87.6 33.1 %all-to-all-start.2 = ((bf16[8,48,1024]{2,1,0:T(8,128)(2,1)}), bf16[8,48,1024]{2,1,0:T(8,128)(2,1)S(1)}, u32[]{:S(2)}, u32[]{:S(2)}) async-start(bf16[8,48,1024]{2,1,0:T(8,128)(2,1)} %bitcast.7), calls=%async_computation.2 | async-start | bytes 1572864 | tf_op jit(solution)/shard_map/all_to_all | solution.py:239
  97.9 11.0 %collective-permute-start.7 = (bf16[384,256]{1,0:T(8,128)(2,1)S(1)}, bf16[384,256]{1,0:T(8,128)(2,1)S(1)}, u32[]{:S(2)}, u32[]{:S(2)}) collective-permute-start(bf16[384,256]{1,0:T(8,128)(2,1)S(1)} %get-tuple-element.27), channel_id=1, source_target_pairs={{16,0},{24,8},{32,16},{40,24},{48,32},{56,40},{64,48},{72,56},{80,... | collective-permute-start | bytes 589832 | tf_op jit(solution)/shard_map/ppermute | solution.py:245
  101.1 18.8 %collective-permute-start.8 = (bf16[384,256]{1,0:T(8,128)(2,1)S(1)}, bf16[384,256]{1,0:T(8,128)(2,1)S(1)}, u32[]{:S(2)}, u32[]{:S(2)}) collective-permute-start(bf16[384,256]{1,0:T(8,128)(2,1)S(1)} %get-tuple-element.28), channel_id=1, source_target_pairs={{32,0},{40,8},{48,16},{56,24},{64,32},{72,40},{80,48},{88,56},{96,... | collective-permute-start | bytes 589832 | tf_op jit(solution)/shard_map/ppermute | solution.py:245
  106.9 12.9 %collective-permute-start.9 = (bf16[384,256]{1,0:T(8,128)(2,1)S(1)}, bf16[384,256]{1,0:T(8,128)(2,1)S(1)}, u32[]{:S(2)}, u32[]{:S(2)}) collective-permute-start(bf16[384,256]{1,0:T(8,128)(2,1)S(1)} %add_convert_fusion.1), channel_id=1, source_target_pairs={{0,1},{1,0},{2,3},{3,2},{4,5},{5,4},{6,7},{7,6},{8,9},{9,8},{10,11... | collective-permute-start | bytes 589832 | tf_op jit(solution)/shard_map/ppermute | solution.py:249
  120.7 5.4 %copy-start = (bf16[8,48,1024]{2,1,0:T(8,128)(2,1)}, bf16[8,48,1024]{2,1,0:T(8,128)(2,1)S(1)}, u32[]{:S(2)}) copy-start(bf16[8,48,1024]{2,1,0:T(8,128)(2,1)S(1)} %all-to-all-done.2.got_ref) | copy-start | bytes 2359300
  120.7 11.3 %all-to-all-start.3 = ((bf16[8,48,256]{2,1,0:T(8,128)(2,1)}), bf16[8,48,256]{2,1,0:T(8,128)(2,1)S(1)}, u32[]{:S(2)}, u32[]{:S(2)}) async-start(bf16[8,48,256]{2,1,0:T(8,128)(2,1)} %bitcast.8), calls=%async_computation.3 | async-start | bytes 393216 | tf_op jit(solution)/shard_map/all_to_all | solution.py:239
  131.9 0.7 copy-start.1

commit v2 on v1

--- a/solution.py
+++ b/solution.py
@@ -17,6 +17,7 @@
 BACK = 2
 OWN = BACK * CHIP
 TK = 256
+STEP = 2 * TK
 WINDOW = OWN + CHIP + TK
 TQ = 128
 QTILES = ROWS // TQ
@@ -108,7 +109,7 @@
             for chip in range(BACK + 1):
                 kv[pl.ds(place + OWN - chip * CHIP, SUB), :] = kv_refs[2 * chip + j][held, :]
     dkv[...] = jnp.zeros_like(dkv)
-    key_iota = lax.broadcasted_iota(jnp.int32, (TK, LANES), 0)
+    key_iota = lax.broadcasted_iota(jnp.int32, (STEP, LANES), 0)
 
     def query_tile(qi, _):
         rows = pl.ds(pl.multiple_of(qi * TQ, TQ), TQ)
@@ -122,35 +123,29 @@
         high = span[QTILES + qi] // TK + 1
         steps = (high - low + 1) // 2
 
-        def tiles(step):
-            first = low + 2 * step
-            return [pl.multiple_of((first + t) * TK, TK) for t in range(2)]
+        def place(step):
+            return pl.multiple_of((low + 2 * step) * TK, TK)
 
         def score(step, top):
-            for base in tiles(step):
-                keys = pl.ds(base, TK)
-                s = dot_nt(kv[keys, :D], q)
-                s = jnp.where((key_iota >= start - base) & (key_iota <= own - base), s, MASKED)
-                weights[keys, :] = s
-                top = jnp.maximum(top, jnp.max(s.reshape(TK // 8, 8, LANES), axis=0))
-            return top
+            base = place(step)
+            keys = pl.ds(base, STEP)
+            s = dot_nt(kv[keys, :D], q)
+            s = jnp.where((key_iota >= start - base) & (key_iota <= own - base), s, MASKED)
+            weights[keys, :] = s
+            return jnp.maximum(top, jnp.max(s.reshape(STEP // 8, 8, LANES), axis=0))
 
         top = lax.fori_loop(0, steps, score, jnp.full((8, LANES), MASKED, jnp.float32))
         top = jnp.max(top, axis=0, keepdims=True) * (SCALE * LOG2E)
         acc_t[...] = jnp.zeros_like(acc_t)
 
         def weigh(step, total):
-            summed = 0.0
-            for base in tiles(step):
-                keys = pl.ds(base, TK)
-                dprobs[keys, :] = dot_nt(kv[keys, D:], do)
-                w = jnp.exp2(weights[keys, :] * (SCALE * LOG2E) - top)
-                w_b = w.astype(jnp.bfloat16)
-                weights_b[keys, :] = w_b
-                summed += dot_tn(kv[keys, D:], w_b)
-                total = total + jnp.sum(w.reshape(TK // 8, 8, LANES), axis=0)
-            acc_t[...] += summed
-            return total
+            keys = pl.ds(place(step), STEP)
+            dprobs[keys, :] = dot_nt(kv[keys, D:], do)
+            w = jnp.exp2(weights[keys, :] * (SCALE * LOG2E) - top)
+            w_b = w.astype(jnp.bfloat16)
+            weights_b[keys, :] = w_b
+            acc_t[...] += dot_tn(kv[keys, D:], w_b)
+            return total + jnp.sum(w.reshape(STEP // 8, 8, LANES), axis=0)
 
         total = lax.fori_loop(0, steps, weigh, jnp.zeros((8, LANES), jnp.float32))
         inverse = 1.0 / jnp.sum(total, axis=0, keepdims=True)
@@ -164,15 +159,12 @@
         acc_t[...] = jnp.zeros_like(acc_t)
 
         def grads(step, carry):
-            summed = 0.0
-            for base in tiles(step):
-                keys = pl.ds(base, TK)
-                probs = weights_b[keys, :] * inverse
-                dscores = probs * (dprobs[keys, :] - delta).astype(jnp.bfloat16)
-                summed += dot_tn(kv[keys, :D], dscores)
-                dkv[keys, :D] += dot(dscores, q)
-                dkv[keys, D:] += dot(probs, do)
-            acc_t[...] += summed
+            keys = pl.ds(place(step), STEP)
+            probs = weights_b[keys, :] * inverse
+            dscores = probs * (dprobs[keys, :] - delta).astype(jnp.bfloat16)
+            acc_t[...] += dot_tn(kv[keys, :D], dscores)
+            dkv[keys, :D] += dot(dscores, q)
+            dkv[keys, D:] += dot(probs, do)
             return carry
 
         lax.fori_loop(0, steps, grads, 0)
@@ -264,7 +256,6 @@
     h1, h2 = shifted(h1, -2), shifted(h2, -4)
     odq_rows = exchanged(odq.reshape(HEADS, SUB, QDO))
     theirs = (h0 + h1.astype(jnp.float32) + h2.astype(jnp.float32)).astype(jnp.bfloat16)
-    theirs, g1, g2 = lax.optimization_barrier((theirs, g1, g2))
     got = half_swapped(theirs).astype(jnp.float32)
     g1, g2 = shifted(g1, -2), shifted(g2, -4)
     total = g0 + g1.astype(jnp.float32) + g2.astype(jnp.float32) + got

time: 135 us -> 134 us (level)
  the two profiles are of different devices: /device:TPU:17 before, /device:TPU:25 now
where the time goes in v2:
time: 134 us
  starting transfers between devices  60.8 us (45%)
  waiting for transfers between devices  50.3 us (38%)
  Pallas kernels  18.8 us (14%)
  local copies, waits for them, and re-layouts  1.62 us (1%)
    ppermute x8, waiting for transfers between devices, shifted(): return lax.ppermute(shard, CTX, pairs)  32.9 us
    ppermute x8, starting transfers between devices, shifted(): return lax.ppermute(shard, CTX, pairs)  29.4 us
    all_to_all x4, starting transfers between devices, exchanged(): lax.all_to_all(pieces, ('core', 'x'), split_axis=0, concat_axis=0, tiled=...  21.4 us
    pallas_call x1, Pallas kernels, attention(): pl.pallas_call(attention_kernel, out_shape=(jax.ShapeDtypeStruct((ROWS, Q...  11.4 us
    ppermute x2, waiting for transfers between devices, half_swapped(): return lax.ppermute(shard, 'y_high', [(0, 1), (1, 0)])  10.7 us
    ppermute x2, starting transfers between devices, half_swapped(): return lax.ppermute(shard, 'y_high', [(0, 1), (1, 0)])  9.95 us
    all_to_all x4, waiting for transfers between devices, exchanged(): lax.all_to_all(pieces, ('core', 'x'), split_axis=0, concat_axis=0, tiled=...  6.66 us
    pallas_call x2, Pallas kernels, pack(): pl.pallas_call(pack_kernel, out_shape=jax.ShapeDtypeStruct((HEADS, SUB, 2...  3.72 us
  transfers between devices with their start and end apart: 14, of which 9 were waited for; matrix products, arithmetic and copies ran while one was open for 1% of the time, Pallas kernels for 3%

profile of v2, /device:TPU:25, one launch (start us, length us, event | category | flops | bytes accessed | tf_op | source)
XLA Modules:
  0.0 133.5 jit_solution(5999943497848905642)
XLA Ops:
  0.6 1.7 %pack.3 = bf16[8,48,256]{2,1,0:T(8,128)(2,1)} custom-call(bf16[48,1024]{1,0:T(8,128)(2,1)} %a_ref.3, bf16[48,1024]{1,0:T(8,128)(2,1)} %b_ref.3), custom_call_target="tpu_custom_call" | custom-call | bytes 393216 | tf_op jit(solution)/shard_map/pack/pallas_call | solution.py:58
  2.3 5.0 %all-to-all-start.1 = ((bf16[8,48,256]{2,1,0:T(8,128)(2,1)}), bf16[8,48,256]{2,1,0:T(8,128)(2,1)S(1)}, u32[]{:S(2)}, u32[]{:S(2)}) async-start(bf16[8,48,256]{2,1,0:T(8,128)(2,1)} %pack.3), calls=%async_computation.1 | async-start | bytes 393216 | tf_op jit(solution)/shard_map/all_to_all | solution.py:231
  7.3 0.0 copy-start.2
  7.3 0.7 copy-done.2
  7.9 0.1 copy.11
  8.0 0.1 reduce-window.8
  8.1 0.1 reduce
  8.2 2.1 %pack.2 = bf16[8,48,1024]{2,1,0:T(8,128)(2,1)} custom-call(bf16[48,4096]{1,0:T(8,128)(2,1)} %a_ref.2, bf16[48,4096]{1,0:T(8,128)(2,1)} %b_ref.2), custom_call_target="tpu_custom_call" | custom-call | bytes 1572864 | tf_op jit(solution)/shard_map/pack/pallas_call | solution.py:58
  10.3 2.8 %all-to-all-done.1 = bf16[8,48,256]{2,1,0:T(8,128)(2,1)S(1)} async-done(((bf16[8,48,256]{2,1,0:T(8,128)(2,1)}), bf16[8,48,256]{2,1,0:T(8,128)(2,1)S(1)}, u32[]{:S(2)}, u32[]{:S(2)}) %all-to-all-start.1) | async-done | bytes 196640 | tf_op jit(solution)/shard_map/all_to_all | solution.py:231
  13.1 3.9 %all-to-all-start = ((bf16[8,48,1024]{2,1,0:T(8,128)(2,1)}), bf16[8,48,1024]{2,1,0:T(8,128)(2,1)S(1)}, u32[]{:S(2)}, u32[]{:S(2)}) async-start(bf16[8,48,1024]{2,1,0:T(8,128)(2,1)} %pack.2), calls=%async_computation | async-start | bytes 1572864 | tf_op jit(solution)/shard_map/all_to_all | solution.py:231
  17.0 0.1 select_reduce_fusion
  17.1 0.1 slice.7
  17.2 0.1 slice.6
  17.3 4.8 %collective-permute-start = (bf16[384,256]{1,0:T(8,128)(2,1)S(1)}, bf16[384,256]{1,0:T(8,128)(2,1)S(1)}, u32[]{:S(2)}, u32[]{:S(2)}) collective-permute-start(bf16[384,256]{1,0:T(8,128)(2,1)S(1)} %bitcast.11), channel_id=1, source_target_pairs={{0,1},{1,0},{2,3},{3,2},{4,5},{5,4},{6,7},{7,6},{8,9},{9,8},{10,11... | collective-permute-start | bytes 589832 | tf_op jit(solution)/shard_map/ppermute | solution.py:241
  22.1 0.1 pad_add_fusion.span
  22.2 5.8 %collective-permute-start.3 = (bf16[384,256]{1,0:T(8,128)(2,1)S(1)}, bf16[384,256]{1,0:T(8,128)(2,1)S(1)}, u32[]{:S(2)}, u32[]{:S(2)}) collective-permute-start(bf16[384,256]{1,0:T(8,128)(2,1)S(1)} %bitcast.12), channel_id=1, source_target_pairs={{0,32},{8,40},{16,48},{24,56},{32,64},{40,72},{48,80},{56,88},{64,... | collective-permute-start | bytes 589832 | tf_op jit(solution)/shard_map/ppermute | solution.py:237
  28.0 4.0 %collective-permute-start.1 = (bf16[384,256]{1,0:T(8,128)(2,1)S(1)}, bf16[384,256]{1,0:T(8,128)(2,1)S(1)}, u32[]{:S(2)}, u32[]{:S(2)}) collective-permute-start(bf16[384,256]{1,0:T(8,128)(2,1)S(1)} %bitcast.13), channel_id=1, source_target_pairs={{0,16},{8,24},{16,32},{24,40},{32,48},{40,56},{48,64},{56,72},{64,... | collective-permute-start | bytes 589832 | tf_op jit(solution)/shard_map/ppermute | solution.py:237
  32.0 0.0 collective-permute-done.refs_1_
  32.0 6.1 %collective-permute-start.4 = (bf16[384,256]{1,0:T(8,128)(2,1)S(1)}, bf16[384,256]{1,0:T(8,128)(2,1)S(1)}, u32[]{:S(2)}, u32[]{:S(2)}) collective-permute-start(bf16[384,256]{1,0:T(8,128)(2,1)S(1)} %collective-permute-done.refs_1_), channel_id=1, source_target_pairs={{0,32},{8,40},{16,48},{24,56},{32,64},{40,72},{48,80},{56,88},{64,... | collective-permute-start | bytes 589832 | tf_op jit(solution)/shard_map/ppermute | solution.py:237
  38.1 3.7 %collective-permute-start.2 = (bf16[384,256]{1,0:T(8,128)(2,1)S(1)}, bf16[384,256]{1,0:T(8,128)(2,1)S(1)}, u32[]{:S(2)}, u32[]{:S(2)}) collective-permute-start(bf16[384,256]{1,0:T(8,128)(2,1)S(1)} %collective-permute-done.refs_1_), channel_id=1, source_target_pairs={{0,16},{8,24},{16,32},{24,40},{32,48},{40,56},{48,64},{56,72},{64,... | collective-permute-start | bytes 589832 | tf_op jit(solution)/shard_map/ppermute | solution.py:237
  41.8 6.3 %collective-permute-done.3.refs_4_ = bf16[384,256]{1,0:T(8,128)(2,1)S(1)} collective-permute-done((bf16[384,256]{1,0:T(8,128)(2,1)S(1)}, bf16[384,256]{1,0:T(8,128)(2,1)S(1)}, u32[]{:S(2)}, u32[]{:S(2)}) %collective-permute-start.3) | collective-permute-done | bytes 196640 | tf_op jit(solution)/shard_map/ppermute | solution.py:237
  48.1 8.6 %collective-permute-done.1.refs_2_ = bf16[384,256]{1,0:T(8,128)(2,1)S(1)} collective-permute-done((bf16[384,256]{1,0:T(8,128)(2,1)S(1)}, bf16[384,256]{1,0:T(8,128)(2,1)S(1)}, u32[]{:S(2)}, u32[]{:S(2)}) %collective-permute-start.1) | collective-permute-done | bytes 196640 | tf_op jit(solution)/shard_map/ppermute | solution.py:237
  56.7 0.0 collective-permute-done.4.refs_5_
  56.7 8.7 %collective-permute-done.2.refs_3_ = bf16[384,256]{1,0:T(8,128)(2,1)S(1)} collective-permute-done((bf16[384,256]{1,0:T(8,128)(2,1)S(1)}, bf16[384,256]{1,0:T(8,128)(2,1)S(1)}, u32[]{:S(2)}, u32[]{:S(2)}) %collective-permute-start.2) | collective-permute-done | bytes 196640 | tf_op jit(solution)/shard_map/ppermute | solution.py:237
  65.4 0.0 all-to-all-done
  65.4 11.4 %attention.1 = (bf16[384,1024]{1,0:T(8,128)(2,1)}, f32[384,256]{1,0:T(8,128)S(1)}, f32[384,256]{1,0:T(8,128)S(1)}, bf16[384,256]{1,0:T(8,128)(2,1)S(1)}, bf16[38...) custom-call(s32[1]{0:T(128)} %bitcast.half, s32[6]{0:T(128)S(1)} %pad_add_fusion.span, ...), custom_call_target="tpu_custom_call" | custom-call | flops 2831155200 | bytes 4194304 | tf_op jit(solution)/shard_map/attention/pallas_call | solution.py:189
  76.8 4.0 %collective-permute-start.7 = (bf16[384,256]{1,0:T(8,128)(2,1)S(1)}, bf16[384,256]{1,0:T(8,128)(2,1)S(1)}, u32[]{:S(2)}, u32[]{:S(2)}) collective-permute-start(bf16[384,256]{1,0:T(8,128)(2,1)S(1)} %get-tuple-element.22), channel_id=1, source_target_pairs={{16,0},{24,8},{32,16},{40,24},{48,32},{56,40},{64,48},{72,56},{80,... | collective-permute-start | bytes 589832 | tf_op jit(solution)/shard_map/ppermute | solution.py:237
  80.8 1.9 %collective-permute-start.8 = (bf16[384,256]{1,0:T(8,128)(2,1)S(1)}, bf16[384,256]{1,0:T(8,128)(2,1)S(1)}, u32[]{:S(2)}, u32[]{:S(2)}) collective-permute-start(bf16[384,256]{1,0:T(8,128)(2,1)S(1)} %get-tuple-element.23), channel_id=1, source_target_pairs={{32,0},{40,8},{48,16},{56,24},{64,32},{72,40},{80,48},{88,56},{96,... | collective-permute-start | bytes 589832 | tf_op jit(solution)/shard_map/ppermute | solution.py:237
  82.7 5.1 %all-to-all-start.2 = ((bf16[8,48,1024]{2,1,0:T(8,128)(2,1)}), bf16[8,48,1024]{2,1,0:T(8,128)(2,1)S(1)}, u32[]{:S(2)}, u32[]{:S(2)}) async-start(bf16[8,48,1024]{2,1,0:T(8,128)(2,1)} %bitcast.7), calls=%async_computation.2 | async-start | bytes 1572864 | tf_op jit(solution)/shard_map/all_to_all | solution.py:231
  87.9 1.9 %collective-permute-start.5 = (bf16[384,256]{1,0:T(8,128)(2,1)S(1)}, bf16[384,256]{1,0:T(8,128)(2,1)S(1)}, u32[]{:S(2)}, u32[]{:S(2)}) collective-permute-start(bf16[384,256]{1,0:T(8,128)(2,1)S(1)} %get-tuple-element.19), channel_id=1, source_target_pairs={{16,0},{24,8},{32,16},{40,24},{48,32},{56,40},{64,48},{72,56},{80,... | collective-permute-start | bytes 589832 | tf_op jit(solution)/shard_map/ppermute | solution.py:237
  89.8 1.9 %collective-permute-start.6 = (bf16[384,256]{1,0:T(8,128)(2,1)S(1)}, bf16[384,256]{1,0:T(8,128)(2,1)S(1)}, u32[]{:S(2)}, u32[]{:S(2)}) collective-permute-start(bf16[384,256]{1,0:T(8,128)(2,1)S(1)} %get-tuple-element.20), channel_id=1, source_target_pairs={{32,0},{40,8},{48,16},{56,24},{64,32},{72,40},{80,48},{88,56},{96,... | collective-permute-start | bytes 589832 | tf_op jit(solution)/shard_map/ppermute | solution.py:237
  91.7 0.0 collective-permute-done.7
  91.8 1.7 %collective-permute-done.8 = bf16[384,256]{1,0:T(8,128)(2,1)S(1)} collective-permute-done((bf16[384,256]{1,0:T(8,128)(2,1)S(1)}, bf16[384,256]{1,0:T(8,128)(2,1)S(1)}, u32[]{:S(2)}, u32[]{:S(2)}) %collective-permute-start.8) | collective-permute-done | bytes 196640 | tf_op jit(solution)/shard_map/ppermute | solution.py:237
  93.4 0.1 add_convert_fusion.1
  93.5 5.2 %collective-permute-start.9 = (bf16[384,256]{1,0:T(8,128)(2,1)S(1)}, bf16[384,256]{1,0:T(8,128)(2,1)S(1)}, u32[]{:S(2)}, u32[]{:S(2)}) collective-permute-start(bf16[384,256]{1,0:T(8,128)(2,1)S(1)} %add_convert_fusion.1), channel_id=1, source_target_pairs={{0,1},{1,0},{2,3},{3,2},{4,5},{5,4},{6,7},{7,6},{8,9},{9,8},{10,11... | collective-permute-start | bytes 589832 | tf_op jit(solution)/shard_map/ppermute | solution.py:241
  98.7 0.7 collective-permute-done.5
  99.4 6.9 %collective-permute-done.6 = bf16[384,256]{1,0:T(8,128)(2,1)S(1)} collective-permute-done((bf16[384,256]{1,0:T(8,128)(2,1)S(1)}, bf16[384,256]{1,0:T(8,128)(2,1)S(1)}, u32[]{:S(2)}, u32[]{:S(2)}) %collective-permute-start.6) | collective-permute-done | bytes 196640 | tf_op jit(solution)/shard_map/ppermute | solution.py:237
  106.4 10.7 %collective-permute-done.9 = bf16[384,256]{1,0:T(8,128)(2,1)S(1)} collective-permute-done((bf16[384,256]{1,0:T(8,128)(2,1)S(1)}, bf16[384,256]{1,0:T(8,128)(2,1)S(1)}, u32[]{:S(2)}, u32[]{:S(2)}) %collective-permute-start.9) | collective-permute-done | bytes 196640 | tf_op jit(solution)/shard_map/ppermute | solution.py:241
  117.1 0.8 add_convert_fusion
  117.9 0.0 all-to-all-done.2.got_ref
  117.9 0.0 copy-start
  117.9 7.4 %all-to-all-start.3 = ((bf16[8,48,256]{2,1,0:T(8,128)(2,1)}), bf16[8,48,256]{2,1,0:T(8,128)(2,1)S(1)}, u32[]{:S(2)}, u32[]{:S(2)}) async-start(bf16[8,48,256]{2,1,0:T(8,128)(2,1)} %bitcast.8), calls=%async_computation.3 | async-start | bytes 393216 | tf_op jit(solution)/shard_map/all_to_all | solution.py:231
  125.3 0.0 copy-done
  125.3 2.1 %unpack.2 = (bf16[48,4096]{1,0:T(8,128)(2,1)}, bf16[48,4096]{1,0:T(8,128)(2,1)}) custom-call(bf16[8,48,1024]{2,1,0:T(8,128)(2,1)} %copy-done), custom_call_target="tpu_custom_call" | custom-call | bytes 1572864 | tf_op jit(solution)/shard_map/unpack/pallas_call | solution.py:80
  127.4 3.8 %all-to-all-done.3.got_ref = bf16[8,48,256]{2,1,0:T(8,128)(2,1)S(1)} async-done(((bf16[8,48,256]{2,1,0:T(8,128)(2,1)}), bf16[8,48,256]{2,1,0:T(8,128)(2,1)S(1)}, u32[]{:S(2)}, u32[]{:S(2)}) %all-to-all-start.3) | async-done | bytes 196640 | tf_op jit(solution)/shard_map/all_to_all | solution.py:231
  131.2 0.0 copy-start.1
  131.2 0.7 copy-done.1
  131.9 1.6 %unpack.3 = (bf16[48,1024]{1,0:T(8,128)(2,1)}, bf16[48,1024]{1,0:T(8,128)(2,1)}) custom-call(bf16[8,48,256]{2,1,0:T(8,128)(2,1)} %copy-done.1), custom_call_target="tpu_custom_call" | custom-call | bytes 393216 | tf_op jit(solution)/shard_map/unpack/pallas_call | solution.py:80
  (6 shorter events, 0.1 us)
Async XLA Ops:
  2.3 10.9 %all-to-all-start.1 = ((bf16[8,48,256]{2,1,0:T(8,128)(2,1)}), bf16[8,48,256]{2,1,0:T(8,128)(2,1)S(1)}, u32[]{:S(2)}, u32[]{:S(2)}) async-start(bf16[8,48,256]{2,1,0:T(8,128)(2,1)} %pack.3), calls=%async_computation.1 | async-start | bytes 393216 | tf_op jit(solution)/shard_map/all_to_all | solution.py:231
  7.3 0.7 copy-start.2
  13.1 52.3 %all-to-all-start = ((bf16[8,48,1024]{2,1,0:T(8,128)(2,1)}), bf16[8,48,1024]{2,1,0:T(8,128)(2,1)S(1)}, u32[]{:S(2)}, u32[]{:S(2)}) async-start(bf16[8,48,1024]{2,1,0:T(8,128)(2,1)} %pack.2), calls=%async_computation | async-start | bytes 1572864 | tf_op jit(solution)/shard_map/all_to_all | solution.py:231
  17.3 14.7 %collective-permute-start = (bf16[384,256]{1,0:T(8,128)(2,1)S(1)}, bf16[384,256]{1,0:T(8,128)(2,1)S(1)}, u32[]{:S(2)}, u32[]{:S(2)}) collective-permute-start(bf16[384,256]{1,0:T(8,128)(2,1)S(1)} %bitcast.11), channel_id=1, source_target_pairs={{0,1},{1,0},{2,3},{3,2},{4,5},{5,4},{6,7},{7,6},{8,9},{9,8},{10,11... | collective-permute-start | bytes 589832 | tf_op jit(solution)/shard_map/ppermute | solution.py:241
  22.2 26.0 %collective-permute-start.3 = (bf16[384,256]{1,0:T(8,128)(2,1)S(1)}, bf16[384,256]{1,0:T(8,128)(2,1)S(1)}, u32[]{:S(2)}, u32[]{:S(2)}) collective-permute-start(bf16[384,256]{1,0:T(8,128)(2,1)S(1)} %bitcast.12), channel_id=1, source_target_pairs={{0,32},{8,40},{16,48},{24,56},{32,64},{40,72},{48,80},{56,88},{64,... | collective-permute-start | bytes 589832 | tf_op jit(solution)/shard_map/ppermute | solution.py:237
  28.0 28.7 %collective-permute-start.1 = (bf16[384,256]{1,0:T(8,128)(2,1)S(1)}, bf16[384,256]{1,0:T(8,128)(2,1)S(1)}, u32[]{:S(2)}, u32[]{:S(2)}) collective-permute-start(bf16[384,256]{1,0:T(8,128)(2,1)S(1)} %bitcast.13), channel_id=1, source_target_pairs={{0,16},{8,24},{16,32},{24,40},{32,48},{40,56},{48,64},{56,72},{64,... | collective-permute-start | bytes 589832 | tf_op jit(solution)/shard_map/ppermute | solution.py:237
  32.0 24.7 %collective-permute-start.4 = (bf16[384,256]{1,0:T(8,128)(2,1)S(1)}, bf16[384,256]{1,0:T(8,128)(2,1)S(1)}, u32[]{:S(2)}, u32[]{:S(2)}) collective-permute-start(bf16[384,256]{1,0:T(8,128)(2,1)S(1)} %collective-permute-done.refs_1_), channel_id=1, source_target_pairs={{0,32},{8,40},{16,48},{24,56},{32,64},{40,72},{48,80},{56,88},{64,... | collective-permute-start | bytes 589832 | tf_op jit(solution)/shard_map/ppermute | solution.py:237
  38.1 27.3 %collective-permute-start.2 = (bf16[384,256]{1,0:T(8,128)(2,1)S(1)}, bf16[384,256]{1,0:T(8,128)(2,1)S(1)}, u32[]{:S(2)}, u32[]{:S(2)}) collective-permute-start(bf16[384,256]{1,0:T(8,128)(2,1)S(1)} %collective-permute-done.refs_1_), channel_id=1, source_target_pairs={{0,16},{8,24},{16,32},{24,40},{32,48},{40,56},{48,64},{56,72},{64,... | collective-permute-start | bytes 589832 | tf_op jit(solution)/shard_map/ppermute | solution.py:237
  76.8 15.0 %collective-permute-start.7 = (bf16[384,256]{1,0:T(8,128)(2,1)S(1)}, bf16[384,256]{1,0:T(8,128)(2,1)S(1)}, u32[]{:S(2)}, u32[]{:S(2)}) collective-permute-start(bf16[384,256]{1,0:T(8,128)(2,1)S(1)} %get-tuple-element.22), channel_id=1, source_target_pairs={{16,0},{24,8},{32,16},{40,24},{48,32},{56,40},{64,48},{72,56},{80,... | collective-permute-start | bytes 589832 | tf_op jit(solution)/shard_map/ppermute | solution.py:237
  80.8 12.6 %collective-permute-start.8 = (bf16[384,256]{1,0:T(8,128)(2,1)S(1)}, bf16[384,256]{1,0:T(8,128)(2,1)S(1)}, u32[]{:S(2)}, u32[]{:S(2)}) collective-permute-start(bf16[384,256]{1,0:T(8,128)(2,1)S(1)} %get-tuple-element.23), channel_id=1, source_target_pairs={{32,0},{40,8},{48,16},{56,24},{64,32},{72,40},{80,48},{88,56},{96,... | collective-permute-start | bytes 589832 | tf_op jit(solution)/shard_map/ppermute | solution.py:237
  82.7 35.1 %all-to-all-start.2 = ((bf16[8,48,1024]{2,1,0:T(8,128)(2,1)}), bf16[8,48,1024]{2,1,0:T(8,128)(2,1)S(1)}, u32[]{:S(2)}, u32[]{:S(2)}) async-start(bf16[8,48,1024]{2,1,0:T(8,128)(2,1)} %bitcast.7), calls=%async_computation.2 | async-start | bytes 1572864 | tf_op jit(solution)/shard_map/all_to_all | solution.py:231
  87.9 11.5 %collective-permute-start.5 = (bf16[384,256]{1,0:T(8,128)(2,1)S(1)}, bf16[384,256]{1,0:T(8,128)(2,1)S(1)}, u32[]{:S(2)}, u32[]{:S(2)}) collective-permute-start(bf16[384,256]{1,0:T(8,128)(2,1)S(1)} %get-tuple-element.19), channel_id=1, source_target_pairs={{16,0},{24,8},{32,16},{40,24},{48,32},{56,40},{64,48},{72,56},{80,... | collective-permute-start | bytes 589832 | tf_op jit(solution)/shard_map/ppermute | solution.py:237
  89.8 16.6 %collective-permute-start.6 = (bf16[384,256]{1,0:T(8,128)(2,1)S(1)}, bf16[384,256]{1,0:T(8,128)(2,1)S(1)}, u32[]{:S(2)}, u32[]{:S(2)}) collective-permute-start(bf16[384,256]{1,0:T(8,128)(2,1)S(1)} %get-tuple-element.20), channel_id=1, source_target_pairs={{32,0},{40,8},{48,16},{56,24},{64,32},{72,40},{80,48},{88,56},{96,... | collective-permute-start | bytes 589832 | tf_op jit(solution)/shard_map/ppermute | solution.py:237
  93.5 23.6 %collective-permute-start.9 = (bf16[384,256]{1,0:T(8,128)(2,1)S(1)}, bf16[384,256]{1,0:T(8,128)(2,1)S(1)}, u32[]{:S(2)}, u32[]{:S(2)}) collective-permute-start(bf16[384,256]{1,0:T(8,128)(2,1)S(1)} %add_convert_fusion.1), channel_id=1, source_target_pairs={{0,1},{1,0},{2,3},{3,2},{4,5},{5,4},{6,7},{7,6},{8,9},{9,8},{10,11... | collective-permute-start | bytes 589832 | tf_op jit(solution)/shard_map/ppermute | solution.py:241
  117.9 7.4 %copy-start = (bf16[8,48,1024]{2,1,0:T(8,128)(2,1)}, bf16[8,48,1024]{2,1,0:T(8,128)(2,1)S(1)}, u32[]{:S(2)}) copy-start(bf16[8,48,1024]{2,1,0:T(8,128)(2,1)S(1)} %all-to-all-done.2.got_ref) | copy-start | bytes 2359300
  117.9 13.3 %all-to-all-start.3 = ((bf16[8,48,256]{2,1,0:T(8,128)(2,1)}), bf16[8,48,256]{2,1,0:T(8,128)(2,1)S(1)}, u32[]{:S(2)}, u32[]{:S(2)}) async-start(bf16[8,48,256]{2,1,0:T(8,128)(2,1)} %bitcast.8), calls=%async_computation.3 | async-start | bytes 393216 | tf_op jit(solution)/shard_map/all_to_all | solution.py:231
  131.2 0.7 copy-start.1

commit v3 on v1

--- a/solution.py
+++ b/solution.py
@@ -17,7 +17,8 @@
 BACK = 2
 OWN = BACK * CHIP
 TK = 256
-WINDOW = OWN + CHIP + TK
+STEP = 2 * TK
+WINDOW = OWN + CHIP + STEP
 TQ = 128
 QTILES = ROWS // TQ
 LANES = TQ * GROUP
@@ -102,7 +103,7 @@
             for x in range(XS)
         ]
 
-    kv[OWN + CHIP :, :] = jnp.zeros((TK, 2 * D), kv.dtype)
+    kv[OWN + CHIP :, :] = jnp.zeros((STEP, 2 * D), kv.dtype)
     for j in range(2):
         for held, place in stripes(j):
             for chip in range(BACK + 1):
@@ -118,13 +119,12 @@
         )
         start = start_ref[qi]
         own = own_ref[qi]
-        low = span[qi] // TK
-        high = span[QTILES + qi] // TK + 1
-        steps = (high - low + 1) // 2
+        low = span[qi] // 16 * 16
+        steps = (span[QTILES + qi] - low) // STEP + 1
 
         def tiles(step):
-            first = low + 2 * step
-            return [pl.multiple_of((first + t) * TK, TK) for t in range(2)]
+            first = low + step * STEP
+            return [pl.multiple_of(first + t * TK, 16) for t in range(2)]
 
         def score(step, top):
             for base in tiles(step):
@@ -256,7 +256,8 @@
     theirs = half_swapped(own)
     own1, own2 = shifted(own, 2), shifted(own, 4)
     qdo = exchanged(pack(queries, output_gradient)).reshape(ROWS, QDO)
-    theirs1, theirs2 = shifted(theirs, 2), shifted(theirs, 4)
+    theirs1 = shifted(theirs, 2)
+    theirs2 = shifted(theirs1, 2)
     span, start, own_pos = query_spans(doc_lengths, place, half)
 
     blocks = (own, theirs, own1, theirs1, own2, theirs2)
@@ -264,7 +265,6 @@
     h1, h2 = shifted(h1, -2), shifted(h2, -4)
     odq_rows = exchanged(odq.reshape(HEADS, SUB, QDO))
     theirs = (h0 + h1.astype(jnp.float32) + h2.astype(jnp.float32)).astype(jnp.bfloat16)
-    theirs, g1, g2 = lax.optimization_barrier((theirs, g1, g2))
     got = half_swapped(theirs).astype(jnp.float32)
     g1, g2 = shifted(g1, -2), shifted(g2, -4)
     total = g0 + g1.astype(jnp.float32) + g2.astype(jnp.float32) + got

time: 135 us -> 137 us (1.015)
  the two profiles are of different devices: /device:TPU:17 before, /device:TPU:9 now
where the time goes in v3:
time: 137 us; the launch traced here: 136 us
  starting transfers between devices  70.8 us (52%)
  waiting for transfers between devices  45.5 us (33%)
  Pallas kernels  15.8 us (12%)
  local copies, waits for them, and re-layouts  1.62 us (1%)
    ppermute x8, starting transfers between devices, shifted(): return lax.ppermute(shard, CTX, pairs)  35.6 us
    ppermute x2, waiting for transfers between devices, half_swapped(): return lax.ppermute(shard, 'y_high', [(0, 1), (1, 0)])  22.1 us
    all_to_all x4, starting transfers between devices, exchanged(): lax.all_to_all(pieces, ('core', 'x'), split_axis=0, concat_axis=0, tiled=...  19.6 us
    ppermute x8, waiting for transfers between devices, shifted(): return lax.ppermute(shard, CTX, pairs)  16.8 us
    ppermute x2, starting transfers between devices, half_swapped(): return lax.ppermute(shard, 'y_high', [(0, 1), (1, 0)])  15.6 us
    pallas_call x1, Pallas kernels, attention(): pl.pallas_call(attention_kernel, out_shape=(jax.ShapeDtypeStruct((ROWS, Q...  8.34 us
    all_to_all x4, waiting for transfers between devices, exchanged(): lax.all_to_all(pieces, ('core', 'x'), split_axis=0, concat_axis=0, tiled=...  6.66 us
    pallas_call x2, Pallas kernels, pack(): pl.pallas_call(pack_kernel, out_shape=jax.ShapeDtypeStruct((HEADS, SUB, 2...  3.72 us
  transfers between devices with their start and end apart: 14, of which 8 were waited for; matrix products, arithmetic and copies ran while one was open for 1% of the time, Pallas kernels for 3%

profile of v3, /device:TPU:9, one launch (start us, length us, event | category | flops | bytes accessed | tf_op | source)
XLA Modules:
  0.0 135.8 jit_solution(9144971111420832649)
XLA Ops:
  0.6 1.7 %pack.3 = bf16[8,48,256]{2,1,0:T(8,128)(2,1)} custom-call(bf16[48,1024]{1,0:T(8,128)(2,1)} %a_ref.3, bf16[48,1024]{1,0:T(8,128)(2,1)} %b_ref.3), custom_call_target="tpu_custom_call" | custom-call | bytes 393216 | tf_op jit(solution)/shard_map/pack/pallas_call | solution.py:58
  2.3 5.0 %all-to-all-start.1 = ((bf16[8,48,256]{2,1,0:T(8,128)(2,1)}), bf16[8,48,256]{2,1,0:T(8,128)(2,1)S(1)}, u32[]{:S(2)}, u32[]{:S(2)}) async-start(bf16[8,48,256]{2,1,0:T(8,128)(2,1)} %pack.3), calls=%async_computation.1 | async-start | bytes 393216 | tf_op jit(solution)/shard_map/all_to_all | solution.py:239
  7.3 0.0 copy-start.2
  7.3 0.7 copy-done.2
  7.9 0.1 copy.11
  8.0 0.1 reduce-window.8
  8.1 0.1 reduce
  8.2 2.1 %pack.2 = bf16[8,48,1024]{2,1,0:T(8,128)(2,1)} custom-call(bf16[48,4096]{1,0:T(8,128)(2,1)} %a_ref.2, bf16[48,4096]{1,0:T(8,128)(2,1)} %b_ref.2), custom_call_target="tpu_custom_call" | custom-call | bytes 1572864 | tf_op jit(solution)/shard_map/pack/pallas_call | solution.py:58
  10.3 2.8 %all-to-all-done.1 = bf16[8,48,256]{2,1,0:T(8,128)(2,1)S(1)} async-done(((bf16[8,48,256]{2,1,0:T(8,128)(2,1)}), bf16[8,48,256]{2,1,0:T(8,128)(2,1)S(1)}, u32[]{:S(2)}, u32[]{:S(2)}) %all-to-all-start.1) | async-done | bytes 196640 | tf_op jit(solution)/shard_map/all_to_all | solution.py:239
  13.1 3.9 %all-to-all-start = ((bf16[8,48,1024]{2,1,0:T(8,128)(2,1)}), bf16[8,48,1024]{2,1,0:T(8,128)(2,1)S(1)}, u32[]{:S(2)}, u32[]{:S(2)}) async-start(bf16[8,48,1024]{2,1,0:T(8,128)(2,1)} %pack.2), calls=%async_computation | async-start | bytes 1572864 | tf_op jit(solution)/shard_map/all_to_all | solution.py:239
  17.0 0.1 select_reduce_fusion
  17.1 0.1 slice.7
  17.2 6.6 %collective-permute-start = (bf16[384,256]{1,0:T(8,128)(2,1)S(1)}, bf16[384,256]{1,0:T(8,128)(2,1)S(1)}, u32[]{:S(2)}, u32[]{:S(2)}) collective-permute-start(bf16[384,256]{1,0:T(8,128)(2,1)S(1)} %bitcast.11), channel_id=1, source_target_pairs={{0,1},{1,0},{2,3},{3,2},{4,5},{5,4},{6,7},{7,6},{8,9},{9,8},{10,11... | collective-permute-start | bytes 589832 | tf_op jit(solution)/shard_map/ppermute | solution.py:249
  23.8 0.1 slice.6
  23.9 8.2 %collective-permute-done.refs_1_ = bf16[384,256]{1,0:T(8,128)(2,1)S(1)} collective-permute-done((bf16[384,256]{1,0:T(8,128)(2,1)S(1)}, bf16[384,256]{1,0:T(8,128)(2,1)S(1)}, u32[]{:S(2)}, u32[]{:S(2)}) %collective-permute-start) | collective-permute-done | bytes 196640 | tf_op jit(solution)/shard_map/ppermute | solution.py:249
  32.1 4.0 %collective-permute-start.2 = (bf16[384,256]{1,0:T(8,128)(2,1)S(1)}, bf16[384,256]{1,0:T(8,128)(2,1)S(1)}, u32[]{:S(2)}, u32[]{:S(2)}) collective-permute-start(bf16[384,256]{1,0:T(8,128)(2,1)S(1)} %collective-permute-done.refs_1_), channel_id=1, source_target_pairs={{0,16},{8,24},{16,32},{24,40},{32,48},{40,56},{48,64},{56,72},{64,... | collective-permute-start | bytes 589832 | tf_op jit(solution)/shard_map/ppermute | solution.py:245
  36.1 0.1 pad_add_fusion.span
  36.2 5.8 %collective-permute-start.3 = (bf16[384,256]{1,0:T(8,128)(2,1)S(1)}, bf16[384,256]{1,0:T(8,128)(2,1)S(1)}, u32[]{:S(2)}, u32[]{:S(2)}) collective-permute-start(bf16[384,256]{1,0:T(8,128)(2,1)S(1)} %bitcast.12), channel_id=1, source_target_pairs={{0,32},{8,40},{16,48},{24,56},{32,64},{40,72},{48,80},{56,88},{64,... | collective-permute-start | bytes 589832 | tf_op jit(solution)/shard_map/ppermute | solution.py:245
  42.0 5.2 %collective-permute-start.1 = (bf16[384,256]{1,0:T(8,128)(2,1)S(1)}, bf16[384,256]{1,0:T(8,128)(2,1)S(1)}, u32[]{:S(2)}, u32[]{:S(2)}) collective-permute-start(bf16[384,256]{1,0:T(8,128)(2,1)S(1)} %bitcast.13), channel_id=1, source_target_pairs={{0,16},{8,24},{16,32},{24,40},{32,48},{40,56},{48,64},{56,72},{64,... | collective-permute-start | bytes 589832 | tf_op jit(solution)/shard_map/ppermute | solution.py:245
  47.3 0.0 collective-permute-done.2.refs_3_
  47.3 3.1 %collective-permute-start.4 = (bf16[384,256]{1,0:T(8,128)(2,1)S(1)}, bf16[384,256]{1,0:T(8,128)(2,1)S(1)}, u32[]{:S(2)}, u32[]{:S(2)}) collective-permute-start(bf16[384,256]{1,0:T(8,128)(2,1)S(1)} %collective-permute-done.2.refs_3_), channel_id=1, source_target_pairs={{0,16},{8,24},{16,32},{24,40},{32,48},{40,56},{48,64},{56,72},{64,... | collective-permute-start | bytes 589832 | tf_op jit(solution)/shard_map/ppermute | solution.py:245
  50.4 1.3 collective-permute-done.3.refs_4_
  51.7 7.4 %collective-permute-done.1.refs_2_ = bf16[384,256]{1,0:T(8,128)(2,1)S(1)} collective-permute-done((bf16[384,256]{1,0:T(8,128)(2,1)S(1)}, bf16[384,256]{1,0:T(8,128)(2,1)S(1)}, u32[]{:S(2)}, u32[]{:S(2)}) %collective-permute-start.1) | collective-permute-done | bytes 196640 | tf_op jit(solution)/shard_map/ppermute | solution.py:245
  59.1 0.0 all-to-all-done
  59.1 4.2 %collective-permute-done.4.refs_5_ = bf16[384,256]{1,0:T(8,128)(2,1)S(1)} collective-permute-done((bf16[384,256]{1,0:T(8,128)(2,1)S(1)}, bf16[384,256]{1,0:T(8,128)(2,1)S(1)}, u32[]{:S(2)}, u32[]{:S(2)}) %collective-permute-start.4) | collective-permute-done | bytes 196640 | tf_op jit(solution)/shard_map/ppermute | solution.py:245
  63.3 8.3 %attention.1 = (bf16[384,1024]{1,0:T(8,128)(2,1)}, f32[384,256]{1,0:T(8,128)S(1)}, f32[384,256]{1,0:T(8,128)S(1)}, bf16[384,256]{1,0:T(8,128)(2,1)S(1)}, bf16[38...) custom-call(s32[1]{0:T(128)} %bitcast.half, s32[6]{0:T(128)S(1)} %pad_add_fusion.span, ...), custom_call_target="tpu_custom_call" | custom-call | flops 2831155200 | bytes 4194304 | tf_op jit(solution)/shard_map/attention/pallas_call | solution.py:197
  71.6 1.9 %collective-permute-start.7 = (bf16[384,256]{1,0:T(8,128)(2,1)S(1)}, bf16[384,256]{1,0:T(8,128)(2,1)S(1)}, u32[]{:S(2)}, u32[]{:S(2)}) collective-permute-start(bf16[384,256]{1,0:T(8,128)(2,1)S(1)} %get-tuple-element.22), channel_id=1, source_target_pairs={{16,0},{24,8},{32,16},{40,24},{48,32},{56,40},{64,48},{72,56},{80,... | collective-permute-start | bytes 589832 | tf_op jit(solution)/shard_map/ppermute | solution.py:245
  73.6 11.7 %collective-permute-start.8 = (bf16[384,256]{1,0:T(8,128)(2,1)S(1)}, bf16[384,256]{1,0:T(8,128)(2,1)S(1)}, u32[]{:S(2)}, u32[]{:S(2)}) collective-permute-start(bf16[384,256]{1,0:T(8,128)(2,1)S(1)} %get-tuple-element.23), channel_id=1, source_target_pairs={{32,0},{40,8},{48,16},{56,24},{64,32},{72,40},{80,48},{88,56},{96,... | collective-permute-start | bytes 589832 | tf_op jit(solution)/shard_map/ppermute | solution.py:245
  85.3 6.5 %all-to-all-start.2 = ((bf16[8,48,1024]{2,1,0:T(8,128)(2,1)}), bf16[8,48,1024]{2,1,0:T(8,128)(2,1)S(1)}, u32[]{:S(2)}, u32[]{:S(2)}) async-start(bf16[8,48,1024]{2,1,0:T(8,128)(2,1)} %bitcast.7), calls=%async_computation.2 | async-start | bytes 1572864 | tf_op jit(solution)/shard_map/all_to_all | solution.py:239
  91.8 1.9 %collective-permute-start.5 = (bf16[384,256]{1,0:T(8,128)(2,1)S(1)}, bf16[384,256]{1,0:T(8,128)(2,1)S(1)}, u32[]{:S(2)}, u32[]{:S(2)}) collective-permute-start(bf16[384,256]{1,0:T(8,128)(2,1)S(1)} %get-tuple-element.19), channel_id=1, source_target_pairs={{16,0},{24,8},{32,16},{40,24},{48,32},{56,40},{64,48},{72,56},{80,... | collective-permute-start | bytes 589832 | tf_op jit(solution)/shard_map/ppermute | solution.py:245
  93.7 1.9 %collective-permute-start.6 = (bf16[384,256]{1,0:T(8,128)(2,1)S(1)}, bf16[384,256]{1,0:T(8,128)(2,1)S(1)}, u32[]{:S(2)}, u32[]{:S(2)}) collective-permute-start(bf16[384,256]{1,0:T(8,128)(2,1)S(1)} %get-tuple-element.20), channel_id=1, source_target_pairs={{32,0},{40,8},{48,16},{56,24},{64,32},{72,40},{80,48},{88,56},{96,... | collective-permute-start | bytes 589832 | tf_op jit(solution)/shard_map/ppermute | solution.py:245
  95.7 0.0 collective-permute-done.7
  95.7 0.0 collective-permute-done.8
  95.7 0.1 add_convert_fusion.1
  95.8 9.1 %collective-permute-start.9 = (bf16[384,256]{1,0:T(8,128)(2,1)S(1)}, bf16[384,256]{1,0:T(8,128)(2,1)S(1)}, u32[]{:S(2)}, u32[]{:S(2)}) collective-permute-start(bf16[384,256]{1,0:T(8,128)(2,1)S(1)} %add_convert_fusion.1), channel_id=1, source_target_pairs={{0,1},{1,0},{2,3},{3,2},{4,5},{5,4},{6,7},{7,6},{8,9},{9,8},{10,11... | collective-permute-start | bytes 589832 | tf_op jit(solution)/shard_map/ppermute | solution.py:249
  104.8 3.8 %collective-permute-done.5 = bf16[384,256]{1,0:T(8,128)(2,1)S(1)} collective-permute-done((bf16[384,256]{1,0:T(8,128)(2,1)S(1)}, bf16[384,256]{1,0:T(8,128)(2,1)S(1)}, u32[]{:S(2)}, u32[]{:S(2)}) %collective-permute-start.5) | collective-permute-done | bytes 196640 | tf_op jit(solution)/shard_map/ppermute | solution.py:245
  108.7 0.0 collective-permute-done.6
  108.7 13.8 %collective-permute-done.9 = bf16[384,256]{1,0:T(8,128)(2,1)S(1)} collective-permute-done((bf16[384,256]{1,0:T(8,128)(2,1)S(1)}, bf16[384,256]{1,0:T(8,128)(2,1)S(1)}, u32[]{:S(2)}, u32[]{:S(2)}) %collective-permute-start.9) | collective-permute-done | bytes 196640 | tf_op jit(solution)/shard_map/ppermute | solution.py:249
  122.5 0.8 add_convert_fusion
  123.3 0.0 all-to-all-done.2.got_ref
  123.3 0.0 copy-start
  123.3 4.3 %all-to-all-start.3 = ((bf16[8,48,256]{2,1,0:T(8,128)(2,1)}), bf16[8,48,256]{2,1,0:T(8,128)(2,1)S(1)}, u32[]{:S(2)}, u32[]{:S(2)}) async-start(bf16[8,48,256]{2,1,0:T(8,128)(2,1)} %bitcast.8), calls=%async_computation.3 | async-start | bytes 393216 | tf_op jit(solution)/shard_map/all_to_all | solution.py:239
  127.6 0.0 copy-done
  127.6 2.1 %unpack.2 = (bf16[48,4096]{1,0:T(8,128)(2,1)}, bf16[48,4096]{1,0:T(8,128)(2,1)}) custom-call(bf16[8,48,1024]{2,1,0:T(8,128)(2,1)} %copy-done), custom_call_target="tpu_custom_call" | custom-call | bytes 1572864 | tf_op jit(solution)/shard_map/unpack/pallas_call | solution.py:80
  129.6 3.8 %all-to-all-done.3.got_ref = bf16[8,48,256]{2,1,0:T(8,128)(2,1)S(1)} async-done(((bf16[8,48,256]{2,1,0:T(8,128)(2,1)}), bf16[8,48,256]{2,1,0:T(8,128)(2,1)S(1)}, u32[]{:S(2)}, u32[]{:S(2)}) %all-to-all-start.3) | async-done | bytes 196640 | tf_op jit(solution)/shard_map/all_to_all | solution.py:239
  133.5 0.0 copy-start.1
  133.5 0.7 copy-done.1
  134.1 1.6 %unpack.3 = (bf16[48,1024]{1,0:T(8,128)(2,1)}, bf16[48,1024]{1,0:T(8,128)(2,1)}) custom-call(bf16[8,48,256]{2,1,0:T(8,128)(2,1)} %copy-done.1), custom_call_target="tpu_custom_call" | custom-call | bytes 393216 | tf_op jit(solution)/shard_map/unpack/pallas_call | solution.py:80
  (6 shorter events, 0.1 us)
Async XLA Ops:
  2.3 10.9 %all-to-all-start.1 = ((bf16[8,48,256]{2,1,0:T(8,128)(2,1)}), bf16[8,48,256]{2,1,0:T(8,128)(2,1)S(1)}, u32[]{:S(2)}, u32[]{:S(2)}) async-start(bf16[8,48,256]{2,1,0:T(8,128)(2,1)} %pack.3), calls=%async_computation.1 | async-start | bytes 393216 | tf_op jit(solution)/shard_map/all_to_all | solution.py:239
  7.3 0.7 copy-start.2
  13.1 45.9 %all-to-all-start = ((bf16[8,48,1024]{2,1,0:T(8,128)(2,1)}), bf16[8,48,1024]{2,1,0:T(8,128)(2,1)S(1)}, u32[]{:S(2)}, u32[]{:S(2)}) async-start(bf16[8,48,1024]{2,1,0:T(8,128)(2,1)} %pack.2), calls=%async_computation | async-start | bytes 1572864 | tf_op jit(solution)/shard_map/all_to_all | solution.py:239
  17.2 14.9 %collective-permute-start = (bf16[384,256]{1,0:T(8,128)(2,1)S(1)}, bf16[384,256]{1,0:T(8,128)(2,1)S(1)}, u32[]{:S(2)}, u32[]{:S(2)}) collective-permute-start(bf16[384,256]{1,0:T(8,128)(2,1)S(1)} %bitcast.11), channel_id=1, source_target_pairs={{0,1},{1,0},{2,3},{3,2},{4,5},{5,4},{6,7},{7,6},{8,9},{9,8},{10,11... | collective-permute-start | bytes 589832 | tf_op jit(solution)/shard_map/ppermute | solution.py:249
  32.1 15.1 %collective-permute-start.2 = (bf16[384,256]{1,0:T(8,128)(2,1)S(1)}, bf16[384,256]{1,0:T(8,128)(2,1)S(1)}, u32[]{:S(2)}, u32[]{:S(2)}) collective-permute-start(bf16[384,256]{1,0:T(8,128)(2,1)S(1)} %collective-permute-done.refs_1_), channel_id=1, source_target_pairs={{0,16},{8,24},{16,32},{24,40},{32,48},{40,56},{48,64},{56,72},{64,... | collective-permute-start | bytes 589832 | tf_op jit(solution)/shard_map/ppermute | solution.py:245
  36.2 15.5 %collective-permute-start.3 = (bf16[384,256]{1,0:T(8,128)(2,1)S(1)}, bf16[384,256]{1,0:T(8,128)(2,1)S(1)}, u32[]{:S(2)}, u32[]{:S(2)}) collective-permute-start(bf16[384,256]{1,0:T(8,128)(2,1)S(1)} %bitcast.12), channel_id=1, source_target_pairs={{0,32},{8,40},{16,48},{24,56},{32,64},{40,72},{48,80},{56,88},{64,... | collective-permute-start | bytes 589832 | tf_op jit(solution)/shard_map/ppermute | solution.py:245
  42.0 17.1 %collective-permute-start.1 = (bf16[384,256]{1,0:T(8,128)(2,1)S(1)}, bf16[384,256]{1,0:T(8,128)(2,1)S(1)}, u32[]{:S(2)}, u32[]{:S(2)}) collective-permute-start(bf16[384,256]{1,0:T(8,128)(2,1)S(1)} %bitcast.13), channel_id=1, source_target_pairs={{0,16},{8,24},{16,32},{24,40},{32,48},{40,56},{48,64},{56,72},{64,... | collective-permute-start | bytes 589832 | tf_op jit(solution)/shard_map/ppermute | solution.py:245
  47.3 16.0 %collective-permute-start.4 = (bf16[384,256]{1,0:T(8,128)(2,1)S(1)}, bf16[384,256]{1,0:T(8,128)(2,1)S(1)}, u32[]{:S(2)}, u32[]{:S(2)}) collective-permute-start(bf16[384,256]{1,0:T(8,128)(2,1)S(1)} %collective-permute-done.2.refs_3_), channel_id=1, source_target_pairs={{0,16},{8,24},{16,32},{24,40},{32,48},{40,56},{48,64},{56,72},{64,... | collective-permute-start | bytes 589832 | tf_op jit(solution)/shard_map/ppermute | solution.py:245
  71.6 24.0 %collective-permute-start.7 = (bf16[384,256]{1,0:T(8,128)(2,1)S(1)}, bf16[384,256]{1,0:T(8,128)(2,1)S(1)}, u32[]{:S(2)}, u32[]{:S(2)}) collective-permute-start(bf16[384,256]{1,0:T(8,128)(2,1)S(1)} %get-tuple-element.22), channel_id=1, source_target_pairs={{16,0},{24,8},{32,16},{40,24},{48,32},{56,40},{64,48},{72,56},{80,... | collective-permute-start | bytes 589832 | tf_op jit(solution)/shard_map/ppermute | solution.py:245
  73.6 22.1 %collective-permute-start.8 = (bf16[384,256]{1,0:T(8,128)(2,1)S(1)}, bf16[384,256]{1,0:T(8,128)(2,1)S(1)}, u32[]{:S(2)}, u32[]{:S(2)}) collective-permute-start(bf16[384,256]{1,0:T(8,128)(2,1)S(1)} %get-tuple-element.23), channel_id=1, source_target_pairs={{32,0},{40,8},{48,16},{56,24},{64,32},{72,40},{80,48},{88,56},{96,... | collective-permute-start | bytes 589832 | tf_op jit(solution)/shard_map/ppermute | solution.py:245
  85.3 38.0 %all-to-all-start.2 = ((bf16[8,48,1024]{2,1,0:T(8,128)(2,1)}), bf16[8,48,1024]{2,1,0:T(8,128)(2,1)S(1)}, u32[]{:S(2)}, u32[]{:S(2)}) async-start(bf16[8,48,1024]{2,1,0:T(8,128)(2,1)} %bitcast.7), calls=%async_computation.2 | async-start | bytes 1572864 | tf_op jit(solution)/shard_map/all_to_all | solution.py:239
  91.8 16.8 %collective-permute-start.5 = (bf16[384,256]{1,0:T(8,128)(2,1)S(1)}, bf16[384,256]{1,0:T(8,128)(2,1)S(1)}, u32[]{:S(2)}, u32[]{:S(2)}) collective-permute-start(bf16[384,256]{1,0:T(8,128)(2,1)S(1)} %get-tuple-element.19), channel_id=1, source_target_pairs={{16,0},{24,8},{32,16},{40,24},{48,32},{56,40},{64,48},{72,56},{80,... | collective-permute-start | bytes 589832 | tf_op jit(solution)/shard_map/ppermute | solution.py:245
  93.7 14.9 %collective-permute-start.6 = (bf16[384,256]{1,0:T(8,128)(2,1)S(1)}, bf16[384,256]{1,0:T(8,128)(2,1)S(1)}, u32[]{:S(2)}, u32[]{:S(2)}) collective-permute-start(bf16[384,256]{1,0:T(8,128)(2,1)S(1)} %get-tuple-element.20), channel_id=1, source_target_pairs={{32,0},{40,8},{48,16},{56,24},{64,32},{72,40},{80,48},{88,56},{96,... | collective-permute-start | bytes 589832 | tf_op jit(solution)/shard_map/ppermute | solution.py:245
  95.8 26.7 %collective-permute-start.9 = (bf16[384,256]{1,0:T(8,128)(2,1)S(1)}, bf16[384,256]{1,0:T(8,128)(2,1)S(1)}, u32[]{:S(2)}, u32[]{:S(2)}) collective-permute-start(bf16[384,256]{1,0:T(8,128)(2,1)S(1)} %add_convert_fusion.1), channel_id=1, source_target_pairs={{0,1},{1,0},{2,3},{3,2},{4,5},{5,4},{6,7},{7,6},{8,9},{9,8},{10,11... | collective-permute-start | bytes 589832 | tf_op jit(solution)/shard_map/ppermute | solution.py:249
  123.3 4.3 %copy-start = (bf16[8,48,1024]{2,1,0:T(8,128)(2,1)}, bf16[8,48,1024]{2,1,0:T(8,128)(2,1)S(1)}, u32[]{:S(2)}) copy-start(bf16[8,48,1024]{2,1,0:T(8,128)(2,1)S(1)} %all-to-all-done.2.got_ref) | copy-start | bytes 2359300
  123.3 10.2 %all-to-all-start.3 = ((bf16[8,48,256]{2,1,0:T(8,128)(2,1)}), bf16[8,48,256]{2,1,0:T(8,128)(2,1)S(1)}, u32[]{:S(2)}, u32[]{:S(2)}) async-start(bf16[8,48,256]{2,1,0:T(8,128)(2,1)} %bitcast.8), calls=%async_computation.3 | async-start | bytes 393216 | tf_op jit(solution)/shard_map/all_to_all | solution.py:239
  133.5 0.7 copy-start.1

commit v4 on v3

--- a/solution.py
+++ b/solution.py
@@ -254,7 +254,8 @@
     half = lax.axis_index("y_high").astype(jnp.int32)
     own = exchanged(pack(keys, values)).reshape(ROWS, 2 * D)
     theirs = half_swapped(own)
-    own1, own2 = shifted(own, 2), shifted(own, 4)
+    theirs, own1 = lax.optimization_barrier((theirs, shifted(own, 2)))
+    own2 = shifted(own1, 2)
     qdo = exchanged(pack(queries, output_gradient)).reshape(ROWS, QDO)
     theirs1 = shifted(theirs, 2)
     theirs2 = shifted(theirs1, 2)

time: 137 us -> 131 us (0.956); the launches traced: 136 us -> 132 us
  starting transfers between devices: 70.8 us -> 66.2 us
    ppermute x8, waiting for transfers between devices: 16.8 us -> 25.6 us  [shifted(): return lax.ppermute(shard, CTX, pairs)]
    ppermute x2, waiting for transfers between devices: 22.1 us -> 14.4 us  [half_swapped(): return lax.ppermute(shard, 'y_high', [(0, 1), (1, 0)])]
    ppermute x8, starting transfers between devices: 35.6 us -> 29.3 us  [shifted(): return lax.ppermute(shard, CTX, pairs)]
    all_to_all x4, starting transfers between devices: 19.6 us -> 22 us  [exchanged(): lax.all_to_all(pieces, ('core', 'x'), split_axis=0, concat_axis=0, tiled=...]
  transfers between devices with their start and end apart: 14 -> 14, of which waited for: 8 -> 9; matrix products, arithmetic and copies ran while one was open for 1% -> 1% of each run, Pallas kernels for 3% -> 3%
where the time goes in v4:
time: 131 us; the launch traced here: 132 us
  starting transfers between devices  66.2 us (51%)
  waiting for transfers between devices  46.6 us (36%)
  Pallas kernels  15.8 us (12%)
  local copies, waits for them, and re-layouts  1.62 us (1%)
    ppermute x8, starting transfers between devices, shifted(): return lax.ppermute(shard, CTX, pairs)  29.3 us
    ppermute x8, waiting for transfers between devices, shifted(): return lax.ppermute(shard, CTX, pairs)  25.6 us
    all_to_all x4, starting transfers between devices, exchanged(): lax.all_to_all(pieces, ('core', 'x'), split_axis=0, concat_axis=0, tiled=...  22 us
    ppermute x2, starting transfers between devices, half_swapped(): return lax.ppermute(shard, 'y_high', [(0, 1), (1, 0)])  14.9 us
    ppermute x2, waiting for transfers between devices, half_swapped(): return lax.ppermute(shard, 'y_high', [(0, 1), (1, 0)])  14.4 us
    pallas_call x1, Pallas kernels, attention(): pl.pallas_call(attention_kernel, out_shape=(jax.ShapeDtypeStruct((ROWS, Q...  8.37 us
    all_to_all x4, waiting for transfers between devices, exchanged(): lax.all_to_all(pieces, ('core', 'x'), split_axis=0, concat_axis=0, tiled=...  6.66 us
    pallas_call x2, Pallas kernels, pack(): pl.pallas_call(pack_kernel, out_shape=jax.ShapeDtypeStruct((HEADS, SUB, 2...  3.72 us
  transfers between devices with their start and end apart: 14, of which 9 were waited for; matrix products, arithmetic and copies ran while one was open for 1% of the time, Pallas kernels for 3%

profile of v4, /device:TPU:9, one launch (start us, length us, event | category | flops | bytes accessed | tf_op | source)
XLA Modules:
  0.0 132.3 jit_solution(10937825105873754677)
XLA Ops:
  0.6 1.7 %pack.3 = bf16[8,48,256]{2,1,0:T(8,128)(2,1)} custom-call(bf16[48,1024]{1,0:T(8,128)(2,1)} %a_ref.3, bf16[48,1024]{1,0:T(8,128)(2,1)} %b_ref.3), custom_call_target="tpu_custom_call" | custom-call | bytes 393216 | tf_op jit(solution)/shard_map/pack/pallas_call | solution.py:58
  2.3 5.0 %all-to-all-start.1 = ((bf16[8,48,256]{2,1,0:T(8,128)(2,1)}), bf16[8,48,256]{2,1,0:T(8,128)(2,1)S(1)}, u32[]{:S(2)}, u32[]{:S(2)}) async-start(bf16[8,48,256]{2,1,0:T(8,128)(2,1)} %pack.3), calls=%async_computation.1 | async-start | bytes 393216 | tf_op jit(solution)/shard_map/all_to_all | solution.py:239
  7.3 0.0 copy-start.2
  7.3 0.7 copy-done.2
  7.9 0.1 copy.11
  8.0 0.1 reduce-window.8
  8.1 0.1 reduce
  8.2 2.1 %pack.2 = bf16[8,48,1024]{2,1,0:T(8,128)(2,1)} custom-call(bf16[48,4096]{1,0:T(8,128)(2,1)} %a_ref.2, bf16[48,4096]{1,0:T(8,128)(2,1)} %b_ref.2), custom_call_target="tpu_custom_call" | custom-call | bytes 1572864 | tf_op jit(solution)/shard_map/pack/pallas_call | solution.py:58
  10.3 2.8 %all-to-all-done.1 = bf16[8,48,256]{2,1,0:T(8,128)(2,1)S(1)} async-done(((bf16[8,48,256]{2,1,0:T(8,128)(2,1)}), bf16[8,48,256]{2,1,0:T(8,128)(2,1)S(1)}, u32[]{:S(2)}, u32[]{:S(2)}) %all-to-all-start.1) | async-done | bytes 196640 | tf_op jit(solution)/shard_map/all_to_all | solution.py:239
  13.1 3.9 %all-to-all-start = ((bf16[8,48,1024]{2,1,0:T(8,128)(2,1)}), bf16[8,48,1024]{2,1,0:T(8,128)(2,1)S(1)}, u32[]{:S(2)}, u32[]{:S(2)}) async-start(bf16[8,48,1024]{2,1,0:T(8,128)(2,1)} %pack.2), calls=%async_computation | async-start | bytes 1572864 | tf_op jit(solution)/shard_map/all_to_all | solution.py:239
  17.0 0.1 select_reduce_fusion
  17.1 0.1 slice.7
  17.2 4.0 %collective-permute-start.1 = (bf16[384,256]{1,0:T(8,128)(2,1)S(1)}, bf16[384,256]{1,0:T(8,128)(2,1)S(1)}, u32[]{:S(2)}, u32[]{:S(2)}) collective-permute-start(bf16[384,256]{1,0:T(8,128)(2,1)S(1)} %bitcast.11), channel_id=1, source_target_pairs={{0,16},{8,24},{16,32},{24,40},{32,48},{40,56},{48,64},{56,72},{64,... | collective-permute-start | bytes 589832 | tf_op jit(solution)/shard_map/ppermute | solution.py:245
  21.2 6.6 %collective-permute-start = (bf16[384,256]{1,0:T(8,128)(2,1)S(1)}, bf16[384,256]{1,0:T(8,128)(2,1)S(1)}, u32[]{:S(2)}, u32[]{:S(2)}) collective-permute-start(bf16[384,256]{1,0:T(8,128)(2,1)S(1)} %bitcast.12), channel_id=1, source_target_pairs={{0,1},{1,0},{2,3},{3,2},{4,5},{5,4},{6,7},{7,6},{8,9},{9,8},{10,11... | collective-permute-start | bytes 589832 | tf_op jit(solution)/shard_map/ppermute | solution.py:249
  27.8 0.1 slice.6
  27.9 5.0 %collective-permute-done.1.refs_2_ = bf16[384,256]{1,0:T(8,128)(2,1)S(1)} collective-permute-done((bf16[384,256]{1,0:T(8,128)(2,1)S(1)}, bf16[384,256]{1,0:T(8,128)(2,1)S(1)}, u32[]{:S(2)}, u32[]{:S(2)}) %collective-permute-start.1) | collective-permute-done | bytes 196640 | tf_op jit(solution)/shard_map/ppermute | solution.py:245
  32.9 2.9 %collective-permute-done.refs_1_ = bf16[384,256]{1,0:T(8,128)(2,1)S(1)} collective-permute-done((bf16[384,256]{1,0:T(8,128)(2,1)S(1)}, bf16[384,256]{1,0:T(8,128)(2,1)S(1)}, u32[]{:S(2)}, u32[]{:S(2)}) %collective-permute-start) | collective-permute-done | bytes 196640 | tf_op jit(solution)/shard_map/ppermute | solution.py:249
  35.8 4.0 %collective-permute-start.2 = (bf16[384,256]{1,0:T(8,128)(2,1)S(1)}, bf16[384,256]{1,0:T(8,128)(2,1)S(1)}, u32[]{:S(2)}, u32[]{:S(2)}) collective-permute-start(bf16[384,256]{1,0:T(8,128)(2,1)S(1)} %collective-permute-done.refs_1_), channel_id=1, source_target_pairs={{0,16},{8,24},{16,32},{24,40},{32,48},{40,56},{48,64},{56,72},{64,... | collective-permute-start | bytes 589832 | tf_op jit(solution)/shard_map/ppermute | solution.py:245
  39.8 0.1 pad_add_fusion.span
  39.9 4.0 %collective-permute-start.3 = (bf16[384,256]{1,0:T(8,128)(2,1)S(1)}, bf16[384,256]{1,0:T(8,128)(2,1)S(1)}, u32[]{:S(2)}, u32[]{:S(2)}) collective-permute-start(bf16[384,256]{1,0:T(8,128)(2,1)S(1)} %collective-permute-done.1.refs_2_), channel_id=1, source_target_pairs={{0,16},{8,24},{16,32},{24,40},{32,48},{40,56},{48,64},{56,72},{64,... | collective-permute-start | bytes 589832 | tf_op jit(solution)/shard_map/ppermute | solution.py:245
  43.9 9.5 %collective-permute-done.2.refs_3_ = bf16[384,256]{1,0:T(8,128)(2,1)S(1)} collective-permute-done((bf16[384,256]{1,0:T(8,128)(2,1)S(1)}, bf16[384,256]{1,0:T(8,128)(2,1)S(1)}, u32[]{:S(2)}, u32[]{:S(2)}) %collective-permute-start.2) | collective-permute-done | bytes 196640 | tf_op jit(solution)/shard_map/ppermute | solution.py:245
  53.4 1.9 %collective-permute-start.4 = (bf16[384,256]{1,0:T(8,128)(2,1)S(1)}, bf16[384,256]{1,0:T(8,128)(2,1)S(1)}, u32[]{:S(2)}, u32[]{:S(2)}) collective-permute-start(bf16[384,256]{1,0:T(8,128)(2,1)S(1)} %collective-permute-done.2.refs_3_), channel_id=1, source_target_pairs={{0,16},{8,24},{16,32},{24,40},{32,48},{40,56},{48,64},{56,72},{64,... | collective-permute-start | bytes 589832 | tf_op jit(solution)/shard_map/ppermute | solution.py:245
  55.3 2.3 %collective-permute-done.3.refs_4_ = bf16[384,256]{1,0:T(8,128)(2,1)S(1)} collective-permute-done((bf16[384,256]{1,0:T(8,128)(2,1)S(1)}, bf16[384,256]{1,0:T(8,128)(2,1)S(1)}, u32[]{:S(2)}, u32[]{:S(2)}) %collective-permute-start.3) | collective-permute-done | bytes 196640 | tf_op jit(solution)/shard_map/ppermute | solution.py:245
  57.6 0.0 all-to-all-done
  57.6 4.3 %collective-permute-done.4.refs_5_ = bf16[384,256]{1,0:T(8,128)(2,1)S(1)} collective-permute-done((bf16[384,256]{1,0:T(8,128)(2,1)S(1)}, bf16[384,256]{1,0:T(8,128)(2,1)S(1)}, u32[]{:S(2)}, u32[]{:S(2)}) %collective-permute-start.4) | collective-permute-done | bytes 196640 | tf_op jit(solution)/shard_map/ppermute | solution.py:245
  61.9 8.4 %attention.1 = (bf16[384,1024]{1,0:T(8,128)(2,1)}, f32[384,256]{1,0:T(8,128)S(1)}, f32[384,256]{1,0:T(8,128)S(1)}, bf16[384,256]{1,0:T(8,128)(2,1)S(1)}, bf16[38...) custom-call(s32[1]{0:T(128)} %bitcast.half, s32[6]{0:T(128)S(1)} %pad_add_fusion.span, ...), custom_call_target="tpu_custom_call" | custom-call | flops 2831155200 | bytes 4194304 | tf_op jit(solution)/shard_map/attention/pallas_call | solution.py:197
  70.3 1.9 %collective-permute-start.7 = (bf16[384,256]{1,0:T(8,128)(2,1)S(1)}, bf16[384,256]{1,0:T(8,128)(2,1)S(1)}, u32[]{:S(2)}, u32[]{:S(2)}) collective-permute-start(bf16[384,256]{1,0:T(8,128)(2,1)S(1)} %get-tuple-element.26), channel_id=1, source_target_pairs={{16,0},{24,8},{32,16},{40,24},{48,32},{56,40},{64,48},{72,56},{80,... | collective-permute-start | bytes 589832 | tf_op jit(solution)/shard_map/ppermute | solution.py:245
  72.2 1.9 %collective-permute-start.8 = (bf16[384,256]{1,0:T(8,128)(2,1)S(1)}, bf16[384,256]{1,0:T(8,128)(2,1)S(1)}, u32[]{:S(2)}, u32[]{:S(2)}) collective-permute-start(bf16[384,256]{1,0:T(8,128)(2,1)S(1)} %get-tuple-element.27), channel_id=1, source_target_pairs={{32,0},{40,8},{48,16},{56,24},{64,32},{72,40},{80,48},{88,56},{96,... | collective-permute-start | bytes 589832 | tf_op jit(solution)/shard_map/ppermute | solution.py:245
  74.1 7.7 %all-to-all-start.2 = ((bf16[8,48,1024]{2,1,0:T(8,128)(2,1)}), bf16[8,48,1024]{2,1,0:T(8,128)(2,1)S(1)}, u32[]{:S(2)}, u32[]{:S(2)}) async-start(bf16[8,48,1024]{2,1,0:T(8,128)(2,1)} %bitcast.7), calls=%async_computation.2 | async-start | bytes 1572864 | tf_op jit(solution)/shard_map/all_to_all | solution.py:239
  81.8 9.7 %collective-permute-start.5 = (bf16[384,256]{1,0:T(8,128)(2,1)S(1)}, bf16[384,256]{1,0:T(8,128)(2,1)S(1)}, u32[]{:S(2)}, u32[]{:S(2)}) collective-permute-start(bf16[384,256]{1,0:T(8,128)(2,1)S(1)} %get-tuple-element.23), channel_id=1, source_target_pairs={{16,0},{24,8},{32,16},{40,24},{48,32},{56,40},{64,48},{72,56},{80,... | collective-permute-start | bytes 589832 | tf_op jit(solution)/shard_map/ppermute | solution.py:245
  91.5 1.9 %collective-permute-start.6 = (bf16[384,256]{1,0:T(8,128)(2,1)S(1)}, bf16[384,256]{1,0:T(8,128)(2,1)S(1)}, u32[]{:S(2)}, u32[]{:S(2)}) collective-permute-start(bf16[384,256]{1,0:T(8,128)(2,1)S(1)} %get-tuple-element.24), channel_id=1, source_target_pairs={{32,0},{40,8},{48,16},{56,24},{64,32},{72,40},{80,48},{88,56},{96,... | collective-permute-start | bytes 589832 | tf_op jit(solution)/shard_map/ppermute | solution.py:245
  93.4 0.0 collective-permute-done.7
  93.5 0.0 collective-permute-done.8
  93.5 0.1 add_convert_fusion.1
  93.5 8.3 %collective-permute-start.9 = (bf16[384,256]{1,0:T(8,128)(2,1)S(1)}, bf16[384,256]{1,0:T(8,128)(2,1)S(1)}, u32[]{:S(2)}, u32[]{:S(2)}) collective-permute-start(bf16[384,256]{1,0:T(8,128)(2,1)S(1)} %add_convert_fusion.1), channel_id=1, source_target_pairs={{0,1},{1,0},{2,3},{3,2},{4,5},{5,4},{6,7},{7,6},{8,9},{9,8},{10,11... | collective-permute-start | bytes 589832 | tf_op jit(solution)/shard_map/ppermute | solution.py:249
  101.9 0.0 collective-permute-done.5
  101.9 4.5 %collective-permute-done.6 = bf16[384,256]{1,0:T(8,128)(2,1)S(1)} collective-permute-done((bf16[384,256]{1,0:T(8,128)(2,1)S(1)}, bf16[384,256]{1,0:T(8,128)(2,1)S(1)}, u32[]{:S(2)}, u32[]{:S(2)}) %collective-permute-start.6) | collective-permute-done | bytes 196640 | tf_op jit(solution)/shard_map/ppermute | solution.py:245
  106.3 11.5 %collective-permute-done.9 = bf16[384,256]{1,0:T(8,128)(2,1)S(1)} collective-permute-done((bf16[384,256]{1,0:T(8,128)(2,1)S(1)}, bf16[384,256]{1,0:T(8,128)(2,1)S(1)}, u32[]{:S(2)}, u32[]{:S(2)}) %collective-permute-start.9) | collective-permute-done | bytes 196640 | tf_op jit(solution)/shard_map/ppermute | solution.py:249
  117.9 0.8 add_convert_fusion
  118.6 0.0 all-to-all-done.2.got_ref
  118.7 0.0 copy-start
  118.7 5.4 %all-to-all-start.3 = ((bf16[8,48,256]{2,1,0:T(8,128)(2,1)}), bf16[8,48,256]{2,1,0:T(8,128)(2,1)S(1)}, u32[]{:S(2)}, u32[]{:S(2)}) async-start(bf16[8,48,256]{2,1,0:T(8,128)(2,1)} %bitcast.8), calls=%async_computation.3 | async-start | bytes 393216 | tf_op jit(solution)/shard_map/all_to_all | solution.py:239
  124.1 0.0 copy-done
  124.1 2.1 %unpack.2 = (bf16[48,4096]{1,0:T(8,128)(2,1)}, bf16[48,4096]{1,0:T(8,128)(2,1)}) custom-call(bf16[8,48,1024]{2,1,0:T(8,128)(2,1)} %copy-done), custom_call_target="tpu_custom_call" | custom-call | bytes 1572864 | tf_op jit(solution)/shard_map/unpack/pallas_call | solution.py:80
  126.1 3.8 %all-to-all-done.3.got_ref = bf16[8,48,256]{2,1,0:T(8,128)(2,1)S(1)} async-done(((bf16[8,48,256]{2,1,0:T(8,128)(2,1)}), bf16[8,48,256]{2,1,0:T(8,128)(2,1)S(1)}, u32[]{:S(2)}, u32[]{:S(2)}) %all-to-all-start.3) | async-done | bytes 196640 | tf_op jit(solution)/shard_map/all_to_all | solution.py:239
  130.0 0.0 copy-start.1
  130.0 0.7 copy-done.1
  130.6 1.6 %unpack.3 = (bf16[48,1024]{1,0:T(8,128)(2,1)}, bf16[48,1024]{1,0:T(8,128)(2,1)}) custom-call(bf16[8,48,256]{2,1,0:T(8,128)(2,1)} %copy-done.1), custom_call_target="tpu_custom_call" | custom-call | bytes 393216 | tf_op jit(solution)/shard_map/unpack/pallas_call | solution.py:80
  (6 shorter events, 0.1 us)
Async XLA Ops:
  2.3 10.9 %all-to-all-start.1 = ((bf16[8,48,256]{2,1,0:T(8,128)(2,1)}), bf16[8,48,256]{2,1,0:T(8,128)(2,1)S(1)}, u32[]{:S(2)}, u32[]{:S(2)}) async-start(bf16[8,48,256]{2,1,0:T(8,128)(2,1)} %pack.3), calls=%async_computation.1 | async-start | bytes 393216 | tf_op jit(solution)/shard_map/all_to_all | solution.py:239
  7.3 0.7 copy-start.2
  13.1 44.5 %all-to-all-start = ((bf16[8,48,1024]{2,1,0:T(8,128)(2,1)}), bf16[8,48,1024]{2,1,0:T(8,128)(2,1)S(1)}, u32[]{:S(2)}, u32[]{:S(2)}) async-start(bf16[8,48,1024]{2,1,0:T(8,128)(2,1)} %pack.2), calls=%async_computation | async-start | bytes 1572864 | tf_op jit(solution)/shard_map/all_to_all | solution.py:239
  17.2 15.7 %collective-permute-start.1 = (bf16[384,256]{1,0:T(8,128)(2,1)S(1)}, bf16[384,256]{1,0:T(8,128)(2,1)S(1)}, u32[]{:S(2)}, u32[]{:S(2)}) collective-permute-start(bf16[384,256]{1,0:T(8,128)(2,1)S(1)} %bitcast.11), channel_id=1, source_target_pairs={{0,16},{8,24},{16,32},{24,40},{32,48},{40,56},{48,64},{56,72},{64,... | collective-permute-start | bytes 589832 | tf_op jit(solution)/shard_map/ppermute | solution.py:245
  21.2 14.6 %collective-permute-start = (bf16[384,256]{1,0:T(8,128)(2,1)S(1)}, bf16[384,256]{1,0:T(8,128)(2,1)S(1)}, u32[]{:S(2)}, u32[]{:S(2)}) collective-permute-start(bf16[384,256]{1,0:T(8,128)(2,1)S(1)} %bitcast.12), channel_id=1, source_target_pairs={{0,1},{1,0},{2,3},{3,2},{4,5},{5,4},{6,7},{7,6},{8,9},{9,8},{10,11... | collective-permute-start | bytes 589832 | tf_op jit(solution)/shard_map/ppermute | solution.py:249
  35.8 17.6 %collective-permute-start.2 = (bf16[384,256]{1,0:T(8,128)(2,1)S(1)}, bf16[384,256]{1,0:T(8,128)(2,1)S(1)}, u32[]{:S(2)}, u32[]{:S(2)}) collective-permute-start(bf16[384,256]{1,0:T(8,128)(2,1)S(1)} %collective-permute-done.refs_1_), channel_id=1, source_target_pairs={{0,16},{8,24},{16,32},{24,40},{32,48},{40,56},{48,64},{56,72},{64,... | collective-permute-start | bytes 589832 | tf_op jit(solution)/shard_map/ppermute | solution.py:245
  39.9 17.7 %collective-permute-start.3 = (bf16[384,256]{1,0:T(8,128)(2,1)S(1)}, bf16[384,256]{1,0:T(8,128)(2,1)S(1)}, u32[]{:S(2)}, u32[]{:S(2)}) collective-permute-start(bf16[384,256]{1,0:T(8,128)(2,1)S(1)} %collective-permute-done.1.refs_2_), channel_id=1, source_target_pairs={{0,16},{8,24},{16,32},{24,40},{32,48},{40,56},{48,64},{56,72},{64,... | collective-permute-start | bytes 589832 | tf_op jit(solution)/shard_map/ppermute | solution.py:245
  53.4 8.5 %collective-permute-start.4 = (bf16[384,256]{1,0:T(8,128)(2,1)S(1)}, bf16[384,256]{1,0:T(8,128)(2,1)S(1)}, u32[]{:S(2)}, u32[]{:S(2)}) collective-permute-start(bf16[384,256]{1,0:T(8,128)(2,1)S(1)} %collective-permute-done.2.refs_3_), channel_id=1, source_target_pairs={{0,16},{8,24},{16,32},{24,40},{32,48},{40,56},{48,64},{56,72},{64,... | collective-permute-start | bytes 589832 | tf_op jit(solution)/shard_map/ppermute | solution.py:245
  70.3 23.2 %collective-permute-start.7 = (bf16[384,256]{1,0:T(8,128)(2,1)S(1)}, bf16[384,256]{1,0:T(8,128)(2,1)S(1)}, u32[]{:S(2)}, u32[]{:S(2)}) collective-permute-start(bf16[384,256]{1,0:T(8,128)(2,1)S(1)} %get-tuple-element.26), channel_id=1, source_target_pairs={{16,0},{24,8},{32,16},{40,24},{48,32},{56,40},{64,48},{72,56},{80,... | collective-permute-start | bytes 589832 | tf_op jit(solution)/shard_map/ppermute | solution.py:245
  72.2 21.3 %collective-permute-start.8 = (bf16[384,256]{1,0:T(8,128)(2,1)S(1)}, bf16[384,256]{1,0:T(8,128)(2,1)S(1)}, u32[]{:S(2)}, u32[]{:S(2)}) collective-permute-start(bf16[384,256]{1,0:T(8,128)(2,1)S(1)} %get-tuple-element.27), channel_id=1, source_target_pairs={{32,0},{40,8},{48,16},{56,24},{64,32},{72,40},{80,48},{88,56},{96,... | collective-permute-start | bytes 589832 | tf_op jit(solution)/shard_map/ppermute | solution.py:245
  74.1 44.5 %all-to-all-start.2 = ((bf16[8,48,1024]{2,1,0:T(8,128)(2,1)}), bf16[8,48,1024]{2,1,0:T(8,128)(2,1)S(1)}, u32[]{:S(2)}, u32[]{:S(2)}) async-start(bf16[8,48,1024]{2,1,0:T(8,128)(2,1)} %bitcast.7), calls=%async_computation.2 | async-start | bytes 1572864 | tf_op jit(solution)/shard_map/all_to_all | solution.py:239
  81.8 20.0 %collective-permute-start.5 = (bf16[384,256]{1,0:T(8,128)(2,1)S(1)}, bf16[384,256]{1,0:T(8,128)(2,1)S(1)}, u32[]{:S(2)}, u32[]{:S(2)}) collective-permute-start(bf16[384,256]{1,0:T(8,128)(2,1)S(1)} %get-tuple-element.23), channel_id=1, source_target_pairs={{16,0},{24,8},{32,16},{40,24},{48,32},{56,40},{64,48},{72,56},{80,... | collective-permute-start | bytes 589832 | tf_op jit(solution)/shard_map/ppermute | solution.py:245
  91.5 14.8 %collective-permute-start.6 = (bf16[384,256]{1,0:T(8,128)(2,1)S(1)}, bf16[384,256]{1,0:T(8,128)(2,1)S(1)}, u32[]{:S(2)}, u32[]{:S(2)}) collective-permute-start(bf16[384,256]{1,0:T(8,128)(2,1)S(1)} %get-tuple-element.24), channel_id=1, source_target_pairs={{32,0},{40,8},{48,16},{56,24},{64,32},{72,40},{80,48},{88,56},{96,... | collective-permute-start | bytes 589832 | tf_op jit(solution)/shard_map/ppermute | solution.py:245
  93.5 24.3 %collective-permute-start.9 = (bf16[384,256]{1,0:T(8,128)(2,1)S(1)}, bf16[384,256]{1,0:T(8,128)(2,1)S(1)}, u32[]{:S(2)}, u32[]{:S(2)}) collective-permute-start(bf16[384,256]{1,0:T(8,128)(2,1)S(1)} %add_convert_fusion.1), channel_id=1, source_target_pairs={{0,1},{1,0},{2,3},{3,2},{4,5},{5,4},{6,7},{7,6},{8,9},{9,8},{10,11... | collective-permute-start | bytes 589832 | tf_op jit(solution)/shard_map/ppermute | solution.py:249
  118.7 5.4 %copy-start = (bf16[8,48,1024]{2,1,0:T(8,128)(2,1)}, bf16[8,48,1024]{2,1,0:T(8,128)(2,1)S(1)}, u32[]{:S(2)}) copy-start(bf16[8,48,1024]{2,1,0:T(8,128)(2,1)S(1)} %all-to-all-done.2.got_ref) | copy-start | bytes 2359300
  118.7 11.3 %all-to-all-start.3 = ((bf16[8,48,256]{2,1,0:T(8,128)(2,1)}), bf16[8,48,256]{2,1,0:T(8,128)(2,1)S(1)}, u32[]{:S(2)}, u32[]{:S(2)}) async-start(bf16[8,48,256]{2,1,0:T(8,128)(2,1)} %bitcast.8), calls=%async_computation.3 | async-start | bytes 393216 | tf_op jit(solution)/shard_map/all_to_all | solution.py:239
  130.0 0.7 copy-start.1

commit v5 on v4

--- a/solution.py
+++ b/solution.py
@@ -253,8 +253,8 @@
     place = lax.axis_index(CTX)
     half = lax.axis_index("y_high").astype(jnp.int32)
     own = exchanged(pack(keys, values)).reshape(ROWS, 2 * D)
-    theirs = half_swapped(own)
-    theirs, own1 = lax.optimization_barrier((theirs, shifted(own, 2)))
+    own1 = shifted(own, 2)
+    own1, theirs = lax.optimization_barrier((own1, half_swapped(own)))
     own2 = shifted(own1, 2)
     qdo = exchanged(pack(queries, output_gradient)).reshape(ROWS, QDO)
     theirs1 = shifted(theirs, 2)

time: 131 us -> 128 us (0.977); the launches traced: 132 us -> 128 us
  starting transfers between devices: 66.2 us -> 52.5 us
  waiting for transfers between devices: 46.6 us -> 54.3 us
  Pallas kernels: 15.8 us -> 17.2 us
    ppermute x8, starting transfers between devices: 29.3 us -> 17.4 us  [shifted(): return lax.ppermute(shard, CTX, pairs)]
    ppermute x8, waiting for transfers between devices: 25.6 us -> 37.3 us  [shifted(): return lax.ppermute(shard, CTX, pairs)]
    ppermute x2, waiting for transfers between devices: 14.4 us -> 10.3 us  [half_swapped(): return lax.ppermute(shard, 'y_high', [(0, 1), (1, 0)])]
    ppermute x2, starting transfers between devices: 14.9 us -> 12.3 us  [half_swapped(): return lax.ppermute(shard, 'y_high', [(0, 1), (1, 0)])]
    pallas_call x1, Pallas kernels: 8.37 us -> 9.78 us  [attention(): pl.pallas_call(attention_kernel, out_shape=(jax.ShapeDtypeStruct((ROWS, Q...]
  transfers between devices with their start and end apart: 14 -> 14, of which waited for: 9 -> 10; matrix products, arithmetic and copies ran while one was open for 1% -> 1% of each run, Pallas kernels for 3% -> 3%
where the time goes in v5:
time: 128 us
  waiting for transfers between devices  54.3 us (42%)
  starting transfers between devices  52.5 us (41%)
  Pallas kernels  17.2 us (13%)
  local copies, waits for them, and re-layouts  1.62 us (1%)
    ppermute x8, waiting for transfers between devices, shifted(): return lax.ppermute(shard, CTX, pairs)  37.3 us
    all_to_all x4, starting transfers between devices, exchanged(): lax.all_to_all(pieces, ('core', 'x'), split_axis=0, concat_axis=0, tiled=...  22.8 us
    ppermute x8, starting transfers between devices, shifted(): return lax.ppermute(shard, CTX, pairs)  17.4 us
    ppermute x2, starting transfers between devices, half_swapped(): return lax.ppermute(shard, 'y_high', [(0, 1), (1, 0)])  12.3 us
    ppermute x2, waiting for transfers between devices, half_swapped(): return lax.ppermute(shard, 'y_high', [(0, 1), (1, 0)])  10.3 us
    pallas_call x1, Pallas kernels, attention(): pl.pallas_call(attention_kernel, out_shape=(jax.ShapeDtypeStruct((ROWS, Q...  9.78 us
    all_to_all x4, waiting for transfers between devices, exchanged(): lax.all_to_all(pieces, ('core', 'x'), split_axis=0, concat_axis=0, tiled=...  6.66 us
    pallas_call x2, Pallas kernels, pack(): pl.pallas_call(pack_kernel, out_shape=jax.ShapeDtypeStruct((HEADS, SUB, 2...  3.72 us
  transfers between devices with their start and end apart: 14, of which 10 were waited for; matrix products, arithmetic and copies ran while one was open for 1% of the time, Pallas kernels for 3%

profile of v5, /device:TPU:9, one launch (start us, length us, event | category | flops | bytes accessed | tf_op | source)
XLA Modules:
  0.0 127.6 jit_solution(15740520989219221372)
XLA Ops:
  0.6 1.7 %pack.3 = bf16[8,48,256]{2,1,0:T(8,128)(2,1)} custom-call(bf16[48,1024]{1,0:T(8,128)(2,1)} %a_ref.3, bf16[48,1024]{1,0:T(8,128)(2,1)} %b_ref.3), custom_call_target="tpu_custom_call" | custom-call | bytes 393216 | tf_op jit(solution)/shard_map/pack/pallas_call | solution.py:58
  2.3 5.0 %all-to-all-start.1 = ((bf16[8,48,256]{2,1,0:T(8,128)(2,1)}), bf16[8,48,256]{2,1,0:T(8,128)(2,1)S(1)}, u32[]{:S(2)}, u32[]{:S(2)}) async-start(bf16[8,48,256]{2,1,0:T(8,128)(2,1)} %pack.3), calls=%async_computation.1 | async-start | bytes 393216 | tf_op jit(solution)/shard_map/all_to_all | solution.py:239
  7.3 0.0 copy-start.2
  7.3 0.7 copy-done.2
  7.9 0.1 copy.11
  8.0 0.1 reduce-window.8
  8.1 0.1 reduce
  8.2 2.1 %pack.2 = bf16[8,48,1024]{2,1,0:T(8,128)(2,1)} custom-call(bf16[48,4096]{1,0:T(8,128)(2,1)} %a_ref.2, bf16[48,4096]{1,0:T(8,128)(2,1)} %b_ref.2), custom_call_target="tpu_custom_call" | custom-call | bytes 1572864 | tf_op jit(solution)/shard_map/pack/pallas_call | solution.py:58
  10.3 2.8 %all-to-all-done.1 = bf16[8,48,256]{2,1,0:T(8,128)(2,1)S(1)} async-done(((bf16[8,48,256]{2,1,0:T(8,128)(2,1)}), bf16[8,48,256]{2,1,0:T(8,128)(2,1)S(1)}, u32[]{:S(2)}, u32[]{:S(2)}) %all-to-all-start.1) | async-done | bytes 196640 | tf_op jit(solution)/shard_map/all_to_all | solution.py:239
  13.1 3.9 %all-to-all-start = ((bf16[8,48,1024]{2,1,0:T(8,128)(2,1)}), bf16[8,48,1024]{2,1,0:T(8,128)(2,1)S(1)}, u32[]{:S(2)}, u32[]{:S(2)}) async-start(bf16[8,48,1024]{2,1,0:T(8,128)(2,1)} %pack.2), calls=%async_computation | async-start | bytes 1572864 | tf_op jit(solution)/shard_map/all_to_all | solution.py:239
  17.0 0.1 select_reduce_fusion
  17.1 0.1 slice.7
  17.2 6.6 %collective-permute-start.1 = (bf16[384,256]{1,0:T(8,128)(2,1)S(1)}, bf16[384,256]{1,0:T(8,128)(2,1)S(1)}, u32[]{:S(2)}, u32[]{:S(2)}) collective-permute-start(bf16[384,256]{1,0:T(8,128)(2,1)S(1)} %bitcast.11), channel_id=1, source_target_pairs={{0,1},{1,0},{2,3},{3,2},{4,5},{5,4},{6,7},{7,6},{8,9},{9,8},{10,11... | collective-permute-start | bytes 589832 | tf_op jit(solution)/shard_map/ppermute | solution.py:249
  23.8 4.0 %collective-permute-start = (bf16[384,256]{1,0:T(8,128)(2,1)S(1)}, bf16[384,256]{1,0:T(8,128)(2,1)S(1)}, u32[]{:S(2)}, u32[]{:S(2)}) collective-permute-start(bf16[384,256]{1,0:T(8,128)(2,1)S(1)} %bitcast.12), channel_id=1, source_target_pairs={{0,16},{8,24},{16,32},{24,40},{32,48},{40,56},{48,64},{56,72},{64,... | collective-permute-start | bytes 589832 | tf_op jit(solution)/shard_map/ppermute | solution.py:245
  27.8 0.1 slice.6
  27.9 4.2 %collective-permute-done.1.refs_1_ = bf16[384,256]{1,0:T(8,128)(2,1)S(1)} collective-permute-done((bf16[384,256]{1,0:T(8,128)(2,1)S(1)}, bf16[384,256]{1,0:T(8,128)(2,1)S(1)}, u32[]{:S(2)}, u32[]{:S(2)}) %collective-permute-start.1) | collective-permute-done | bytes 196640 | tf_op jit(solution)/shard_map/ppermute | solution.py:249
  32.1 14.7 %collective-permute-done.refs_2_ = bf16[384,256]{1,0:T(8,128)(2,1)S(1)} collective-permute-done((bf16[384,256]{1,0:T(8,128)(2,1)S(1)}, bf16[384,256]{1,0:T(8,128)(2,1)S(1)}, u32[]{:S(2)}, u32[]{:S(2)}) %collective-permute-start) | collective-permute-done | bytes 196640 | tf_op jit(solution)/shard_map/ppermute | solution.py:245
  46.8 1.9 %collective-permute-start.2 = (bf16[384,256]{1,0:T(8,128)(2,1)S(1)}, bf16[384,256]{1,0:T(8,128)(2,1)S(1)}, u32[]{:S(2)}, u32[]{:S(2)}) collective-permute-start(bf16[384,256]{1,0:T(8,128)(2,1)S(1)} %collective-permute-done.1.refs_1_), channel_id=1, source_target_pairs={{0,16},{8,24},{16,32},{24,40},{32,48},{40,56},{48,64},{56,72},{64,... | collective-permute-start | bytes 589832 | tf_op jit(solution)/shard_map/ppermute | solution.py:245
  48.7 0.1 pad_add_fusion.span
  48.8 1.9 %collective-permute-start.3 = (bf16[384,256]{1,0:T(8,128)(2,1)S(1)}, bf16[384,256]{1,0:T(8,128)(2,1)S(1)}, u32[]{:S(2)}, u32[]{:S(2)}) collective-permute-start(bf16[384,256]{1,0:T(8,128)(2,1)S(1)} %collective-permute-done.refs_2_), channel_id=1, source_target_pairs={{0,16},{8,24},{16,32},{24,40},{32,48},{40,56},{48,64},{56,72},{64,... | collective-permute-start | bytes 589832 | tf_op jit(solution)/shard_map/ppermute | solution.py:245
  50.7 5.6 %collective-permute-done.2.refs_3_ = bf16[384,256]{1,0:T(8,128)(2,1)S(1)} collective-permute-done((bf16[384,256]{1,0:T(8,128)(2,1)S(1)}, bf16[384,256]{1,0:T(8,128)(2,1)S(1)}, u32[]{:S(2)}, u32[]{:S(2)}) %collective-permute-start.2) | collective-permute-done | bytes 196640 | tf_op jit(solution)/shard_map/ppermute | solution.py:245
  56.4 1.9 %collective-permute-start.4 = (bf16[384,256]{1,0:T(8,128)(2,1)S(1)}, bf16[384,256]{1,0:T(8,128)(2,1)S(1)}, u32[]{:S(2)}, u32[]{:S(2)}) collective-permute-start(bf16[384,256]{1,0:T(8,128)(2,1)S(1)} %collective-permute-done.2.refs_3_), channel_id=1, source_target_pairs={{0,16},{8,24},{16,32},{24,40},{32,48},{40,56},{48,64},{56,72},{64,... | collective-permute-start | bytes 589832 | tf_op jit(solution)/shard_map/ppermute | solution.py:245
  58.3 2.3 %collective-permute-done.3.refs_4_ = bf16[384,256]{1,0:T(8,128)(2,1)S(1)} collective-permute-done((bf16[384,256]{1,0:T(8,128)(2,1)S(1)}, bf16[384,256]{1,0:T(8,128)(2,1)S(1)}, u32[]{:S(2)}, u32[]{:S(2)}) %collective-permute-start.3) | collective-permute-done | bytes 196640 | tf_op jit(solution)/shard_map/ppermute | solution.py:245
  60.6 0.0 all-to-all-done
  60.6 4.3 %collective-permute-done.4.refs_5_ = bf16[384,256]{1,0:T(8,128)(2,1)S(1)} collective-permute-done((bf16[384,256]{1,0:T(8,128)(2,1)S(1)}, bf16[384,256]{1,0:T(8,128)(2,1)S(1)}, u32[]{:S(2)}, u32[]{:S(2)}) %collective-permute-start.4) | collective-permute-done | bytes 196640 | tf_op jit(solution)/shard_map/ppermute | solution.py:245
  64.9 9.8 %attention.1 = (bf16[384,1024]{1,0:T(8,128)(2,1)}, f32[384,256]{1,0:T(8,128)S(1)}, f32[384,256]{1,0:T(8,128)S(1)}, bf16[384,256]{1,0:T(8,128)(2,1)S(1)}, bf16[38...) custom-call(s32[1]{0:T(128)} %bitcast.half, s32[6]{0:T(128)S(1)} %pad_add_fusion.span, ...), custom_call_target="tpu_custom_call" | custom-call | flops 2831155200 | bytes 4194304 | tf_op jit(solution)/shard_map/attention/pallas_call | solution.py:197
  74.7 1.9 %collective-permute-start.7 = (bf16[384,256]{1,0:T(8,128)(2,1)S(1)}, bf16[384,256]{1,0:T(8,128)(2,1)S(1)}, u32[]{:S(2)}, u32[]{:S(2)}) collective-permute-start(bf16[384,256]{1,0:T(8,128)(2,1)S(1)} %get-tuple-element.26), channel_id=1, source_target_pairs={{16,0},{24,8},{32,16},{40,24},{48,32},{56,40},{64,48},{72,56},{80,... | collective-permute-start | bytes 589832 | tf_op jit(solution)/shard_map/ppermute | solution.py:245
  76.6 1.9 %collective-permute-start.8 = (bf16[384,256]{1,0:T(8,128)(2,1)S(1)}, bf16[384,256]{1,0:T(8,128)(2,1)S(1)}, u32[]{:S(2)}, u32[]{:S(2)}) collective-permute-start(bf16[384,256]{1,0:T(8,128)(2,1)S(1)} %get-tuple-element.27), channel_id=1, source_target_pairs={{32,0},{40,8},{48,16},{56,24},{64,32},{72,40},{80,48},{88,56},{96,... | collective-permute-start | bytes 589832 | tf_op jit(solution)/shard_map/ppermute | solution.py:245
  78.5 8.6 %all-to-all-start.2 = ((bf16[8,48,1024]{2,1,0:T(8,128)(2,1)}), bf16[8,48,1024]{2,1,0:T(8,128)(2,1)S(1)}, u32[]{:S(2)}, u32[]{:S(2)}) async-start(bf16[8,48,1024]{2,1,0:T(8,128)(2,1)} %bitcast.7), calls=%async_computation.2 | async-start | bytes 1572864 | tf_op jit(solution)/shard_map/all_to_all | solution.py:239
  87.1 1.9 %collective-permute-start.5 = (bf16[384,256]{1,0:T(8,128)(2,1)S(1)}, bf16[384,256]{1,0:T(8,128)(2,1)S(1)}, u32[]{:S(2)}, u32[]{:S(2)}) collective-permute-start(bf16[384,256]{1,0:T(8,128)(2,1)S(1)} %get-tuple-element.23), channel_id=1, source_target_pairs={{16,0},{24,8},{32,16},{40,24},{48,32},{56,40},{64,48},{72,56},{80,... | collective-permute-start | bytes 589832 | tf_op jit(solution)/shard_map/ppermute | solution.py:245
  89.1 1.9 %collective-permute-start.6 = (bf16[384,256]{1,0:T(8,128)(2,1)S(1)}, bf16[384,256]{1,0:T(8,128)(2,1)S(1)}, u32[]{:S(2)}, u32[]{:S(2)}) collective-permute-start(bf16[384,256]{1,0:T(8,128)(2,1)S(1)} %get-tuple-element.24), channel_id=1, source_target_pairs={{32,0},{40,8},{48,16},{56,24},{64,32},{72,40},{80,48},{88,56},{96,... | collective-permute-start | bytes 589832 | tf_op jit(solution)/shard_map/ppermute | solution.py:245
  91.0 0.0 collective-permute-done.7
  91.0 0.0 collective-permute-done.8
  91.0 0.1 add_convert_fusion.1
  91.1 5.7 %collective-permute-start.9 = (bf16[384,256]{1,0:T(8,128)(2,1)S(1)}, bf16[384,256]{1,0:T(8,128)(2,1)S(1)}, u32[]{:S(2)}, u32[]{:S(2)}) collective-permute-start(bf16[384,256]{1,0:T(8,128)(2,1)S(1)} %add_convert_fusion.1), channel_id=1, source_target_pairs={{0,1},{1,0},{2,3},{3,2},{4,5},{5,4},{6,7},{7,6},{8,9},{9,8},{10,11... | collective-permute-start | bytes 589832 | tf_op jit(solution)/shard_map/ppermute | solution.py:249
  96.8 2.5 %collective-permute-done.5 = bf16[384,256]{1,0:T(8,128)(2,1)S(1)} collective-permute-done((bf16[384,256]{1,0:T(8,128)(2,1)S(1)}, bf16[384,256]{1,0:T(8,128)(2,1)S(1)}, u32[]{:S(2)}, u32[]{:S(2)}) %collective-permute-start.5) | collective-permute-done | bytes 196640 | tf_op jit(solution)/shard_map/ppermute | solution.py:245
  99.4 7.9 %collective-permute-done.6 = bf16[384,256]{1,0:T(8,128)(2,1)S(1)} collective-permute-done((bf16[384,256]{1,0:T(8,128)(2,1)S(1)}, bf16[384,256]{1,0:T(8,128)(2,1)S(1)}, u32[]{:S(2)}, u32[]{:S(2)}) %collective-permute-start.6) | collective-permute-done | bytes 196640 | tf_op jit(solution)/shard_map/ppermute | solution.py:245
  107.3 6.0 %collective-permute-done.9 = bf16[384,256]{1,0:T(8,128)(2,1)S(1)} collective-permute-done((bf16[384,256]{1,0:T(8,128)(2,1)S(1)}, bf16[384,256]{1,0:T(8,128)(2,1)S(1)}, u32[]{:S(2)}, u32[]{:S(2)}) %collective-permute-start.9) | collective-permute-done | bytes 196640 | tf_op jit(solution)/shard_map/ppermute | solution.py:249
  113.3 0.8 add_convert_fusion
  114.1 0.0 all-to-all-done.2.got_ref
  114.1 0.0 copy-start
  114.1 5.3 %all-to-all-start.3 = ((bf16[8,48,256]{2,1,0:T(8,128)(2,1)}), bf16[8,48,256]{2,1,0:T(8,128)(2,1)S(1)}, u32[]{:S(2)}, u32[]{:S(2)}) async-start(bf16[8,48,256]{2,1,0:T(8,128)(2,1)} %bitcast.8), calls=%async_computation.3 | async-start | bytes 393216 | tf_op jit(solution)/shard_map/all_to_all | solution.py:239
  119.4 0.0 copy-done
  119.4 2.1 %unpack.2 = (bf16[48,4096]{1,0:T(8,128)(2,1)}, bf16[48,4096]{1,0:T(8,128)(2,1)}) custom-call(bf16[8,48,1024]{2,1,0:T(8,128)(2,1)} %copy-done), custom_call_target="tpu_custom_call" | custom-call | bytes 1572864 | tf_op jit(solution)/shard_map/unpack/pallas_call | solution.py:80
  121.5 3.8 %all-to-all-done.3.got_ref = bf16[8,48,256]{2,1,0:T(8,128)(2,1)S(1)} async-done(((bf16[8,48,256]{2,1,0:T(8,128)(2,1)}), bf16[8,48,256]{2,1,0:T(8,128)(2,1)S(1)}, u32[]{:S(2)}, u32[]{:S(2)}) %all-to-all-start.3) | async-done | bytes 196640 | tf_op jit(solution)/shard_map/all_to_all | solution.py:239
  125.3 0.0 copy-start.1
  125.3 0.7 copy-done.1
  126.0 1.6 %unpack.3 = (bf16[48,1024]{1,0:T(8,128)(2,1)}, bf16[48,1024]{1,0:T(8,128)(2,1)}) custom-call(bf16[8,48,256]{2,1,0:T(8,128)(2,1)} %copy-done.1), custom_call_target="tpu_custom_call" | custom-call | bytes 393216 | tf_op jit(solution)/shard_map/unpack/pallas_call | solution.py:80
  (6 shorter events, 0.1 us)
Async XLA Ops:
  2.3 10.9 %all-to-all-start.1 = ((bf16[8,48,256]{2,1,0:T(8,128)(2,1)}), bf16[8,48,256]{2,1,0:T(8,128)(2,1)S(1)}, u32[]{:S(2)}, u32[]{:S(2)}) async-start(bf16[8,48,256]{2,1,0:T(8,128)(2,1)} %pack.3), calls=%async_computation.1 | async-start | bytes 393216 | tf_op jit(solution)/shard_map/all_to_all | solution.py:239
  7.3 0.7 copy-start.2
  13.1 47.4 %all-to-all-start = ((bf16[8,48,1024]{2,1,0:T(8,128)(2,1)}), bf16[8,48,1024]{2,1,0:T(8,128)(2,1)S(1)}, u32[]{:S(2)}, u32[]{:S(2)}) async-start(bf16[8,48,1024]{2,1,0:T(8,128)(2,1)} %pack.2), calls=%async_computation | async-start | bytes 1572864 | tf_op jit(solution)/shard_map/all_to_all | solution.py:239
  17.2 14.9 %collective-permute-start.1 = (bf16[384,256]{1,0:T(8,128)(2,1)S(1)}, bf16[384,256]{1,0:T(8,128)(2,1)S(1)}, u32[]{:S(2)}, u32[]{:S(2)}) collective-permute-start(bf16[384,256]{1,0:T(8,128)(2,1)S(1)} %bitcast.11), channel_id=1, source_target_pairs={{0,1},{1,0},{2,3},{3,2},{4,5},{5,4},{6,7},{7,6},{8,9},{9,8},{10,11... | collective-permute-start | bytes 589832 | tf_op jit(solution)/shard_map/ppermute | solution.py:249
  23.8 23.0 %collective-permute-start = (bf16[384,256]{1,0:T(8,128)(2,1)S(1)}, bf16[384,256]{1,0:T(8,128)(2,1)S(1)}, u32[]{:S(2)}, u32[]{:S(2)}) collective-permute-start(bf16[384,256]{1,0:T(8,128)(2,1)S(1)} %bitcast.12), channel_id=1, source_target_pairs={{0,16},{8,24},{16,32},{24,40},{32,48},{40,56},{48,64},{56,72},{64,... | collective-permute-start | bytes 589832 | tf_op jit(solution)/shard_map/ppermute | solution.py:245
  46.8 9.6 %collective-permute-start.2 = (bf16[384,256]{1,0:T(8,128)(2,1)S(1)}, bf16[384,256]{1,0:T(8,128)(2,1)S(1)}, u32[]{:S(2)}, u32[]{:S(2)}) collective-permute-start(bf16[384,256]{1,0:T(8,128)(2,1)S(1)} %collective-permute-done.1.refs_1_), channel_id=1, source_target_pairs={{0,16},{8,24},{16,32},{24,40},{32,48},{40,56},{48,64},{56,72},{64,... | collective-permute-start | bytes 589832 | tf_op jit(solution)/shard_map/ppermute | solution.py:245
  48.8 11.8 %collective-permute-start.3 = (bf16[384,256]{1,0:T(8,128)(2,1)S(1)}, bf16[384,256]{1,0:T(8,128)(2,1)S(1)}, u32[]{:S(2)}, u32[]{:S(2)}) collective-permute-start(bf16[384,256]{1,0:T(8,128)(2,1)S(1)} %collective-permute-done.refs_2_), channel_id=1, source_target_pairs={{0,16},{8,24},{16,32},{24,40},{32,48},{40,56},{48,64},{56,72},{64,... | collective-permute-start | bytes 589832 | tf_op jit(solution)/shard_map/ppermute | solution.py:245
  56.4 8.5 %collective-permute-start.4 = (bf16[384,256]{1,0:T(8,128)(2,1)S(1)}, bf16[384,256]{1,0:T(8,128)(2,1)S(1)}, u32[]{:S(2)}, u32[]{:S(2)}) collective-permute-start(bf16[384,256]{1,0:T(8,128)(2,1)S(1)} %collective-permute-done.2.refs_3_), channel_id=1, source_target_pairs={{0,16},{8,24},{16,32},{24,40},{32,48},{40,56},{48,64},{56,72},{64,... | collective-permute-start | bytes 589832 | tf_op jit(solution)/shard_map/ppermute | solution.py:245
  74.7 16.3 %collective-permute-start.7 = (bf16[384,256]{1,0:T(8,128)(2,1)S(1)}, bf16[384,256]{1,0:T(8,128)(2,1)S(1)}, u32[]{:S(2)}, u32[]{:S(2)}) collective-permute-start(bf16[384,256]{1,0:T(8,128)(2,1)S(1)} %get-tuple-element.26), channel_id=1, source_target_pairs={{16,0},{24,8},{32,16},{40,24},{48,32},{56,40},{64,48},{72,56},{80,... | collective-permute-start | bytes 589832 | tf_op jit(solution)/shard_map/ppermute | solution.py:245
  76.6 14.4 %collective-permute-start.8 = (bf16[384,256]{1,0:T(8,128)(2,1)S(1)}, bf16[384,256]{1,0:T(8,128)(2,1)S(1)}, u32[]{:S(2)}, u32[]{:S(2)}) collective-permute-start(bf16[384,256]{1,0:T(8,128)(2,1)S(1)} %get-tuple-element.27), channel_id=1, source_target_pairs={{32,0},{40,8},{48,16},{56,24},{64,32},{72,40},{80,48},{88,56},{96,... | collective-permute-start | bytes 589832 | tf_op jit(solution)/shard_map/ppermute | solution.py:245
  78.5 35.6 %all-to-all-start.2 = ((bf16[8,48,1024]{2,1,0:T(8,128)(2,1)}), bf16[8,48,1024]{2,1,0:T(8,128)(2,1)S(1)}, u32[]{:S(2)}, u32[]{:S(2)}) async-start(bf16[8,48,1024]{2,1,0:T(8,128)(2,1)} %bitcast.7), calls=%async_computation.2 | async-start | bytes 1572864 | tf_op jit(solution)/shard_map/all_to_all | solution.py:239
  87.1 12.2 %collective-permute-start.5 = (bf16[384,256]{1,0:T(8,128)(2,1)S(1)}, bf16[384,256]{1,0:T(8,128)(2,1)S(1)}, u32[]{:S(2)}, u32[]{:S(2)}) collective-permute-start(bf16[384,256]{1,0:T(8,128)(2,1)S(1)} %get-tuple-element.23), channel_id=1, source_target_pairs={{16,0},{24,8},{32,16},{40,24},{48,32},{56,40},{64,48},{72,56},{80,... | collective-permute-start | bytes 589832 | tf_op jit(solution)/shard_map/ppermute | solution.py:245
  89.1 18.2 %collective-permute-start.6 = (bf16[384,256]{1,0:T(8,128)(2,1)S(1)}, bf16[384,256]{1,0:T(8,128)(2,1)S(1)}, u32[]{:S(2)}, u32[]{:S(2)}) collective-permute-start(bf16[384,256]{1,0:T(8,128)(2,1)S(1)} %get-tuple-element.24), channel_id=1, source_target_pairs={{32,0},{40,8},{48,16},{56,24},{64,32},{72,40},{80,48},{88,56},{96,... | collective-permute-start | bytes 589832 | tf_op jit(solution)/shard_map/ppermute | solution.py:245
  91.1 22.2 %collective-permute-start.9 = (bf16[384,256]{1,0:T(8,128)(2,1)S(1)}, bf16[384,256]{1,0:T(8,128)(2,1)S(1)}, u32[]{:S(2)}, u32[]{:S(2)}) collective-permute-start(bf16[384,256]{1,0:T(8,128)(2,1)S(1)} %add_convert_fusion.1), channel_id=1, source_target_pairs={{0,1},{1,0},{2,3},{3,2},{4,5},{5,4},{6,7},{7,6},{8,9},{9,8},{10,11... | collective-permute-start | bytes 589832 | tf_op jit(solution)/shard_map/ppermute | solution.py:249
  114.1 5.3 %copy-start = (bf16[8,48,1024]{2,1,0:T(8,128)(2,1)}, bf16[8,48,1024]{2,1,0:T(8,128)(2,1)S(1)}, u32[]{:S(2)}) copy-start(bf16[8,48,1024]{2,1,0:T(8,128)(2,1)S(1)} %all-to-all-done.2.got_ref) | copy-start | bytes 2359300
  114.1 11.2 %all-to-all-start.3 = ((bf16[8,48,256]{2,1,0:T(8,128)(2,1)}), bf16[8,48,256]{2,1,0:T(8,128)(2,1)S(1)}, u32[]{:S(2)}, u32[]{:S(2)}) async-start(bf16[8,48,256]{2,1,0:T(8,128)(2,1)} %bitcast.8), calls=%async_computation.3 | async-start | bytes 393216 | tf_op jit(solution)/shard_map/all_to_all | solution.py:239
  125.3 0.7 copy-start.1

commit v6 on v4

--- a/solution.py
+++ b/solution.py
@@ -263,12 +263,14 @@
 
     blocks = (own, theirs, own1, theirs1, own2, theirs2)
     odq, g0, h0, g1, h1, g2, h2 = attention(half.reshape(1), span, start, own_pos, qdo, blocks)
-    h1, h2 = shifted(h1, -2), shifted(h2, -4)
+    h1 = h1.astype(jnp.float32) + shifted(h2, -2).astype(jnp.float32)
+    h1 = shifted(h1.astype(jnp.bfloat16), -2)
     odq_rows = exchanged(odq.reshape(HEADS, SUB, QDO))
-    theirs = (h0 + h1.astype(jnp.float32) + h2.astype(jnp.float32)).astype(jnp.bfloat16)
+    theirs = (h0 + h1.astype(jnp.float32)).astype(jnp.bfloat16)
     got = half_swapped(theirs).astype(jnp.float32)
-    g1, g2 = shifted(g1, -2), shifted(g2, -4)
-    total = g0 + g1.astype(jnp.float32) + g2.astype(jnp.float32) + got
+    g1 = g1.astype(jnp.float32) + shifted(g2, -2).astype(jnp.float32)
+    g1 = shifted(g1.astype(jnp.bfloat16), -2)
+    total = g0 + g1.astype(jnp.float32) + got
     odq_rows, total = lax.optimization_barrier((odq_rows, total.astype(jnp.bfloat16)))
     dkv_rows = exchanged(total.reshape(HEADS, SUB, 2 * D))
     return (*unpack(odq_rows), *unpack(dkv_rows))

time: 131 us -> 128 us (0.977)
  starting transfers between devices: 66.2 us -> 58.4 us
  Pallas kernels: 15.8 us -> 20 us
    pallas_call x1, Pallas kernels: 8.37 us -> 12.5 us  [attention(): pl.pallas_call(attention_kernel, out_shape=(jax.ShapeDtypeStruct((ROWS, Q...]
    ppermute x8, starting transfers between devices: 29.3 us -> 25.2 us  [shifted(): return lax.ppermute(shard, CTX, pairs)]
    ppermute x2, starting transfers between devices: 14.9 us -> 11.5 us  [half_swapped(): return lax.ppermute(shard, 'y_high', [(0, 1), (1, 0)])]
    ppermute x2, waiting for transfers between devices: 14.4 us -> 11.2 us  [half_swapped(): return lax.ppermute(shard, 'y_high', [(0, 1), (1, 0)])]
    ppermute x8, waiting for transfers between devices: 25.6 us -> 28.2 us  [shifted(): return lax.ppermute(shard, CTX, pairs)]
  transfers between devices with their start and end apart: 14 -> 14, of which waited for: 9 -> 10; matrix products, arithmetic and copies ran while one was open for 1% -> 1% of each run, Pallas kernels for 3% -> 3%
where the time goes in v6:
time: 128 us
  starting transfers between devices  58.4 us (46%)
  waiting for transfers between devices  46.1 us (36%)
  Pallas kernels  20 us (16%)
  local copies, waits for them, and re-layouts  1.62 us (1%)
  other arithmetic  1.32 us (1%)
    ppermute x8, waiting for transfers between devices, shifted(): return lax.ppermute(shard, CTX, pairs)  28.2 us
    ppermute x8, starting transfers between devices, shifted(): return lax.ppermute(shard, CTX, pairs)  25.2 us
    all_to_all x4, starting transfers between devices, exchanged(): lax.all_to_all(pieces, ('core', 'x'), split_axis=0, concat_axis=0, tiled=...  21.7 us
    pallas_call x1, Pallas kernels, attention(): pl.pallas_call(attention_kernel, out_shape=(jax.ShapeDtypeStruct((ROWS, Q...  12.5 us
    ppermute x2, starting transfers between devices, half_swapped(): return lax.ppermute(shard, 'y_high', [(0, 1), (1, 0)])  11.5 us
    ppermute x2, waiting for transfers between devices, half_swapped(): return lax.ppermute(shard, 'y_high', [(0, 1), (1, 0)])  11.2 us
    all_to_all x4, waiting for transfers between devices, exchanged(): lax.all_to_all(pieces, ('core', 'x'), split_axis=0, concat_axis=0, tiled=...  6.66 us
    pallas_call x2, Pallas kernels, pack(): pl.pallas_call(pack_kernel, out_shape=jax.ShapeDtypeStruct((HEADS, SUB, 2...  3.72 us
  transfers between devices with their start and end apart: 14, of which 10 were waited for; matrix products, arithmetic and copies ran while one was open for 1% of the time, Pallas kernels for 3%

profile of v6, /device:TPU:9, one launch (start us, length us, event | category | flops | bytes accessed | tf_op | source)
XLA Modules:
  0.0 128.2 jit_solution(17227507007838843170)
XLA Ops:
  0.6 1.7 %pack.3 = bf16[8,48,256]{2,1,0:T(8,128)(2,1)} custom-call(bf16[48,1024]{1,0:T(8,128)(2,1)} %a_ref.3, bf16[48,1024]{1,0:T(8,128)(2,1)} %b_ref.3), custom_call_target="tpu_custom_call" | custom-call | bytes 393216 | tf_op jit(solution)/shard_map/pack/pallas_call | solution.py:58
  2.3 5.0 %all-to-all-start.1 = ((bf16[8,48,256]{2,1,0:T(8,128)(2,1)}), bf16[8,48,256]{2,1,0:T(8,128)(2,1)S(1)}, u32[]{:S(2)}, u32[]{:S(2)}) async-start(bf16[8,48,256]{2,1,0:T(8,128)(2,1)} %pack.3), calls=%async_computation.1 | async-start | bytes 393216 | tf_op jit(solution)/shard_map/all_to_all | solution.py:239
  7.3 0.0 copy-start.2
  7.3 0.7 copy-done.2
  7.9 0.1 copy.11
  8.0 0.1 reduce-window.8
  8.1 0.1 reduce
  8.2 2.1 %pack.2 = bf16[8,48,1024]{2,1,0:T(8,128)(2,1)} custom-call(bf16[48,4096]{1,0:T(8,128)(2,1)} %a_ref.2, bf16[48,4096]{1,0:T(8,128)(2,1)} %b_ref.2), custom_call_target="tpu_custom_call" | custom-call | bytes 1572864 | tf_op jit(solution)/shard_map/pack/pallas_call | solution.py:58
  10.3 2.8 %all-to-all-done.1 = bf16[8,48,256]{2,1,0:T(8,128)(2,1)S(1)} async-done(((bf16[8,48,256]{2,1,0:T(8,128)(2,1)}), bf16[8,48,256]{2,1,0:T(8,128)(2,1)S(1)}, u32[]{:S(2)}, u32[]{:S(2)}) %all-to-all-start.1) | async-done | bytes 196640 | tf_op jit(solution)/shard_map/all_to_all | solution.py:239
  13.1 3.9 %all-to-all-start = ((bf16[8,48,1024]{2,1,0:T(8,128)(2,1)}), bf16[8,48,1024]{2,1,0:T(8,128)(2,1)S(1)}, u32[]{:S(2)}, u32[]{:S(2)}) async-start(bf16[8,48,1024]{2,1,0:T(8,128)(2,1)} %pack.2), calls=%async_computation | async-start | bytes 1572864 | tf_op jit(solution)/shard_map/all_to_all | solution.py:239
  17.0 0.1 select_reduce_fusion
  17.1 0.1 slice.7
  17.2 4.0 %collective-permute-start.1 = (bf16[384,256]{1,0:T(8,128)(2,1)S(1)}, bf16[384,256]{1,0:T(8,128)(2,1)S(1)}, u32[]{:S(2)}, u32[]{:S(2)}) collective-permute-start(bf16[384,256]{1,0:T(8,128)(2,1)S(1)} %bitcast.11), channel_id=1, source_target_pairs={{0,16},{8,24},{16,32},{24,40},{32,48},{40,56},{48,64},{56,72},{64,... | collective-permute-start | bytes 589832 | tf_op jit(solution)/shard_map/ppermute | solution.py:245
  21.2 6.6 %collective-permute-start = (bf16[384,256]{1,0:T(8,128)(2,1)S(1)}, bf16[384,256]{1,0:T(8,128)(2,1)S(1)}, u32[]{:S(2)}, u32[]{:S(2)}) collective-permute-start(bf16[384,256]{1,0:T(8,128)(2,1)S(1)} %bitcast.12), channel_id=1, source_target_pairs={{0,1},{1,0},{2,3},{3,2},{4,5},{5,4},{6,7},{7,6},{8,9},{9,8},{10,11... | collective-permute-start | bytes 589832 | tf_op jit(solution)/shard_map/ppermute | solution.py:249
  27.8 0.1 slice.6
  27.9 5.0 %collective-permute-done.1.refs_2_ = bf16[384,256]{1,0:T(8,128)(2,1)S(1)} collective-permute-done((bf16[384,256]{1,0:T(8,128)(2,1)S(1)}, bf16[384,256]{1,0:T(8,128)(2,1)S(1)}, u32[]{:S(2)}, u32[]{:S(2)}) %collective-permute-start.1) | collective-permute-done | bytes 196640 | tf_op jit(solution)/shard_map/ppermute | solution.py:245
  32.9 2.9 %collective-permute-done.refs_1_ = bf16[384,256]{1,0:T(8,128)(2,1)S(1)} collective-permute-done((bf16[384,256]{1,0:T(8,128)(2,1)S(1)}, bf16[384,256]{1,0:T(8,128)(2,1)S(1)}, u32[]{:S(2)}, u32[]{:S(2)}) %collective-permute-start) | collective-permute-done | bytes 196640 | tf_op jit(solution)/shard_map/ppermute | solution.py:249
  35.8 4.0 %collective-permute-start.2 = (bf16[384,256]{1,0:T(8,128)(2,1)S(1)}, bf16[384,256]{1,0:T(8,128)(2,1)S(1)}, u32[]{:S(2)}, u32[]{:S(2)}) collective-permute-start(bf16[384,256]{1,0:T(8,128)(2,1)S(1)} %collective-permute-done.refs_1_), channel_id=1, source_target_pairs={{0,16},{8,24},{16,32},{24,40},{32,48},{40,56},{48,64},{56,72},{64,... | collective-permute-start | bytes 589832 | tf_op jit(solution)/shard_map/ppermute | solution.py:245
  39.8 0.1 pad_add_fusion.span
  39.9 4.0 %collective-permute-start.3 = (bf16[384,256]{1,0:T(8,128)(2,1)S(1)}, bf16[384,256]{1,0:T(8,128)(2,1)S(1)}, u32[]{:S(2)}, u32[]{:S(2)}) collective-permute-start(bf16[384,256]{1,0:T(8,128)(2,1)S(1)} %collective-permute-done.1.refs_2_), channel_id=1, source_target_pairs={{0,16},{8,24},{16,32},{24,40},{32,48},{40,56},{48,64},{56,72},{64,... | collective-permute-start | bytes 589832 | tf_op jit(solution)/shard_map/ppermute | solution.py:245
  43.9 9.5 %collective-permute-done.2.refs_3_ = bf16[384,256]{1,0:T(8,128)(2,1)S(1)} collective-permute-done((bf16[384,256]{1,0:T(8,128)(2,1)S(1)}, bf16[384,256]{1,0:T(8,128)(2,1)S(1)}, u32[]{:S(2)}, u32[]{:S(2)}) %collective-permute-start.2) | collective-permute-done | bytes 196640 | tf_op jit(solution)/shard_map/ppermute | solution.py:245
  53.4 1.9 %collective-permute-start.4 = (bf16[384,256]{1,0:T(8,128)(2,1)S(1)}, bf16[384,256]{1,0:T(8,128)(2,1)S(1)}, u32[]{:S(2)}, u32[]{:S(2)}) collective-permute-start(bf16[384,256]{1,0:T(8,128)(2,1)S(1)} %collective-permute-done.2.refs_3_), channel_id=1, source_target_pairs={{0,16},{8,24},{16,32},{24,40},{32,48},{40,56},{48,64},{56,72},{64,... | collective-permute-start | bytes 589832 | tf_op jit(solution)/shard_map/ppermute | solution.py:245
  55.3 2.3 %collective-permute-done.3.refs_4_ = bf16[384,256]{1,0:T(8,128)(2,1)S(1)} collective-permute-done((bf16[384,256]{1,0:T(8,128)(2,1)S(1)}, bf16[384,256]{1,0:T(8,128)(2,1)S(1)}, u32[]{:S(2)}, u32[]{:S(2)}) %collective-permute-start.3) | collective-permute-done | bytes 196640 | tf_op jit(solution)/shard_map/ppermute | solution.py:245
  57.6 0.0 all-to-all-done
  57.6 4.3 %collective-permute-done.4.refs_5_ = bf16[384,256]{1,0:T(8,128)(2,1)S(1)} collective-permute-done((bf16[384,256]{1,0:T(8,128)(2,1)S(1)}, bf16[384,256]{1,0:T(8,128)(2,1)S(1)}, u32[]{:S(2)}, u32[]{:S(2)}) %collective-permute-start.4) | collective-permute-done | bytes 196640 | tf_op jit(solution)/shard_map/ppermute | solution.py:245
  61.9 12.5 %attention.1 = (bf16[384,1024]{1,0:T(8,128)(2,1)}, f32[384,256]{1,0:T(8,128)S(1)}, f32[384,256]{1,0:T(8,128)S(1)}, bf16[384,256]{1,0:T(8,128)(2,1)S(1)}, bf16[38...) custom-call(s32[1]{0:T(128)} %bitcast.half, s32[6]{0:T(128)S(1)} %pad_add_fusion.span, ...), custom_call_target="tpu_custom_call" | custom-call | flops 2831155200 | bytes 4194304 | tf_op jit(solution)/shard_map/attention/pallas_call | solution.py:197
  74.4 3.2 %collective-permute-start.7 = (bf16[384,256]{1,0:T(8,128)(2,1)S(1)}, bf16[384,256]{1,0:T(8,128)(2,1)S(1)}, u32[]{:S(2)}, u32[]{:S(2)}) collective-permute-start(bf16[384,256]{1,0:T(8,128)(2,1)S(1)} %get-tuple-element.27), channel_id=1, source_target_pairs={{16,0},{24,8},{32,16},{40,24},{48,32},{56,40},{64,48},{72,56},{80,... | collective-permute-start | bytes 589832 | tf_op jit(solution)/shard_map/ppermute | solution.py:245
  77.7 7.8 %all-to-all-start.2 = ((bf16[8,48,1024]{2,1,0:T(8,128)(2,1)}), bf16[8,48,1024]{2,1,0:T(8,128)(2,1)S(1)}, u32[]{:S(2)}, u32[]{:S(2)}) async-start(bf16[8,48,1024]{2,1,0:T(8,128)(2,1)} %bitcast.7), calls=%async_computation.2 | async-start | bytes 1572864 | tf_op jit(solution)/shard_map/all_to_all | solution.py:239
  85.5 1.9 %collective-permute-start.5 = (bf16[384,256]{1,0:T(8,128)(2,1)S(1)}, bf16[384,256]{1,0:T(8,128)(2,1)S(1)}, u32[]{:S(2)}, u32[]{:S(2)}) collective-permute-start(bf16[384,256]{1,0:T(8,128)(2,1)S(1)} %get-tuple-element.24), channel_id=1, source_target_pairs={{16,0},{24,8},{32,16},{40,24},{48,32},{56,40},{64,48},{72,56},{80,... | collective-permute-start | bytes 589832 | tf_op jit(solution)/shard_map/ppermute | solution.py:245
  87.4 0.0 collective-permute-done.7
  87.4 0.1 add_convert_fusion.2
  87.5 1.9 %collective-permute-start.8 = (bf16[384,256]{1,0:T(8,128)(2,1)S(1)}, bf16[384,256]{1,0:T(8,128)(2,1)S(1)}, u32[]{:S(2)}, u32[]{:S(2)}) collective-permute-start(bf16[384,256]{1,0:T(8,128)(2,1)S(1)} %add_convert_fusion.2), channel_id=1, source_target_pairs={{16,0},{24,8},{32,16},{40,24},{48,32},{56,40},{64,48},{72,56},{80,... | collective-permute-start | bytes 589832 | tf_op jit(solution)/shard_map/ppermute | solution.py:245
  89.4 4.5 %collective-permute-done.5 = bf16[384,256]{1,0:T(8,128)(2,1)S(1)} collective-permute-done((bf16[384,256]{1,0:T(8,128)(2,1)S(1)}, bf16[384,256]{1,0:T(8,128)(2,1)S(1)}, u32[]{:S(2)}, u32[]{:S(2)}) %collective-permute-start.5) | collective-permute-done | bytes 196640 | tf_op jit(solution)/shard_map/ppermute | solution.py:245
  94.0 4.2 %collective-permute-start.6 = (bf16[384,256]{1,0:T(8,128)(2,1)S(1)}, bf16[384,256]{1,0:T(8,128)(2,1)S(1)}, u32[]{:S(2)}, u32[]{:S(2)}) collective-permute-start(bf16[384,256]{1,0:T(8,128)(2,1)S(1)} %add_convert_fusion.3), channel_id=1, source_target_pairs={{16,0},{24,8},{32,16},{40,24},{48,32},{56,40},{64,48},{72,56},{80,... | collective-permute-start | bytes 589832 | tf_op jit(solution)/shard_map/ppermute | solution.py:245
  98.2 0.0 collective-permute-done.8
  98.3 5.0 %collective-permute-start.9 = (bf16[384,256]{1,0:T(8,128)(2,1)S(1)}, bf16[384,256]{1,0:T(8,128)(2,1)S(1)}, u32[]{:S(2)}, u32[]{:S(2)}) collective-permute-start(bf16[384,256]{1,0:T(8,128)(2,1)S(1)} %add_convert_fusion.1), channel_id=1, source_target_pairs={{0,1},{1,0},{2,3},{3,2},{4,5},{5,4},{6,7},{7,6},{8,9},{9,8},{10,11... | collective-permute-start | bytes 589832 | tf_op jit(solution)/shard_map/ppermute | solution.py:249
  103.2 2.6 %collective-permute-done.6 = bf16[384,256]{1,0:T(8,128)(2,1)S(1)} collective-permute-done((bf16[384,256]{1,0:T(8,128)(2,1)S(1)}, bf16[384,256]{1,0:T(8,128)(2,1)S(1)}, u32[]{:S(2)}, u32[]{:S(2)}) %collective-permute-start.6) | collective-permute-done | bytes 196640 | tf_op jit(solution)/shard_map/ppermute | solution.py:245
  105.9 8.3 %collective-permute-done.9 = bf16[384,256]{1,0:T(8,128)(2,1)S(1)} collective-permute-done((bf16[384,256]{1,0:T(8,128)(2,1)S(1)}, bf16[384,256]{1,0:T(8,128)(2,1)S(1)}, u32[]{:S(2)}, u32[]{:S(2)}) %collective-permute-start.9) | collective-permute-done | bytes 196640 | tf_op jit(solution)/shard_map/ppermute | solution.py:249
  114.2 0.7 add_convert_fusion
  115.0 0.0 all-to-all-done.2.got_ref
  115.0 0.0 copy-start
  115.0 5.1 %all-to-all-start.3 = ((bf16[8,48,256]{2,1,0:T(8,128)(2,1)}), bf16[8,48,256]{2,1,0:T(8,128)(2,1)S(1)}, u32[]{:S(2)}, u32[]{:S(2)}) async-start(bf16[8,48,256]{2,1,0:T(8,128)(2,1)} %bitcast.8), calls=%async_computation.3 | async-start | bytes 393216 | tf_op jit(solution)/shard_map/all_to_all | solution.py:239
  120.0 0.0 copy-done
  120.0 2.1 %unpack.2 = (bf16[48,4096]{1,0:T(8,128)(2,1)}, bf16[48,4096]{1,0:T(8,128)(2,1)}) custom-call(bf16[8,48,1024]{2,1,0:T(8,128)(2,1)} %copy-done), custom_call_target="tpu_custom_call" | custom-call | bytes 1572864 | tf_op jit(solution)/shard_map/unpack/pallas_call | solution.py:80
  122.1 3.8 %all-to-all-done.3.got_ref = bf16[8,48,256]{2,1,0:T(8,128)(2,1)S(1)} async-done(((bf16[8,48,256]{2,1,0:T(8,128)(2,1)}), bf16[8,48,256]{2,1,0:T(8,128)(2,1)S(1)}, u32[]{:S(2)}, u32[]{:S(2)}) %all-to-all-start.3) | async-done | bytes 196640 | tf_op jit(solution)/shard_map/all_to_all | solution.py:239
  125.9 0.0 copy-start.1
  125.9 0.7 copy-done.1
  126.6 1.6 %unpack.3 = (bf16[48,1024]{1,0:T(8,128)(2,1)}, bf16[48,1024]{1,0:T(8,128)(2,1)}) custom-call(bf16[8,48,256]{2,1,0:T(8,128)(2,1)} %copy-done.1), custom_call_target="tpu_custom_call" | custom-call | bytes 393216 | tf_op jit(solution)/shard_map/unpack/pallas_call | solution.py:80
  (8 shorter events, 0.2 us)
Async XLA Ops:
  2.3 10.9 %all-to-all-start.1 = ((bf16[8,48,256]{2,1,0:T(8,128)(2,1)}), bf16[8,48,256]{2,1,0:T(8,128)(2,1)S(1)}, u32[]{:S(2)}, u32[]{:S(2)}) async-start(bf16[8,48,256]{2,1,0:T(8,128)(2,1)} %pack.3), calls=%async_computation.1 | async-start | bytes 393216 | tf_op jit(solution)/shard_map/all_to_all | solution.py:239
  7.3 0.7 copy-start.2
  13.1 44.5 %all-to-all-start = ((bf16[8,48,1024]{2,1,0:T(8,128)(2,1)}), bf16[8,48,1024]{2,1,0:T(8,128)(2,1)S(1)}, u32[]{:S(2)}, u32[]{:S(2)}) async-start(bf16[8,48,1024]{2,1,0:T(8,128)(2,1)} %pack.2), calls=%async_computation | async-start | bytes 1572864 | tf_op jit(solution)/shard_map/all_to_all | solution.py:239
  17.2 15.7 %collective-permute-start.1 = (bf16[384,256]{1,0:T(8,128)(2,1)S(1)}, bf16[384,256]{1,0:T(8,128)(2,1)S(1)}, u32[]{:S(2)}, u32[]{:S(2)}) collective-permute-start(bf16[384,256]{1,0:T(8,128)(2,1)S(1)} %bitcast.11), channel_id=1, source_target_pairs={{0,16},{8,24},{16,32},{24,40},{32,48},{40,56},{48,64},{56,72},{64,... | collective-permute-start | bytes 589832 | tf_op jit(solution)/shard_map/ppermute | solution.py:245
  21.2 14.6 %collective-permute-start = (bf16[384,256]{1,0:T(8,128)(2,1)S(1)}, bf16[384,256]{1,0:T(8,128)(2,1)S(1)}, u32[]{:S(2)}, u32[]{:S(2)}) collective-permute-start(bf16[384,256]{1,0:T(8,128)(2,1)S(1)} %bitcast.12), channel_id=1, source_target_pairs={{0,1},{1,0},{2,3},{3,2},{4,5},{5,4},{6,7},{7,6},{8,9},{9,8},{10,11... | collective-permute-start | bytes 589832 | tf_op jit(solution)/shard_map/ppermute | solution.py:249
  35.8 17.6 %collective-permute-start.2 = (bf16[384,256]{1,0:T(8,128)(2,1)S(1)}, bf16[384,256]{1,0:T(8,128)(2,1)S(1)}, u32[]{:S(2)}, u32[]{:S(2)}) collective-permute-start(bf16[384,256]{1,0:T(8,128)(2,1)S(1)} %collective-permute-done.refs_1_), channel_id=1, source_target_pairs={{0,16},{8,24},{16,32},{24,40},{32,48},{40,56},{48,64},{56,72},{64,... | collective-permute-start | bytes 589832 | tf_op jit(solution)/shard_map/ppermute | solution.py:245
  39.9 17.7 %collective-permute-start.3 = (bf16[384,256]{1,0:T(8,128)(2,1)S(1)}, bf16[384,256]{1,0:T(8,128)(2,1)S(1)}, u32[]{:S(2)}, u32[]{:S(2)}) collective-permute-start(bf16[384,256]{1,0:T(8,128)(2,1)S(1)} %collective-permute-done.1.refs_2_), channel_id=1, source_target_pairs={{0,16},{8,24},{16,32},{24,40},{32,48},{40,56},{48,64},{56,72},{64,... | collective-permute-start | bytes 589832 | tf_op jit(solution)/shard_map/ppermute | solution.py:245
  53.4 8.5 %collective-permute-start.4 = (bf16[384,256]{1,0:T(8,128)(2,1)S(1)}, bf16[384,256]{1,0:T(8,128)(2,1)S(1)}, u32[]{:S(2)}, u32[]{:S(2)}) collective-permute-start(bf16[384,256]{1,0:T(8,128)(2,1)S(1)} %collective-permute-done.2.refs_3_), channel_id=1, source_target_pairs={{0,16},{8,24},{16,32},{24,40},{32,48},{40,56},{48,64},{56,72},{64,... | collective-permute-start | bytes 589832 | tf_op jit(solution)/shard_map/ppermute | solution.py:245
  74.4 13.0 %collective-permute-start.7 = (bf16[384,256]{1,0:T(8,128)(2,1)S(1)}, bf16[384,256]{1,0:T(8,128)(2,1)S(1)}, u32[]{:S(2)}, u32[]{:S(2)}) collective-permute-start(bf16[384,256]{1,0:T(8,128)(2,1)S(1)} %get-tuple-element.27), channel_id=1, source_target_pairs={{16,0},{24,8},{32,16},{40,24},{48,32},{56,40},{64,48},{72,56},{80,... | collective-permute-start | bytes 589832 | tf_op jit(solution)/shard_map/ppermute | solution.py:245
  77.7 37.3 %all-to-all-start.2 = ((bf16[8,48,1024]{2,1,0:T(8,128)(2,1)}), bf16[8,48,1024]{2,1,0:T(8,128)(2,1)S(1)}, u32[]{:S(2)}, u32[]{:S(2)}) async-start(bf16[8,48,1024]{2,1,0:T(8,128)(2,1)} %bitcast.7), calls=%async_computation.2 | async-start | bytes 1572864 | tf_op jit(solution)/shard_map/all_to_all | solution.py:239
  85.5 8.4 %collective-permute-start.5 = (bf16[384,256]{1,0:T(8,128)(2,1)S(1)}, bf16[384,256]{1,0:T(8,128)(2,1)S(1)}, u32[]{:S(2)}, u32[]{:S(2)}) collective-permute-start(bf16[384,256]{1,0:T(8,128)(2,1)S(1)} %get-tuple-element.24), channel_id=1, source_target_pairs={{16,0},{24,8},{32,16},{40,24},{48,32},{56,40},{64,48},{72,56},{80,... | collective-permute-start | bytes 589832 | tf_op jit(solution)/shard_map/ppermute | solution.py:245
  87.5 10.7 %collective-permute-start.8 = (bf16[384,256]{1,0:T(8,128)(2,1)S(1)}, bf16[384,256]{1,0:T(8,128)(2,1)S(1)}, u32[]{:S(2)}, u32[]{:S(2)}) collective-permute-start(bf16[384,256]{1,0:T(8,128)(2,1)S(1)} %add_convert_fusion.2), channel_id=1, source_target_pairs={{16,0},{24,8},{32,16},{40,24},{48,32},{56,40},{64,48},{72,56},{80,... | collective-permute-start | bytes 589832 | tf_op jit(solution)/shard_map/ppermute | solution.py:245
  94.0 11.9 %collective-permute-start.6 = (bf16[384,256]{1,0:T(8,128)(2,1)S(1)}, bf16[384,256]{1,0:T(8,128)(2,1)S(1)}, u32[]{:S(2)}, u32[]{:S(2)}) collective-permute-start(bf16[384,256]{1,0:T(8,128)(2,1)S(1)} %add_convert_fusion.3), channel_id=1, source_target_pairs={{16,0},{24,8},{32,16},{40,24},{48,32},{56,40},{64,48},{72,56},{80,... | collective-permute-start | bytes 589832 | tf_op jit(solution)/shard_map/ppermute | solution.py:245
  98.3 15.9 %collective-permute-start.9 = (bf16[384,256]{1,0:T(8,128)(2,1)S(1)}, bf16[384,256]{1,0:T(8,128)(2,1)S(1)}, u32[]{:S(2)}, u32[]{:S(2)}) collective-permute-start(bf16[384,256]{1,0:T(8,128)(2,1)S(1)} %add_convert_fusion.1), channel_id=1, source_target_pairs={{0,1},{1,0},{2,3},{3,2},{4,5},{5,4},{6,7},{7,6},{8,9},{9,8},{10,11... | collective-permute-start | bytes 589832 | tf_op jit(solution)/shard_map/ppermute | solution.py:249
  115.0 5.1 %copy-start = (bf16[8,48,1024]{2,1,0:T(8,128)(2,1)}, bf16[8,48,1024]{2,1,0:T(8,128)(2,1)S(1)}, u32[]{:S(2)}) copy-start(bf16[8,48,1024]{2,1,0:T(8,128)(2,1)S(1)} %all-to-all-done.2.got_ref) | copy-start | bytes 2359300
  115.0 11.0 %all-to-all-start.3 = ((bf16[8,48,256]{2,1,0:T(8,128)(2,1)}), bf16[8,48,256]{2,1,0:T(8,128)(2,1)S(1)}, u32[]{:S(2)}, u32[]{:S(2)}) async-start(bf16[8,48,256]{2,1,0:T(8,128)(2,1)} %bitcast.8), calls=%async_computation.3 | async-start | bytes 393216 | tf_op jit(solution)/shard_map/all_to_all | solution.py:239
  125.9 0.7 copy-start.1
